TPU v7x, 32 devices: a whole 2x2x4 slice. The times are simulated.
32 devices in a mesh: ctx: 4 (over y, core), exp: 8 (over z, x).
Axes of the slice: x: 2, y: 2, z: 4, core: 2. Of those that a mesh axis runs over, the one named last changes fastest.
Arguments:
- residual_in: bfloat16 [2048, 3584], P(('ctx', 'exp')), may hold values from -1.5 to 1.5
- norm_gain: float32 [3584], replicated, may hold values from 0.25 to 1.75
- q_nope: bfloat16 [2048, 16, 512], P('ctx', 'exp'), may hold values from -64 to 64
- q_rope: bfloat16 [2048, 1024], P('ctx', 'exp'), may hold values from -6 to 6
- latent: bfloat16 [2048, 512], P('ctx'), may hold values from -6 to 6
- k_rope: bfloat16 [2048, 64], P('ctx'), may hold values from -6 to 6
- doc_ids: int32 [2048], P('ctx'), may hold values from 0 to 3, never falling along the last dimension, each value on 1 to 1024 neighbouring positions
- uv_weight: bfloat16 [16, 512, 128], P('exp'), may hold values from -0.25 to 0.25
- out_weight: bfloat16 [2048, 3584], P('exp'), may hold values from -0.125 to 0.125
- expert_ids: int32 [2048, 8], P(('ctx', 'exp')), may hold values from 0 to 7, all different within a row; in each aligned block of 64 rows (0 to 63, 64 to 127, ...) at most 64 rows name the same one
- gate_levels: int32 [2048, 8], P(('ctx', 'exp')), may hold values from 1 to 255
- bin_ids: int32 [2048, 8], P(('ctx', 'exp')), may hold values from 0 to 2047
- gate_weight: bfloat16 [8, 3584, 1024], P('exp', None, 'ctx'), may hold values from -0.09375 to 0.09375
- up_weight: bfloat16 [8, 3584, 1024], P('exp', None, 'ctx'), may hold values from -0.09375 to 0.09375
- down_weight: bfloat16 [8, 1024, 3584], P('exp', 'ctx'), may hold values from -0.1875 to 0.1875
Outputs:
- layer_out: bfloat16 [2048, 3584], P(('ctx', 'exp'))
- histogram: float32 [8, 2048], P('exp', 'ctx')
Inputs may be any that keep to these rules, and one draw needn't show every extreme that they name: `expert_ids`: each row names 8 different experts; within the rows of one device (aligned blocks of 64 rows) no expert is named more than 64 times, a bound that some block reaches. `doc_ids`: document numbers never fall along the sequence; each document has 1 to 1024 tokens, one exactly 1024.
All inputs are finite; a program needn't handle non-finite values.
Results may differ from a plain program's by a relative error of at most 0.03.
Values may be sent and summed in bfloat16 or wider, within the bound.
No kernel may reach another device: no remote copies, remote signals or barrier semaphores. Data moves between devices by JAX's collectives and lax.ppermute only.
A program may use at most 128 MiB of HBM per device.

v0:
```python
import jax
import jax.numpy as jnp
from jax import lax
from jax.sharding import PartitionSpec as P

HID = 1024
NBINS = 2048


softmax_scale = 192.0 ** (-0.5)
norm_eps = 1e-06
masked_score = -1e30


def route_slots(expert_ids, experts, capacity):
    flat_ids = expert_ids.reshape(-1)
    onehot = (flat_ids[:, None] == jnp.arange(experts, dtype=jnp.int32)[None, :]).astype(jnp.int32)
    before = jnp.cumsum(onehot, axis=0) - onehot
    slot_rank = jnp.sum(before * onehot, axis=1)
    return (flat_ids * capacity + slot_rank).reshape(expert_ids.shape)


def key_scores(query_nope, query_rope, lat_rows, rope_rows):
    scores = jnp.einsum("qhl,kl->hqk", query_nope, lat_rows, preferred_element_type=jnp.float32)
    scores = scores + jnp.einsum(
        "qhr,kr->hqk", query_rope, rope_rows, preferred_element_type=jnp.float32
    )
    return scores * softmax_scale


def attend_piece(running, key_piece, query_nope, query_rope, query_pos, query_docs):
    lat_rows, rope_rows, doc_rows = key_piece
    key_pos = jnp.arange(lat_rows.shape[0], dtype=jnp.int32)
    allowed = (key_pos[None, :] <= query_pos[:, None]) & (doc_rows[None, :] == query_docs[:, None])
    scores = jnp.where(
        allowed[None], key_scores(query_nope, query_rope, lat_rows, rope_rows), masked_score
    )
    run_max, run_sum, accum = running
    new_max = jnp.maximum(run_max, jnp.max(scores, axis=2))
    probs = jnp.where(allowed[None], jnp.exp(scores - new_max[:, :, None]), 0.0)
    run_sum = jnp.sum(probs, axis=2)
    accum = jnp.einsum(
        "hqk,kl->hql", probs.astype(jnp.bfloat16), lat_rows, preferred_element_type=jnp.float32
    )
    return (new_max, run_sum, accum)


def project_values(context, uv_weight):
    values = jnp.einsum(
        "hql,hlv->qhv", context, uv_weight, preferred_element_type=jnp.float32
    ).astype(jnp.bfloat16)
    return values.reshape(values.shape[0], values.shape[1] * values.shape[2])


def fold_projection(running, uv_weight, out_weight):
    context = (running[2] / running[1][:, :, None]).astype(jnp.bfloat16)
    values = project_values(context, uv_weight)

    def head_rows(row_start, row_count):
        return jnp.dot(values, out_weight, preferred_element_type=jnp.float32)

    return head_rows


def expert_hidden(row_data, w_gate, w_up):
    gate_part = jnp.dot(row_data, w_gate, preferred_element_type=jnp.float32)
    up_part = jnp.dot(row_data, w_up, preferred_element_type=jnp.float32)
    activation = jax.nn.silu(gate_part) * up_part
    return (activation.astype(jnp.bfloat16), jnp.sum(activation * activation, axis=1) / HID)


def bin_energy(energy, slot_bins):
    onehot = (slot_bins[:, None] == jnp.arange(NBINS, dtype=jnp.int32)[None, :]).astype(jnp.float32)
    return jnp.dot(energy[None, :], onehot, precision=lax.Precision.HIGHEST)[0]


def on_device(
    residual_in,
    norm_gain,
    q_nope,
    q_rope,
    latent,
    k_rope,
    doc_ids,
    uv_weight,
    out_weight,
    expert_ids,
    gate_levels,
    bin_ids,
    gate_weight,
    up_weight,
    down_weight,
):
    exp_devices = lax.axis_size("exp")
    block_len, head_count, lat_width = q_nope.shape
    rope_width = k_rope.shape[1]
    query_first = lax.axis_index("ctx") * block_len
    query_pos = query_first + jnp.arange(block_len, dtype=jnp.int32)
    query_rope = q_rope.reshape(block_len, head_count, rope_width)
    token_count = residual_in.shape[0]
    keys_local = (latent, k_rope, doc_ids)
    initial = (
        jnp.full((head_count, block_len), masked_score, jnp.float32),
        jnp.zeros((head_count, block_len), jnp.float32),
        jnp.zeros((head_count, block_len, lat_width), jnp.float32),
    )
    running = attend_piece(
        initial,
        (
            lax.all_gather(keys_local[0], "ctx", axis=0, tiled=True),
            lax.all_gather(keys_local[1], "ctx", axis=0, tiled=True),
            lax.all_gather(keys_local[2], "ctx", axis=0, tiled=True),
        ),
        q_nope,
        query_rope,
        query_pos,
        doc_ids,
    )
    head_rows = fold_projection(running, uv_weight, out_weight)
    attended = lax.psum_scatter(
        head_rows(jnp.int32(0), token_count * lax.axis_size("exp")),
        "exp",
        scatter_dimension=0,
        tiled=True,
    )
    stream_state = residual_in.astype(jnp.float32) + attended
    normed = (
        stream_state
        * lax.rsqrt(jnp.mean(stream_state * stream_state, axis=1, keepdims=True) + norm_eps)
        * norm_gain
    ).astype(jnp.bfloat16)
    top_count = expert_ids.shape[1]
    capacity = min(token_count, max(2, 2 * token_count * top_count // exp_devices))
    slot_total = exp_devices * capacity
    destination = route_slots(expert_ids, exp_devices, capacity)
    slot_match = destination[:, :, None] == jnp.arange(slot_total, dtype=jnp.int32)[None, None, :]
    selector = jnp.sum(slot_match.astype(jnp.int32), axis=1).astype(jnp.bfloat16)
    outgoing = jnp.einsum("ts,td->sd", selector, normed, preferred_element_type=jnp.float32).astype(
        jnp.bfloat16
    )
    outgoing = outgoing.reshape(exp_devices, capacity, outgoing.shape[1])
    slot_bins = jnp.sum(jnp.where(slot_match, bin_ids[:, :, None], 0), axis=(0, 1)).reshape(
        exp_devices, capacity
    )
    incoming, incoming_bins = (
        lax.all_to_all(outgoing, "exp", split_axis=0, concat_axis=1, tiled=True),
        lax.all_to_all(slot_bins, "exp", split_axis=0, concat_axis=1, tiled=True),
    )
    all_rows, all_bins = (
        lax.all_gather(incoming, "ctx", axis=1, tiled=True),
        lax.all_gather(incoming_bins, "ctx", axis=1, tiled=True),
    )
    hidden, energy = expert_hidden(all_rows[0], gate_weight[0], up_weight[0])
    bin_part = bin_energy(energy, all_bins[0])
    down_local = down_weight[0]
    expert_out = lax.psum_scatter(
        jnp.dot(hidden, down_local, preferred_element_type=jnp.float32).astype(jnp.bfloat16),
        "ctx",
        scatter_dimension=0,
        tiled=True,
    )
    histogram = lax.psum_scatter(bin_part[None, :], "ctx", scatter_dimension=1, tiled=True)
    returned = lax.all_to_all(expert_out[None], "exp", split_axis=1, concat_axis=0, tiled=True)
    levels = gate_levels.astype(jnp.float32)
    route_weights = levels / jnp.sum(levels, axis=1, keepdims=True)
    combiner = jnp.sum(jnp.where(slot_match, route_weights[:, :, None], 0.0), axis=1)
    mixture = jnp.dot(
        combiner,
        returned.reshape(slot_total, returned.shape[2]).astype(jnp.float32),
        precision=lax.Precision.HIGHEST,
    )
    layer_out = (stream_state + mixture).astype(jnp.bfloat16)
    return (layer_out, histogram)


def solution(mesh):
    return jax.shard_map(
        on_device,
        mesh=mesh,
        in_specs=(
            P(("ctx", "exp"), None),
            P(),
            P("ctx", "exp", None),
            P("ctx", "exp"),
            P("ctx", None),
            P("ctx", None),
            P("ctx"),
            P("exp", None, None),
            P("exp", None),
            P(("ctx", "exp"), None),
            P(("ctx", "exp"), None),
            P(("ctx", "exp"), None),
            P("exp", None, "ctx"),
            P("exp", None, "ctx"),
            P("exp", "ctx", None),
        ),
        out_specs=(P(("ctx", "exp"), None), P("exp", "ctx")),
        check_vma=False,
    )
```

profile of v0, /device:TPU:0, one launch (start us, length us, event | category | flops | bytes accessed | tf_op | source)
XLA Modules:
  0.0 668.5 jit_solution(7229321450326501757)
XLA Ops:
  9.0 6.3 all-gather
  15.3 6.4 all_gather.17
  23.4 11.5 %all-gather.4.cloned.1.call-done = bf16[2048,512]{1,0:T(8,128)(2,1)} async-done(((bf16[512,512]{1,0:T(8,128)(2,1)}), bf16[2048,512]{1,0:T(8,128)(2,1)}) %all-gather.4.cloned.1.call-update) | async-done | bytes 2097168 | tf_op jit(solution)/shard_map/all_gather | solution.py:110
  34.9 4.2 fusion.22
  46.4 6.8 %convolution_convert_fusion.2 = bf16[2,512,128]{1,2,0:T(8,128)(2,1)S(1)} fusion(bf16[2,512,128]{2,1,0:T(8,128)(2,1)S(1)} %copy-done.8, f32[2,512]{1,0:T(2,128)S(1)} %fusion.6, f32[2,512,2048]{1,2,0:T(8,128)} %copy-done.1, f32[2,512]{1,0:T(2,128)S(1)} %broadcast_maximum_fusion, pred[512,2048]{0,1:T(8,128)(4,1)S(1)} %fusion.13, ...), kind=kOutput, calls=%fused_computation.33 | convolution fusion | flops 2289172480 | bytes 12066816 | tf_op jit(solution)/shard_map/hql,hlv->qhv/dot_general | solution.py:49
  53.1 5.6 fusion.47
  62.0 129.6 %reduce-scatter.6.cloned.1.call-done = f32[64,3584]{1,0:T(8,128)} async-done(((f32[512,3584]{1,0:T(8,128)}), f32[64,3584]{1,0:T(8,128)}) %reduce-scatter.6.cloned.1.call-update) | async-done | bytes 917520 | tf_op jit(solution)/shard_map/reduce_scatter | solution.py:120
  195.4 85.7 %all_to_all.37 = bf16[8,64,3584]{2,1,0:T(8,128)(2,1)} all-to-all(bf16[8,64,3584]{2,1,0:T(8,128)(2,1)S(1)} %bitcast.76), channel_id=1, replica_groups=mesh['ctx'=4,'exp'=8] {'exp'}, dimensions={0} | all-to-all | bytes 7340032 | tf_op jit(solution)/shard_map/all_to_all | solution.py:146
  281.2 93.2 %all-gather.6.cloned.1.call-done = bf16[1,2048,3584]{2,1,0:T(8,128)(2,1)} async-done(((bf16[1,512,3584]{2,1,0:T(8,128)(2,1)}), bf16[1,2048,3584]{2,1,0:T(8,128)(2,1)}) %all-gather.6.cloned.1.call-update) | async-done | bytes 14680080 | tf_op jit(solution)/shard_map/all_gather | solution.py:150
  374.3 11.0 %fusion.3 = f32[2048,256]{0,1:T(8,128)} fusion(bf16[1,2048,3584]{2,1,0:T(8,128)(2,1)} %all-gather.6.cloned.1.call-done, bf16[1,3584,256]{2,1,0:T(8,128)(2,1)} %param.27), kind=kOutput, calls=%fused_computation.5 | convolution fusion | flops 3758096384 | bytes 18612224 | tf_op jit(solution)/shard_map/dot_general | solution.py:66
  385.3 11.7 %multiply_reduce_fusion = (f32[2048]{0:T(1024)S(1)}, bf16[2048,256]{0,1:T(8,128)(2,1)}) fusion(bf16[1,3584,256]{2,1,0:T(8,128)(2,1)} %param.28, bf16[1,2048,3584]{2,1,0:T(8,128)(2,1)} %all-gather.6.cloned.1.call-done, f32[2048,256]{0,1:T(8,128)} %fusion.3), kind=kOutput, calls=%fused_computation.28 | convolution fusion | flops 3762288640 | bytes 19668992 | tf_op jit(solution)/shard_map/dot_general | solution.py:67
  397.0 8.5 %convolution_convert_fusion = bf16[2048,3584]{1,0:T(8,128)(2,1)} fusion(bf16[1,256,3584]{2,1,0:T(8,128)(2,1)S(1)} %copy-done, bf16[2048,256]{0,1:T(8,128)(2,1)} %get-tuple-element.7), kind=kOutput, calls=%fused_computation.2 | convolution fusion | flops 3765436416 | bytes 17563648 | tf_op jit(solution)/shard_map/dot_general | solution.py:157
  406.3 14.4 %all-to-all-start.2 = ((s32[8,1,64]{2,1,0:T(1,128)}), s32[8,1,64]{2,1,0:T(1,128)S(1)}, u32[]{:S(2)}, u32[]{:S(2)}) async-start(s32[8,1,64]{2,1,0:T(1,128)} %all_to_all.31), calls=%async_computation.4 | async-start | bytes 8192 | tf_op jit(solution)/shard_map/all_to_all | solution.py:147
  420.7 98.0 %reduce-scatter.8.cloned.1.call-done = bf16[512,3584]{1,0:T(8,128)(2,1)} async-done(((bf16[2048,3584]{1,0:T(8,128)(2,1)}), bf16[512,3584]{1,0:T(8,128)(2,1)}) %reduce-scatter.8.cloned.1.call-update) | async-done | bytes 3670032 | tf_op jit(solution)/shard_map/reduce_scatter | solution.py:156
  518.7 7.9 %copy.88 = bf16[1,512,3584]{2,0,1:T(2,128)(2,1)} copy(bf16[1,512,3584]{2,1,0:T(8,128)(2,1)} %bitcast.77) | data formatting | bytes 7340032 | tf_op jit(solution)/shard_map/broadcast_in_dim | solution.py:163
  527.1 25.4 %reduce.6 = bf16[512,3584]{1,0:T(8,128)(2,1)} reduce(bf16[512,1,3584]{2,1,0:T(2,128)(2,1)} %bitcast.73, bf16[]{:T(256)} %broadcast.86), dimensions={1}, to_apply=%bitcast.72.reduce_sub_computation | reduce | bytes 7340034
  552.5 7.4 %reshape.149 = bf16[8,2,114688]{2,1,0:T(2,128)(2,1)} reshape(bf16[512,3584]{1,0:T(8,128)(2,1)} %reduce.6) | data formatting | bytes 7340032
  559.9 5.6 all-to-all-start.1
  567.0 5.2 all_gather.19
  572.1 14.6 %fusion.20 = f32[2048,1]{1,0:T(8,128)} fusion(f32[2048,1]{0,1:T(1,128)S(1)} %bitcast.84, s32[2048]{0:T(1024)S(1)} %bitcast.83), kind=kOutput, calls=%fused_computation.24 | convolution fusion | flops 54525952 | bytes 24576
  587.2 25.1 %reduce-scatter.10.cloned.1.call-done = f32[512,1]{1,0:T(8,128)} async-done(((f32[2048,1]{1,0:T(8,128)}), f32[512,1]{1,0:T(8,128)}) %reduce-scatter.10.cloned.1.call-update) | async-done | bytes 2064
  613.9 33.7 %all-to-all-done.1 = bf16[8,2,114688]{2,1,0:T(2,128)(2,1)} async-done(((bf16[8,2,114688]{2,1,0:T(2,128)(2,1)}), bf16[8,2,114688]{2,1,0:T(2,128)(2,1)}, u32[]{:S(2)}, u32[]{:S(2)}) %all-to-all-start.1) | async-done | bytes 3670048 | tf_op jit(solution)/shard_map/all_to_all | solution.py:163
  647.6 8.3 %reshape.150 = bf16[512,1,3584]{2,1,0:T(2,128)(2,1)} reshape(bf16[8,2,114688]{2,1,0:T(2,128)(2,1)} %all-to-all-done.1) | data formatting | bytes 7340032
  655.9 5.9 fusion.8
  (64 shorter events, 22.4 us)
Async XLA Ops:
  7.2 389.9 %copy-start = (bf16[1,256,3584]{2,1,0:T(8,128)(2,1)S(1)}, bf16[1,256,3584]{2,1,0:T(8,128)(2,1)}, u32[]{:S(2)}) copy-start(bf16[1,256,3584]{2,1,0:T(8,128)(2,1)} %param.29) | copy-start | bytes 5505028
  7.2 27.7 %all-gather.4.cloned.1.call-start = ((), (), s32[]{:S(2)}) async-start(), calls=%async_computation.6 | async-start | bytes 2621440 | tf_op jit(solution)/shard_map/all_gather | solution.py:110
  7.9 183.8 %reduce-scatter.6.cloned.1.call-start = ((), (), s32[]{:S(2)}) async-start(), calls=%async_computation.7 | async-start | bytes 8257536 | tf_op jit(solution)/shard_map/reduce_scatter | solution.py:120
  41.5 3.2 copy-start.1
  44.7 1.7 copy-start.8
  58.8 0.7 copy-start.5
  58.8 2.7 copy-start.7
  58.8 132.9 %copy-start.3 = (bf16[64,3584]{1,0:T(8,128)(2,1)S(1)}, bf16[64,3584]{1,0:T(8,128)(2,1)}, u32[]{:S(2)}) copy-start(bf16[64,3584]{1,0:T(8,128)(2,1)} %param.15) | copy-start | bytes 1376260
  58.8 134.3 %copy-start.4 = (f32[3584]{0:T(1024)S(1)}, f32[3584]{0:T(1024)}, u32[]{:S(2)}) copy-start(f32[3584]{0:T(1024)} %param.16) | copy-start | bytes 43012
  58.8 315.6 %all-gather.6.cloned.1.call-start = ((), (), s32[]{:S(2)}) async-start(), calls=%async_computation.8 | async-start | bytes 18350080 | tf_op jit(solution)/shard_map/all_gather | solution.py:150
  281.1 237.6 %reduce-scatter.8.cloned.1.call-start = ((), (), s32[]{:S(2)}) async-start(), calls=%async_computation.9 | async-start | bytes 18350080 | tf_op jit(solution)/shard_map/reduce_scatter | solution.py:156
  406.3 153.6 %all-to-all-start.2 = ((s32[8,1,64]{2,1,0:T(1,128)}), s32[8,1,64]{2,1,0:T(1,128)S(1)}, u32[]{:S(2)}, u32[]{:S(2)}) async-start(s32[8,1,64]{2,1,0:T(1,128)} %all_to_all.31), calls=%async_computation.4 | async-start | bytes 8192 | tf_op jit(solution)/shard_map/all_to_all | solution.py:147
  559.9 5.7 copy-start.6
  559.9 87.7 %all-to-all-start.1 = ((bf16[8,2,114688]{2,1,0:T(2,128)(2,1)}), bf16[8,2,114688]{2,1,0:T(2,128)(2,1)}, u32[]{:S(2)}, u32[]{:S(2)}) async-start(bf16[8,2,114688]{2,1,0:T(2,128)(2,1)} %reshape.149), calls=%async_computation.3 | async-start | bytes 7340032 | tf_op jit(solution)/shard_map/all_to_all | solution.py:163
  565.5 46.7 %reduce-scatter.10.cloned.1.call-start = ((), (), s32[]{:S(2)}) async-start(), calls=%async_computation.10 | async-start | bytes 1310720
  613.9 42.0 %copy-start.2 = (f32[64,3584]{1,0:T(8,128)S(1)}, f32[64,3584]{1,0:T(8,128)}, u32[]{:S(2)}) copy-start(f32[64,3584]{1,0:T(8,128)} %reduce-scatter.6.cloned.1.call-done) | copy-start | bytes 2752516
Sparse Core Ops, SparseCore 0:
  9.6 25.2 all-gather.3
  58.9 132.7 reduce-scatter.5
  281.3 93.0 all-gather.5
  405.7 112.9 reduce-scatter.7
  586.9 25.2 reduce-scatter.9
where the time goes:
time: 677 us; the launch traced here: 668 us
  waiting for transfers between devices  392 us (58%)
  blocking collectives  104 us (15%)
  matrix products  73 us (11%)
  other arithmetic  33 us (5%)
  local copies, waits for them, and re-layouts  32.4 us (5%)
  starting transfers between devices  20.5 us (3%)
  between operations  14.2 us (2%)
    reduce_scatter x1, waiting for transfers between devices, on_device(): lax.psum_scatter(head_rows(jnp.int32(0), token_count * lax.axis_size('exp...  130 us
    reduce_scatter x1, waiting for transfers between devices, on_device(): lax.psum_scatter(jnp.dot(hidden, down_local, preferred_element_type=jnp.f...  98 us
    all_gather x1, waiting for transfers between devices, on_device(): lax.all_gather(incoming, 'ctx', axis=1, tiled=True)  93.2 us
    all_to_all x1, blocking collectives, on_device(): lax.all_to_all(outgoing, 'exp', split_axis=0, concat_axis=1, tiled=True)  85.7 us
    all_to_all x1, waiting for transfers between devices, on_device(): lax.all_to_all(expert_out[None], 'exp', split_axis=1, concat_axis=0, tile...  33.7 us
    unnamed x6, waiting for transfers between devices  25.8 us
    unnamed x1, other arithmetic  25.4 us
    unnamed x25, local copies, waits for them, and re-layouts  22.6 us
  transfers between devices with their start and end apart: 7, of which 6 were waited for; matrix products, arithmetic and copies ran while one was open for 10% of the time, Pallas kernels for 0%

commit v1 on v0

--- a/solution.py
+++ b/solution.py
@@ -1,6 +1,8 @@
 import jax
 import jax.numpy as jnp
 from jax import lax
+from jax.experimental import pallas as pl
+from jax.experimental.pallas import tpu as pltpu
 from jax.sharding import PartitionSpec as P
 
 HID = 1024
@@ -74,7 +76,7 @@
     return jnp.dot(energy[None, :], onehot, precision=lax.Precision.HIGHEST)[0]
 
 
-def on_device(
+def routed_device(
     residual_in,
     norm_gain,
     q_nope,
@@ -173,7 +175,220 @@
     return (layer_out, histogram)
 
 
+def relative_order(exp_devices):
+    here = lax.axis_index("exp")
+    rows = exp_devices // 2
+    z_at, x_at = here // 2, here % 2
+    return [((z_at - step + rows) % rows) * 2 + (x_at if side == 0 else 1 - x_at) for step in range(rows) for side in range(2)]
+
+
+def swap_x(value, exp_devices):
+    return lax.ppermute(value, "exp", [(e, e ^ 1) for e in range(exp_devices)])
+
+
+def ring_z(value, exp_devices):
+    return lax.ppermute(value, "exp", [(e, (e + 2) % exp_devices) for e in range(exp_devices)])
+
+
+def swap_core(value):
+    return lax.ppermute(value, "ctx", [(c, c ^ 1) for c in range(lax.axis_size("ctx"))])
+
+
+def swap_y(value):
+    return lax.ppermute(value, "ctx", [(c, c ^ 2) for c in range(lax.axis_size("ctx"))])
+
+
+def gather_exp(block, exp_devices):
+    found = []
+    for step in range(exp_devices // 2):
+        found.append(block)
+        found.append(swap_x(block, exp_devices))
+        if step + 1 < exp_devices // 2:
+            block = ring_z(block, exp_devices)
+    return found
+
+
+def reduce_exp(blocks, exp_devices):
+    rows = exp_devices // 2
+    across = {}
+    for step in list(range(1, rows)) + [0]:
+        got = swap_x(blocks[2 * step + 1], exp_devices)
+        across[step] = blocks[2 * step].astype(jnp.float32) + got.astype(jnp.float32)
+    total = across[1]
+    for step in list(range(2, rows)) + [0]:
+        moved = ring_z(total.astype(jnp.bfloat16), exp_devices)
+        total = across[step] + moved.astype(jnp.float32)
+    return total
+
+
+def block_attention(q_nope, query_rope, query_pos, query_docs, latent, k_rope, doc_ids):
+    ctx_devices = lax.axis_size("ctx")
+    here = lax.axis_index("ctx")
+    block_len = latent.shape[0]
+    reach = min(ctx_devices - 1, 2)
+    lat_blocks, rope_blocks, doc_blocks = [latent], [k_rope], [doc_ids]
+    for back in range(1, reach + 1):
+        pairs = [(c, c + back) for c in range(ctx_devices - back)]
+        lat_blocks.append(lax.ppermute(latent, "ctx", pairs))
+        rope_blocks.append(lax.ppermute(k_rope, "ctx", pairs))
+        doc_blocks.append(lax.ppermute(doc_ids, "ctx", pairs))
+    keys = jnp.concatenate(lat_blocks, axis=0)
+    ropes = jnp.concatenate(rope_blocks, axis=0)
+    docs = jnp.concatenate(doc_blocks, axis=0)
+    local = jnp.arange(block_len, dtype=jnp.int32)
+    key_pos = jnp.concatenate([local + (here - back) * block_len for back in range(reach + 1)], axis=0)
+    allowed = (
+        (key_pos[None, :] <= query_pos[:, None])
+        & (key_pos[None, :] >= 0)
+        & (docs[None, :] == query_docs[:, None])
+    )
+    scores = jnp.where(allowed[None], key_scores(q_nope, query_rope, keys, ropes), masked_score)
+    top = jnp.max(scores, axis=2)
+    probs = jnp.where(allowed[None], jnp.exp(scores - top[:, :, None]), 0.0)
+    total = jnp.sum(probs, axis=2)
+    accum = jnp.einsum("hqk,kl->hql", probs.astype(jnp.bfloat16), keys, preferred_element_type=jnp.float32)
+    return (accum / total[:, :, None]).astype(jnp.bfloat16), keys
+
+
+def down_kernel(h0, h1, h2, h3, w0, w1, w2, w3, scale, out):
+    total = jnp.dot(h0[...], w0[...], preferred_element_type=jnp.float32)
+    total += jnp.dot(h1[...], w1[...], preferred_element_type=jnp.float32)
+    total += jnp.dot(h2[...], w2[...], preferred_element_type=jnp.float32)
+    total += jnp.dot(h3[...], w3[...], preferred_element_type=jnp.float32)
+    out[...] = (total * scale[...]).astype(out.dtype)
+
+
+def down_rows(hidden, weights, scale):
+    rows, units = hidden[0].shape
+    width = weights[0].shape[1]
+    tile = 512
+    return pl.pallas_call(
+        down_kernel,
+        grid=(width // tile,),
+        in_specs=[pl.BlockSpec((rows, units), lambda n: (0, 0))] * 4
+        + [pl.BlockSpec((units, tile), lambda n: (0, n))] * 4
+        + [pl.BlockSpec((rows, 1), lambda n: (0, 0))],
+        out_specs=pl.BlockSpec((rows, tile), lambda n: (0, n)),
+        out_shape=jax.ShapeDtypeStruct((rows, width), jnp.bfloat16),
+        compiler_params=pltpu.CompilerParams(vmem_limit_bytes=32 * 1024 * 1024),
+        cost_estimate=pl.CostEstimate(
+            flops=8 * rows * units * width,
+            bytes_accessed=8 * units * width + 2 * rows * width,
+            transcendentals=0,
+        ),
+    )(*hidden, *weights, scale)
+
+
+def after(value, earlier):
+    return lax.optimization_barrier((value, earlier))[0]
+
+
+def dense_device(
+    residual_in,
+    norm_gain,
+    q_nope,
+    q_rope,
+    latent,
+    k_rope,
+    doc_ids,
+    uv_weight,
+    out_weight,
+    expert_ids,
+    gate_levels,
+    bin_ids,
+    gate_weight,
+    up_weight,
+    down_weight,
+):
+    exp_devices = lax.axis_size("exp")
+    ctx_here, exp_here = lax.axis_index("ctx"), lax.axis_index("exp")
+    block_len, head_count, lat_width = q_nope.shape
+    token_count = residual_in.shape[0]
+    order = jnp.stack(relative_order(exp_devices)).astype(jnp.int32)
+
+    def reorder(value):
+        return value.reshape((exp_devices, token_count) + value.shape[1:])[order].reshape(value.shape)
+
+    levels = gate_levels.astype(jnp.float32)
+    route_weights = levels / jnp.sum(levels, axis=1, keepdims=True)
+    named = expert_ids[:, :, None] == jnp.arange(exp_devices, dtype=jnp.int32)[None, None, :]
+    table = jnp.concatenate(
+        [
+            jnp.sum(jnp.where(named, route_weights[:, :, None], 0.0), axis=1),
+            jnp.sum(jnp.where(named, bin_ids.astype(jnp.float32)[:, :, None], 0.0), axis=1),
+        ],
+        axis=1,
+    )
+    tables = reorder(lax.all_gather(table, "exp", axis=0, tiled=True))
+    mine = (jnp.arange(exp_devices, dtype=jnp.int32) == exp_here).astype(jnp.float32)
+    row_scale = jnp.sum(tables[:, :exp_devices] * mine, axis=1, keepdims=True)
+    row_bins = jnp.sum(tables[:, exp_devices:] * mine, axis=1).astype(jnp.int32)
+
+    query_first = ctx_here * block_len
+    query_pos = reorder(query_first + jnp.arange(block_len, dtype=jnp.int32))
+    context, keys = block_attention(
+        reorder(q_nope),
+        reorder(q_rope).reshape(block_len, head_count, k_rope.shape[1]),
+        query_pos,
+        reorder(doc_ids),
+        latent,
+        k_rope,
+        doc_ids,
+    )
+
+    w_gate, w_up, w_down = gate_weight[0], up_weight[0], down_weight[0]
+    far_gate = swap_y(after(w_gate, keys))
+    far_up = swap_y(after(w_up, far_gate))
+    far_down = swap_y(after(w_down, far_up))
+    gates = [w_gate, swap_core(w_gate), far_gate, swap_core(far_gate)]
+    ups = [w_up, swap_core(w_up), far_up, swap_core(far_up)]
+    downs = [w_down, swap_core(w_down), far_down, swap_core(far_down)]
+
+    values = project_values(context, uv_weight)
+    partial = jnp.dot(values, out_weight, preferred_element_type=jnp.float32).astype(jnp.bfloat16)
+    partial = partial.reshape(exp_devices, token_count, partial.shape[1])
+    attended = reduce_exp([partial[at] for at in range(exp_devices)], exp_devices)
+    stream_state = residual_in.astype(jnp.float32) + attended
+    normed = (
+        stream_state
+        * lax.rsqrt(jnp.mean(stream_state * stream_state, axis=1, keepdims=True) + norm_eps)
+        * norm_gain
+    ).astype(jnp.bfloat16)
+    rows = jnp.concatenate(gather_exp(normed, exp_devices), axis=0)
+    hidden, energy = [], 0.0
+    for gate, up in zip(gates, ups):
+        part, part_energy = expert_hidden(rows, gate, up)
+        hidden.append(part)
+        energy = energy + part_energy
+    expert_out = down_rows(hidden, downs, row_scale)
+    expert_out = expert_out.reshape(exp_devices, token_count, expert_out.shape[1])
+    mixture = reduce_exp([expert_out[at] for at in range(exp_devices)], exp_devices)
+    layer_out = (stream_state + mixture).astype(jnp.bfloat16)
+
+    lanes = 128
+    high = (row_bins[:, None] // lanes == jnp.arange(NBINS // lanes, dtype=jnp.int32)[None, :]).astype(jnp.float32)
+    low = (row_bins[:, None] % lanes == jnp.arange(lanes, dtype=jnp.int32)[None, :]).astype(jnp.float32)
+    counts = lax.dot_general(
+        high * energy[:, None], low, (((0,), (0,)), ((), ())), precision=lax.Precision.HIGHEST
+    ).reshape(2, 2, NBINS // 4)
+    y_here, core_here = ctx_here // 2, ctx_here % 2
+    counts = lax.dynamic_index_in_dim(counts, y_here, 0, keepdims=False) + swap_y(
+        lax.dynamic_index_in_dim(counts, 1 - y_here, 0, keepdims=False)
+    )
+    histogram = lax.dynamic_index_in_dim(counts, core_here, 0, keepdims=True) + swap_core(
+        lax.dynamic_index_in_dim(counts, 1 - core_here, 0, keepdims=True)
+    )
+    return (layer_out, histogram)
+
+
 def solution(mesh):
+    sizes = mesh.shape
+
+    def on_device(*arrays):
+        named_experts = arrays[9].shape[1]
+        dense = sizes["exp"] == 8 and sizes["ctx"] == 4 and named_experts == sizes["exp"]
+        return (dense_device if dense else routed_device)(*arrays)
+
     return jax.shard_map(
         on_device,
         mesh=mesh,

time: 677 us -> 293 us (0.43); the launches traced: 668 us -> 293 us
  waiting for transfers between devices: 392 us -> 139 us
  blocking collectives: 104 us -> 33.6 us
  matrix products: 73 us -> 37.6 us
  other arithmetic: 33 us -> 13.1 us
  starting transfers between devices: 20.5 us -> 39.4 us
  between operations: 14.2 us -> 1.17 us
  local copies, waits for them, and re-layouts: 32.4 us -> 23.1 us
    reduce_scatter x2 -> x0, waiting for transfers between devices: 228 us -> none  [the longest x1 130 us: on_device(): lax.psum_scatter(head_rows(jnp.int32(0), token_count * lax.axis_size('exp...]
    ppermute x0 -> x38, waiting for transfers between devices: none -> 139 us  [the longest x12 49.6 us: swap_x(): return lax.ppermute(value, 'exp', [(e, e ^ 1) for e in range(exp_devices)])]
    all_gather x2 -> x0, waiting for transfers between devices: 105 us -> none  [the longest x1 93.2 us: on_device(): lax.all_gather(incoming, 'ctx', axis=1, tiled=True)]
    all_to_all x1 -> x0, blocking collectives: 85.7 us -> none  [on_device(): lax.all_to_all(outgoing, 'exp', split_axis=0, concat_axis=1, tiled=True)]
    ppermute x0 -> x38, starting transfers between devices: none -> 39.4 us  [the longest x12 14.8 us: swap_x(): return lax.ppermute(value, 'exp', [(e, e ^ 1) for e in range(exp_devices)])]
    all_to_all x2 -> x0, waiting for transfers between devices: 33.7 us -> none  [the longest x1 33.7 us: on_device(): lax.all_to_all(expert_out[None], 'exp', split_axis=1, concat_axis=0, tile...]
    unnamed x6 -> x0, waiting for transfers between devices: 25.8 us -> none
    dot_general x5 -> x2, matrix products: 26.6 us -> 1.76 us  [the longest x1 1.14 us: dense_device(): jnp.dot(values, out_weight, preferred_element_type=jnp.float32)]
  transfers between devices with their start and end apart: 7 -> 38, of which waited for: 6 -> 20; matrix products, arithmetic and copies ran while one was open for 10% -> 18% of each run, Pallas kernels for 0% -> 0%
where the time goes in v1:
time: 293 us
  waiting for transfers between devices  139 us (47%)
  starting transfers between devices  39.4 us (13%)
  matrix products  37.6 us (13%)
  blocking collectives  33.6 us (11%)
  local copies, waits for them, and re-layouts  23.1 us (8%)
  other arithmetic  13.1 us (4%)
  Pallas kernels  5.78 us (2%)
    ppermute x12, waiting for transfers between devices, swap_x(): return lax.ppermute(value, 'exp', [(e, e ^ 1) for e in range(exp_devices)])  49.6 us
    ppermute x9, waiting for transfers between devices, ring_z(): lax.ppermute(value, 'exp', [(e, (e + 2) % exp_devices) for e in range(exp...  47.5 us
    ppermute x4, waiting for transfers between devices, swap_y(): lax.ppermute(value, 'ctx', [(c, c ^ 2) for c in range(lax.axis_size('ctx'...  36.9 us
    all_gather x1, blocking collectives, dense_device(): tables = reorder(lax.all_gather(table, 'exp', axis=0, tiled=True))  33.6 us
    ppermute x12, starting transfers between devices, swap_x(): return lax.ppermute(value, 'exp', [(e, e ^ 1) for e in range(exp_devices)])  14.8 us
    unnamed x40, local copies, waits for them, and re-layouts  11.1 us
    dot_general x4, matrix products, expert_hidden(): gate_part = jnp.dot(row_data, w_gate, preferred_element_type=jnp.float32)  10.2 us
    sub x1, matrix products, block_attention(): probs = jnp.where(allowed[None], jnp.exp(scores - top[:, :, None]), 0.0)  9.69 us
  transfers between devices with their start and end apart: 38, of which 20 were waited for; matrix products, arithmetic and copies ran while one was open for 18% of the time, Pallas kernels for 0%

profile of v1, /device:TPU:0, one launch (start us, length us, event | category | flops | bytes accessed | tf_op | source)
XLA Modules:
  0.0 292.8 jit_solution(6345961600575531432)
XLA Ops:
  3.2 4.4 %collective-permute-start.5 = (bf16[512,64]{0,1:T(8,128)(2,1)}, bf16[512,64]{0,1:T(8,128)(2,1)S(1)}, u32[]{:S(2)}, u32[]{:S(2)}) collective-permute-start(bf16[512,64]{0,1:T(8,128)(2,1)} %param.20), channel_id=1, source_target_pairs={{0,16},{8,24},{1,17},{9,25},{2,18},{10,26},{3,19},{11,27},{4,20},{... | collective-permute-start | bytes 196616 | tf_op jit(solution)/shard_map/ppermute | solution.py:233
  17.5 3.9 %gather_fusion.2 = bf16[8,64,2,512]{3,2,1,0:T(2,128)(2,1)S(1)} fusion(bf16[8,64,2,512]{3,2,1,0:T(2,128)(2,1)} %bitcast.76, s32[1024]{0:T(1024)S(1)} %pad_clamp_fusion), kind=kCustom, calls=%fused_computation.2 | custom fusion | bytes 2097184 | tf_op jit(solution)/shard_map/gather | solution.py:310
  27.8 3.6 %fusion.14 = f32[1536,512,2]{1,0,2:T(8,128)} fusion(bf16[512,2,64]{2,1,0:T(2,128)(2,1)S(1)} %reshape.613, bf16[512,64]{0,1:T(8,128)(2,1)S(1)} %collective-permute-done.5, bf16[512,64]{0,1:T(8,128)(2,1)S(1)} %collective-permute-done.4, bf16[512,64]{0,1:T(8,128)(2,1)S(1)} %copy-done.9), kind=kOutput, calls=%fused_computation.35 | convolution fusion | flops 201916416 | bytes 6619136 | tf_op jit(solution)/shard_map/qhr,kr->hqk/dot_general | solution.py:27
  32.5 3.9 %collective-permute-done.3 = bf16[512,512]{1,0:T(8,128)(2,1)S(1)} collective-permute-done((bf16[512,512]{1,0:T(8,128)(2,1)}, bf16[512,512]{1,0:T(8,128)(2,1)S(1)}, u32[]{:S(2)}, u32[]{:S(2)}) %collective-permute-start.3) | collective-permute-done | bytes 524320 | tf_op jit(solution)/shard_map/ppermute | solution.py:232
  37.7 9.7 %fusion.40 = (f32[2,512]{1,0:T(2,128)S(1)}, bf16[2,512,1536]{1,2,0:T(8,128)(2,1)}) fusion(pred[512,1536]{0,1:T(8,128)(4,1)} %compare_and_fusion, f32[1536,512,2]{1,0,2:T(8,128)} %fusion.14, bf16[512,2,512]{2,0,1:T(8,128)(2,1)S(1)} %bitcast.77, bf16[1536,512]{1,0:T(8,128)(2,1)} %copy-done.8), kind=kOutput, calls=%fused_computation.105 | convolution fusion | flops 1621624320 | bytes 12849152 | tf_op jit(solution)/shard_map/sub | solution.py:247
  47.4 4.5 %convolution_convert_fusion.1 = bf16[2,512,128]{1,2,0:T(8,128)(2,1)S(1)} fusion(bf16[2,512,128]{2,1,0:T(8,128)(2,1)} %param.22, bf16[1536,512]{1,0:T(8,128)(2,1)} %copy-done.8, bf16[2,512,1536]{1,2,0:T(8,128)(2,1)} %get-tuple-element.33, f32[2,512]{1,0:T(2,128)S(1)} %get-tuple-element.32), kind=kOutput, calls=%fused_computation.15 | convolution fusion | flops 1746010112 | bytes 5246976 | tf_op jit(solution)/shard_map/hql,hlv->qhv/dot_general | solution.py:51
  55.3 11.4 %collective-permute-done.9 = bf16[64,3584]{1,0:T(8,128)(2,1)S(1)} collective-permute-done((bf16[64,3584]{1,0:T(8,128)(2,1)S(1)}, bf16[64,3584]{1,0:T(8,128)(2,1)S(1)}, u32[]{:S(2)}, u32[]{:S(2)}) %collective-permute-start.9) | collective-permute-done | bytes 458784 | tf_op jit(solution)/shard_map/ppermute | solution.py:186
  70.0 6.6 %collective-permute-done.8 = bf16[64,3584]{1,0:T(8,128)(2,1)S(1)} collective-permute-done((bf16[64,3584]{1,0:T(8,128)(2,1)S(1)}, bf16[64,3584]{1,0:T(8,128)(2,1)S(1)}, u32[]{:S(2)}, u32[]{:S(2)}) %collective-permute-start.8) | collective-permute-done | bytes 458784 | tf_op jit(solution)/shard_map/ppermute | solution.py:186
  79.9 6.5 %collective-permute-done.7 = bf16[64,3584]{1,0:T(8,128)(2,1)S(1)} collective-permute-done((bf16[64,3584]{1,0:T(8,128)(2,1)S(1)}, bf16[64,3584]{1,0:T(8,128)(2,1)S(1)}, u32[]{:S(2)}, u32[]{:S(2)}) %collective-permute-start.7) | collective-permute-done | bytes 458784 | tf_op jit(solution)/shard_map/ppermute | solution.py:186
  86.4 3.2 %collective-permute-done.11 = bf16[64,3584]{1,0:T(8,128)(2,1)S(1)} collective-permute-done((bf16[64,3584]{1,0:T(8,128)(2,1)S(1)}, bf16[64,3584]{1,0:T(8,128)(2,1)S(1)}, u32[]{:S(2)}, u32[]{:S(2)}) %collective-permute-start.11) | collective-permute-done | bytes 458784 | tf_op jit(solution)/shard_map/ppermute | solution.py:190
  93.9 6.2 %collective-permute-done.12 = bf16[64,3584]{1,0:T(8,128)(2,1)S(1)} collective-permute-done((bf16[64,3584]{1,0:T(8,128)(2,1)S(1)}, bf16[64,3584]{1,0:T(8,128)(2,1)S(1)}, u32[]{:S(2)}, u32[]{:S(2)}) %collective-permute-start.12) | collective-permute-done | bytes 458784 | tf_op jit(solution)/shard_map/ppermute | solution.py:190
  104.0 33.6 %all-gather = f32[8,64,16]{1,2,0:T(8,128)S(1)} all-gather(f32[1,64,16]{1,2,0:T(8,128)S(1)} %maximum_bitcast_fusion.2), channel_id=1, replica_groups=mesh['ctx'=4,'exp'=8] {'exp'}, dimensions={0}, use_global_device_ids=true | all-gather | bytes 36864 | tf_op jit(solution)/shard_map/all_gather | solution.py:322
  144.7 8.8 %collective-permute-done.16 = bf16[64,3584]{1,0:T(8,128)(2,1)S(1)} collective-permute-done((bf16[64,3584]{1,0:T(8,128)(2,1)}, bf16[64,3584]{1,0:T(8,128)(2,1)S(1)}, u32[]{:S(2)}, u32[]{:S(2)}) %collective-permute-start.16) | collective-permute-done | bytes 458784 | tf_op jit(solution)/shard_map/ppermute | solution.py:190
  157.6 4.8 %collective-permute-done.17 = bf16[64,3584]{1,0:T(8,128)(2,1)S(1)} collective-permute-done((bf16[64,3584]{1,0:T(8,128)(2,1)S(1)}, bf16[64,3584]{1,0:T(8,128)(2,1)S(1)}, u32[]{:S(2)}, u32[]{:S(2)}) %collective-permute-start.17) | collective-permute-done | bytes 458784 | tf_op jit(solution)/shard_map/ppermute | solution.py:186
  162.4 3.8 %collective-permute-done.18 = bf16[64,3584]{1,0:T(8,128)(2,1)S(1)} collective-permute-done((bf16[64,3584]{1,0:T(8,128)(2,1)S(1)}, bf16[64,3584]{1,0:T(8,128)(2,1)S(1)}, u32[]{:S(2)}, u32[]{:S(2)}) %collective-permute-start.18) | collective-permute-done | bytes 458784 | tf_op jit(solution)/shard_map/ppermute | solution.py:190
  167.9 7.3 %collective-permute-done.23 = bf16[3584,256]{1,0:T(8,128)(2,1)S(1)} collective-permute-done((bf16[3584,256]{1,0:T(8,128)(2,1)}, bf16[3584,256]{1,0:T(8,128)(2,1)S(1)}, u32[]{:S(2)}, u32[]{:S(2)}) %collective-permute-start.23) | collective-permute-done | bytes 1835040 | tf_op jit(solution)/shard_map/ppermute | solution.py:198
  177.5 3.9 %fusion.35 = f32[512,256]{1,0:T(8,128)S(1)} fusion(bf16[512,3584]{1,0:T(8,128)(2,1)} %constant_dynamic-update-slice_fusion.3, bf16[1,3584,256]{2,1,0:T(8,128)(2,1)} %param.27), kind=kOutput, calls=%fused_computation.100 | convolution fusion | flops 939524096 | bytes 6029312 | tf_op jit(solution)/shard_map/dot_general | solution.py:68
  188.0 29.6 %collective-permute-done.27.w2 = bf16[256,3584]{1,0:T(8,128)(2,1)S(1)} collective-permute-done((bf16[256,3584]{1,0:T(8,128)(2,1)S(1)}, bf16[256,3584]{1,0:T(8,128)(2,1)S(1)}, u32[]{:S(2)}, u32[]{:S(2)}) %collective-permute-start.27) | collective-permute-done | bytes 1835040 | tf_op jit(solution)/shard_map/ppermute | solution.py:198
  225.3 5.8 %shard_map.158 = bf16[512,3584]{1,0:T(8,128)(2,1)S(1)} custom-call(bf16[512,256]{1,0:T(8,128)(2,1)S(1)} %get-tuple-element.29.h0, bf16[512,256]{1,0:T(8,128)(2,1)S(1)} %get-tuple-element.13.h1, bf16[512,256]{1,0:T(8,128)(2,1)S(1)} %get-tuple-element.15.h2, bf16[512,256]{1,0:T(8,128)(2,1)S(1)} %get-tuple-element.17.h3, bf16[256,3584]{1,0:T(8,128)(2,1)S(1)} %bitcast.75, ...), custom_call_target="tpu_custom_call" | custom-call | flops 3758096384 | bytes 11010048 | tf_op jit(solution)/shard_map/pallas_call | solution.py:265
  234.4 11.3 %collective-permute-done.32 = bf16[64,3584]{1,0:T(8,128)(2,1)S(1)} collective-permute-done((bf16[64,3584]{1,0:T(8,128)(2,1)S(1)}, bf16[64,3584]{1,0:T(8,128)(2,1)S(1)}, u32[]{:S(2)}, u32[]{:S(2)}) %collective-permute-start.32) | collective-permute-done | bytes 458784 | tf_op jit(solution)/shard_map/ppermute | solution.py:186
  248.2 7.5 %collective-permute-done.31 = bf16[64,3584]{1,0:T(8,128)(2,1)} collective-permute-done((bf16[64,3584]{1,0:T(8,128)(2,1)}, bf16[64,3584]{1,0:T(8,128)(2,1)}, u32[]{:S(2)}, u32[]{:S(2)}) %collective-permute-start.31) | collective-permute-done | bytes 458784 | tf_op jit(solution)/shard_map/ppermute | solution.py:186
  255.6 4.9 %collective-permute-done.33 = bf16[64,3584]{1,0:T(8,128)(2,1)} collective-permute-done((bf16[64,3584]{1,0:T(8,128)(2,1)}, bf16[64,3584]{1,0:T(8,128)(2,1)}, u32[]{:S(2)}, u32[]{:S(2)}) %collective-permute-start.33) | collective-permute-done | bytes 458784 | tf_op jit(solution)/shard_map/ppermute | solution.py:190
  266.4 9.4 %collective-permute-done.34 = bf16[64,3584]{1,0:T(8,128)(2,1)} collective-permute-done((bf16[64,3584]{1,0:T(8,128)(2,1)}, bf16[64,3584]{1,0:T(8,128)(2,1)}, u32[]{:S(2)}, u32[]{:S(2)}) %collective-permute-start.34) | collective-permute-done | bytes 458784 | tf_op jit(solution)/shard_map/ppermute | solution.py:190
  279.9 10.3 %collective-permute-done.35 = bf16[64,3584]{1,0:T(8,128)(2,1)} collective-permute-done((bf16[64,3584]{1,0:T(8,128)(2,1)}, bf16[64,3584]{1,0:T(8,128)(2,1)}, u32[]{:S(2)}, u32[]{:S(2)}) %collective-permute-start.35) | collective-permute-done | bytes 458784 | tf_op jit(solution)/shard_map/ppermute | solution.py:190
  (158 shorter events, 86.8 us)
Async XLA Ops:
  0.7 27.1 %collective-permute-start.4 = (bf16[512,64]{0,1:T(8,128)(2,1)}, bf16[512,64]{0,1:T(8,128)(2,1)S(1)}, u32[]{:S(2)}, u32[]{:S(2)}) collective-permute-start(bf16[512,64]{0,1:T(8,128)(2,1)} %param.20), channel_id=1, source_target_pairs={{0,8},{8,16},{16,24},{1,9},{9,17},{17,25},{2,10},{10,18},{18,26},{... | collective-permute-start | bytes 196616 | tf_op jit(solution)/shard_map/ppermute | solution.py:233
  3.2 24.6 %collective-permute-start.5 = (bf16[512,64]{0,1:T(8,128)(2,1)}, bf16[512,64]{0,1:T(8,128)(2,1)S(1)}, u32[]{:S(2)}, u32[]{:S(2)}) collective-permute-start(bf16[512,64]{0,1:T(8,128)(2,1)} %param.20), channel_id=1, source_target_pairs={{0,16},{8,24},{1,17},{9,25},{2,18},{10,26},{3,19},{11,27},{4,20},{... | collective-permute-start | bytes 196616 | tf_op jit(solution)/shard_map/ppermute | solution.py:233
  7.6 16.3 %collective-permute-start = (s32[512]{0:T(512)}, s32[512]{0:T(512)S(1)}, u32[]{:S(2)}, u32[]{:S(2)}) collective-permute-start(s32[512]{0:T(512)} %param.21), channel_id=1, source_target_pairs={{0,8},{8,16},{16,24},{1,9},{9,17},{17,25},{2,10},{10,18},{18,26},{... | collective-permute-start | bytes 6152 | tf_op jit(solution)/shard_map/ppermute | solution.py:234
  9.0 16.4 %collective-permute-start.1 = (s32[512]{0:T(512)}, s32[512]{0:T(512)S(1)}, u32[]{:S(2)}, u32[]{:S(2)}) collective-permute-start(s32[512]{0:T(512)} %param.21), channel_id=1, source_target_pairs={{0,16},{8,24},{1,17},{9,25},{2,18},{10,26},{3,19},{11,27},{4,20},{... | collective-permute-start | bytes 6152 | tf_op jit(solution)/shard_map/ppermute | solution.py:234
  10.8 20.6 %collective-permute-start.2 = (bf16[512,512]{1,0:T(8,128)(2,1)}, bf16[512,512]{1,0:T(8,128)(2,1)}, u32[]{:S(2)}, u32[]{:S(2)}) collective-permute-start(bf16[512,512]{1,0:T(8,128)(2,1)} %param.19), channel_id=1, source_target_pairs={{0,8},{8,16},{16,24},{1,9},{9,17},{17,25},{2,10},{10,18},{18,26},{... | collective-permute-start | bytes 1572872 | tf_op jit(solution)/shard_map/ppermute | solution.py:232
  54.8 21.8 %collective-permute-start.8 = (bf16[64,3584]{1,0:T(8,128)(2,1)S(1)}, bf16[64,3584]{1,0:T(8,128)(2,1)S(1)}, u32[]{:S(2)}, u32[]{:S(2)}) collective-permute-start(bf16[64,3584]{1,0:T(8,128)(2,1)S(1)} %get-tuple-element.26), channel_id=1, source_target_pairs={{0,1},{1,0},{2,3},{3,2},{4,5},{5,4},{6,7},{7,6},{8,9},{9,8},{10,11... | collective-permute-start | bytes 1376264 | tf_op jit(solution)/shard_map/ppermute | solution.py:186
  68.5 17.9 %collective-permute-start.7 = (bf16[64,3584]{1,0:T(8,128)(2,1)S(1)}, bf16[64,3584]{1,0:T(8,128)(2,1)S(1)}, u32[]{:S(2)}, u32[]{:S(2)}) collective-permute-start(bf16[64,3584]{1,0:T(8,128)(2,1)S(1)} %get-tuple-element.27), channel_id=1, source_target_pairs={{0,1},{1,0},{2,3},{3,2},{4,5},{5,4},{6,7},{7,6},{8,9},{9,8},{10,11... | collective-permute-start | bytes 1376264 | tf_op jit(solution)/shard_map/ppermute | solution.py:186
  78.4 15.5 %collective-permute-start.6 = (bf16[64,3584]{1,0:T(8,128)(2,1)S(1)}, bf16[64,3584]{1,0:T(8,128)(2,1)S(1)}, u32[]{:S(2)}, u32[]{:S(2)}) collective-permute-start(bf16[64,3584]{1,0:T(8,128)(2,1)S(1)} %get-tuple-element.24), channel_id=1, source_target_pairs={{0,1},{1,0},{2,3},{3,2},{4,5},{5,4},{6,7},{7,6},{8,9},{9,8},{10,11... | collective-permute-start | bytes 1376264 | tf_op jit(solution)/shard_map/ppermute | solution.py:186
  89.8 127.8 %collective-permute-start.20 = (bf16[3584,256]{1,0:T(8,128)(2,1)}, bf16[3584,256]{1,0:T(8,128)(2,1)}, u32[]{:S(2)}, u32[]{:S(2)}) collective-permute-start(bf16[3584,256]{1,0:T(8,128)(2,1)} %bitcast.17), channel_id=1, source_target_pairs={{0,8},{8,0},{16,24},{24,16},{1,9},{9,1},{17,25},{25,17},{2,10},{10... | collective-permute-start | bytes 5505032 | tf_op jit(solution)/shard_map/ppermute | solution.py:194
  89.9 131.5 %collective-permute-start.21 = (bf16[3584,256]{1,0:T(8,128)(2,1)}, bf16[3584,256]{1,0:T(8,128)(2,1)}, u32[]{:S(2)}, u32[]{:S(2)}) collective-permute-start(bf16[3584,256]{1,0:T(8,128)(2,1)} %bitcast.18), channel_id=1, source_target_pairs={{0,8},{8,0},{16,24},{24,16},{1,9},{9,1},{17,25},{25,17},{2,10},{10... | collective-permute-start | bytes 5505032 | tf_op jit(solution)/shard_map/ppermute | solution.py:194
  90.4 48.0 %collective-permute-start.22 = (bf16[3584,256]{1,0:T(8,128)(2,1)}, bf16[3584,256]{1,0:T(8,128)(2,1)}, u32[]{:S(2)}, u32[]{:S(2)}) collective-permute-start(bf16[3584,256]{1,0:T(8,128)(2,1)} %bitcast.17), channel_id=1, source_target_pairs={{0,16},{8,24},{16,0},{24,8},{1,17},{9,25},{17,1},{25,9},{2,18},{10... | collective-permute-start | bytes 5505032 | tf_op jit(solution)/shard_map/ppermute | solution.py:198
  101.7 39.3 %collective-permute-start.13 = (bf16[64,3584]{1,0:T(8,128)(2,1)}, bf16[64,3584]{1,0:T(8,128)(2,1)}, u32[]{:S(2)}, u32[]{:S(2)}) collective-permute-start(bf16[64,3584]{1,0:T(8,128)(2,1)} %get-tuple-element.19), channel_id=1, source_target_pairs={{0,1},{1,0},{2,3},{3,2},{4,5},{5,4},{6,7},{7,6},{8,9},{9,8},{10,11... | collective-permute-start | bytes 1376264 | tf_op jit(solution)/shard_map/ppermute | solution.py:186
  103.9 37.1 %collective-permute-start.14 = (bf16[64,3584]{1,0:T(8,128)(2,1)}, bf16[64,3584]{1,0:T(8,128)(2,1)}, u32[]{:S(2)}, u32[]{:S(2)}) collective-permute-start(bf16[64,3584]{1,0:T(8,128)(2,1)} %get-tuple-element.19), channel_id=1, source_target_pairs={{0,2},{1,3},{2,4},{3,5},{4,6},{5,7},{6,0},{7,1},{8,10},{9,11},{10,... | collective-permute-start | bytes 1376264 | tf_op jit(solution)/shard_map/ppermute | solution.py:190
  138.5 36.7 %collective-permute-start.23 = (bf16[3584,256]{1,0:T(8,128)(2,1)}, bf16[3584,256]{1,0:T(8,128)(2,1)S(1)}, u32[]{:S(2)}, u32[]{:S(2)}) collective-permute-start(bf16[3584,256]{1,0:T(8,128)(2,1)} %bitcast.18), channel_id=1, source_target_pairs={{0,16},{8,24},{16,0},{24,8},{1,17},{9,25},{17,1},{25,9},{2,18},{10... | collective-permute-start | bytes 5505032 | tf_op jit(solution)/shard_map/ppermute | solution.py:198
  141.0 15.0 %collective-permute-start.15 = (bf16[64,3584]{1,0:T(8,128)(2,1)}, bf16[64,3584]{1,0:T(8,128)(2,1)S(1)}, u32[]{:S(2)}, u32[]{:S(2)}) collective-permute-start(bf16[64,3584]{1,0:T(8,128)(2,1)} %collective-permute-done.14), channel_id=1, source_target_pairs={{0,1},{1,0},{2,3},{3,2},{4,5},{5,4},{6,7},{7,6},{8,9},{9,8},{10,11... | collective-permute-start | bytes 1376264 | tf_op jit(solution)/shard_map/ppermute | solution.py:186
  162.4 24.3 %collective-permute-start.24 = (bf16[3584,256]{1,0:T(8,128)(2,1)}, bf16[3584,256]{1,0:T(8,128)(2,1)S(1)}, u32[]{:S(2)}, u32[]{:S(2)}) collective-permute-start(bf16[3584,256]{1,0:T(8,128)(2,1)} %collective-permute-done.22), channel_id=1, source_target_pairs={{0,8},{8,0},{16,24},{24,16},{1,9},{9,1},{17,25},{25,17},{2,10},{10... | collective-permute-start | bytes 5505032 | tf_op jit(solution)/shard_map/ppermute | solution.py:194
  175.2 50.2 %collective-permute-start.26 = (bf16[256,3584]{1,0:T(8,128)(2,1)S(1)}, bf16[256,3584]{1,0:T(8,128)(2,1)S(1)}, u32[]{:S(2)}, u32[]{:S(2)}) collective-permute-start(bf16[256,3584]{1,0:T(8,128)(2,1)S(1)} %bitcast.73), channel_id=1, source_target_pairs={{0,8},{8,0},{16,24},{24,16},{1,9},{9,1},{17,25},{25,17},{2,10},{10... | collective-permute-start | bytes 5505032 | tf_op jit(solution)/shard_map/ppermute | solution.py:194
  175.6 42.0 %collective-permute-start.27 = (bf16[256,3584]{1,0:T(8,128)(2,1)S(1)}, bf16[256,3584]{1,0:T(8,128)(2,1)S(1)}, u32[]{:S(2)}, u32[]{:S(2)}) collective-permute-start(bf16[256,3584]{1,0:T(8,128)(2,1)S(1)} %bitcast.74), channel_id=1, source_target_pairs={{0,16},{8,24},{16,0},{24,8},{1,17},{9,25},{17,1},{25,9},{2,18},{10... | collective-permute-start | bytes 5505032 | tf_op jit(solution)/shard_map/ppermute | solution.py:198
  186.7 37.5 %collective-permute-start.25 = (bf16[3584,256]{1,0:T(8,128)(2,1)S(1)}, bf16[3584,256]{1,0:T(8,128)(2,1)S(1)}, u32[]{:S(2)}, u32[]{:S(2)}) collective-permute-start(bf16[3584,256]{1,0:T(8,128)(2,1)S(1)} %collective-permute-done.23), channel_id=1, source_target_pairs={{0,8},{8,0},{16,24},{24,16},{1,9},{9,1},{17,25},{25,17},{2,10},{10... | collective-permute-start | bytes 5505032 | tf_op jit(solution)/shard_map/ppermute | solution.py:194
  233.9 21.7 %collective-permute-start.31 = (bf16[64,3584]{1,0:T(8,128)(2,1)}, bf16[64,3584]{1,0:T(8,128)(2,1)}, u32[]{:S(2)}, u32[]{:S(2)}) collective-permute-start(bf16[64,3584]{1,0:T(8,128)(2,1)} %get-tuple-element.22), channel_id=1, source_target_pairs={{0,1},{1,0},{2,3},{3,2},{4,5},{5,4},{6,7},{7,6},{8,9},{9,8},{10,11... | collective-permute-start | bytes 1376264 | tf_op jit(solution)/shard_map/ppermute | solution.py:186
  246.6 14.0 %collective-permute-start.33 = (bf16[64,3584]{1,0:T(8,128)(2,1)}, bf16[64,3584]{1,0:T(8,128)(2,1)}, u32[]{:S(2)}, u32[]{:S(2)}) collective-permute-start(bf16[64,3584]{1,0:T(8,128)(2,1)} %add_convert_fusion.3), channel_id=1, source_target_pairs={{0,2},{1,3},{2,4},{3,5},{4,6},{5,7},{6,0},{7,1},{8,10},{9,11},{10,... | collective-permute-start | bytes 1376264 | tf_op jit(solution)/shard_map/ppermute | solution.py:190
  246.6 19.8 %collective-permute-start.30 = (bf16[64,3584]{1,0:T(8,128)(2,1)}, bf16[64,3584]{1,0:T(8,128)(2,1)}, u32[]{:S(2)}, u32[]{:S(2)}) collective-permute-start(bf16[64,3584]{1,0:T(8,128)(2,1)} %get-tuple-element.23), channel_id=1, source_target_pairs={{0,1},{1,0},{2,3},{3,2},{4,5},{5,4},{6,7},{7,6},{8,9},{9,8},{10,11... | collective-permute-start | bytes 1376264 | tf_op jit(solution)/shard_map/ppermute | solution.py:186
  263.5 14.6 %collective-permute-start.36 = (f32[2,512]{1,0:T(2,128)S(1)}, f32[2,512]{1,0:T(2,128)S(1)}, u32[]{:S(2)}, u32[]{:S(2)}) collective-permute-start(f32[2,512]{1,0:T(2,128)S(1)} %dynamic-slice_bitcast_fusion), channel_id=1, source_target_pairs={{0,16},{8,24},{16,0},{24,8},{1,17},{9,25},{17,1},{25,9},{2,18},{10... | collective-permute-start | bytes 12296 | tf_op jit(solution)/shard_map/ppermute | solution.py:198
  264.9 15.0 %collective-permute-start.29 = (bf16[64,3584]{1,0:T(8,128)(2,1)}, bf16[64,3584]{1,0:T(8,128)(2,1)}, u32[]{:S(2)}, u32[]{:S(2)}) collective-permute-start(bf16[64,3584]{1,0:T(8,128)(2,1)} %get-tuple-element.20), channel_id=1, source_target_pairs={{0,1},{1,0},{2,3},{3,2},{4,5},{5,4},{6,7},{7,6},{8,9},{9,8},{10,11... | collective-permute-start | bytes 1376264 | tf_op jit(solution)/shard_map/ppermute | solution.py:186
  (30 other events, 648.4 us)

commit v2 on v0

--- a/solution.py
+++ b/solution.py
@@ -1,6 +1,11 @@
+import functools
+import math
+
 import jax
 import jax.numpy as jnp
 from jax import lax
+from jax.experimental import pallas as pl
+from jax.experimental.pallas import tpu as pltpu
 from jax.sharding import PartitionSpec as P
 
 HID = 1024
@@ -10,6 +15,9 @@
 softmax_scale = 192.0 ** (-0.5)
 norm_eps = 1e-06
 masked_score = -1e30
+LOG2_E = math.log2(math.e)
+FIRST_ROWS = (448, 1280)
+VMEM_BYTES = 61 * 1024 * 1024
 
 
 def route_slots(expert_ids, experts, capacity):
@@ -74,7 +82,7 @@
     return jnp.dot(energy[None, :], onehot, precision=lax.Precision.HIGHEST)[0]
 
 
-def on_device(
+def routed_device(
     residual_in,
     norm_gain,
     q_nope,
@@ -173,7 +181,406 @@
     return (layer_out, histogram)
 
 
+def relative_order(exp_devices):
+    here = lax.axis_index("exp")
+    rows = exp_devices // 2
+    z_at, x_at = here // 2, here % 2
+    return jnp.stack(
+        [
+            ((z_at - step + rows) % rows) * 2 + (x_at if side == 0 else 1 - x_at)
+            for step in range(rows)
+            for side in range(2)
+        ]
+    ).astype(jnp.int32)
+
+
+def swap_exp(value, bit=1):
+    return lax.ppermute(value, "exp", [(e, e ^ bit) for e in range(lax.axis_size("exp"))])
+
+
+def ring_z(value):
+    exp_devices = lax.axis_size("exp")
+    return lax.ppermute(value, "exp", [(e, (e + 2) % exp_devices) for e in range(exp_devices)])
+
+
+def swap_ctx(value, bit):
+    return lax.ppermute(value, "ctx", [(c, c ^ bit) for c in range(lax.axis_size("ctx"))])
+
+
+def after(value, earlier):
+    return lax.optimization_barrier((value, earlier))[0]
+
+
+def one_step(work, *inputs):
+    taken = lax.axis_index("ctx") // lax.axis_size("ctx") == 0
+
+    def blank(*arrays):
+        return jax.tree.map(lambda leaf: jnp.zeros(leaf.shape, leaf.dtype), jax.eval_shape(work, *arrays))
+
+    return lax.cond(taken, work, blank, *inputs)
+
+
+def reduce_exp(*blocks):
+    rows, across = len(blocks) // 2, {}
+    for step in list(range(1, rows)) + [0]:
+        got = swap_exp(blocks[2 * step + 1])
+        across[step] = blocks[2 * step].astype(jnp.float32) + got.astype(jnp.float32)
+    total = across[1]
+    for step in list(range(2, rows)) + [0]:
+        total = across[step] + ring_z(total.astype(jnp.bfloat16)).astype(jnp.float32)
+    return total
+
+
+def gather_exp(block):
+    found = []
+    for step in range(lax.axis_size("exp") // 2):
+        if step:
+            block = ring_z(after(block, found[-3]) if step > 1 else block)
+            found.append(block)
+        found.append(swap_exp(block))
+    return found
+
+
+def attend_kernel(scalars, q_nope, q_rope, own, near, far, uv, out, *, heads, rope_width):
+    tile = out.shape[0]
+    lat_width = uv.shape[1]
+    first = pl.program_id(0) * tile
+    keys = own.shape[0]
+    doc_at = lat_width + rope_width
+    pick = (lax.broadcasted_iota(jnp.int32, (8, 128), 1) == rope_width).astype(jnp.bfloat16)
+    query_docs = own[pl.ds(pl.multiple_of(first, tile), tile), lat_width:][:, rope_width : rope_width + 1].astype(jnp.float32)
+    over = (((1,), (1,)), ((), ()))
+    allowed = []
+    for back, block in enumerate((own, near, far)):
+        docs = lax.dot_general(pick, block[:, lat_width:], over, preferred_element_type=jnp.float32)[0:1, :]
+        docs = jnp.where(scalars[0] >= back, docs, -1.0)
+        same = docs == query_docs
+        if back == 0:
+            key_at = lax.broadcasted_iota(jnp.int32, (tile, keys), 1)
+            query_at = lax.broadcasted_iota(jnp.int32, (tile, keys), 0) + first
+            same = same & (key_at <= query_at)
+        allowed.append(same)
+    spare = jnp.zeros((tile, own.shape[1] - doc_at), jnp.bfloat16)
+    for head in range(heads):
+        query = jnp.concatenate(
+            [
+                q_nope[:, head * lat_width : (head + 1) * lat_width],
+                q_rope[:, head * rope_width : (head + 1) * rope_width],
+                spare,
+            ],
+            axis=1,
+        )
+        scores = []
+        for block, same in zip((own, near, far), allowed):
+            raw = lax.dot_general(query, block[...], over, preferred_element_type=jnp.float32)
+            scores.append(jnp.where(same, raw * (softmax_scale * LOG2_E), masked_score))
+        top = jnp.maximum(
+            jnp.maximum(jnp.max(scores[0], axis=1, keepdims=True), jnp.max(scores[1], axis=1, keepdims=True)),
+            jnp.max(scores[2], axis=1, keepdims=True),
+        )
+        total, accum = 0.0, 0.0
+        for block, score in zip((own, near, far), scores):
+            probs = jnp.exp2(score - top)
+            total = total + jnp.sum(probs, axis=1, keepdims=True)
+            accum = accum + jnp.dot(
+                probs.astype(jnp.bfloat16), block[:, :lat_width], preferred_element_type=jnp.float32
+            )
+        context = (accum / total).astype(jnp.bfloat16)
+        value = jnp.dot(context, uv[head], preferred_element_type=jnp.float32)
+        width = uv.shape[2]
+        out[:, head * width : (head + 1) * width] = value.astype(out.dtype)
+
+
+def attend(ctx_here, q_nope, q_rope, own, near, far, uv_weight, rope_width):
+    queries, width = q_nope.shape[0], own.shape[1]
+    heads, lat_width, value_width = uv_weight.shape
+    tile = 128
+    whole = lambda shape: pl.BlockSpec(shape, lambda i, s: (0,) * len(shape))
+    return pl.pallas_call(
+        functools.partial(attend_kernel, heads=heads, rope_width=rope_width),
+        grid_spec=pltpu.PrefetchScalarGridSpec(
+            num_scalar_prefetch=1,
+            grid=(queries // tile,),
+            in_specs=[
+                pl.BlockSpec((tile, heads * lat_width), lambda i, s: (i, 0)),
+                pl.BlockSpec((tile, heads * rope_width), lambda i, s: (i, 0)),
+                whole(own.shape),
+                whole(own.shape),
+                whole(own.shape),
+                whole(uv_weight.shape),
+            ],
+            out_specs=pl.BlockSpec((tile, heads * value_width), lambda i, s: (i, 0)),
+        ),
+        out_shape=jax.ShapeDtypeStruct((queries, heads * value_width), jnp.bfloat16),
+        compiler_params=pltpu.CompilerParams(vmem_limit_bytes=40 * 1024 * 1024),
+        cost_estimate=pl.CostEstimate(
+            flops=6 * heads * queries * own.shape[0] * (width + lat_width),
+            bytes_accessed=2 * (q_nope.size + 3 * own.size + uv_weight.size),
+            transcendentals=3 * heads * queries * own.shape[0],
+        ),
+        name="attend",
+    )(ctx_here.reshape(1), q_nope, q_rope, own, near, far, uv_weight)
+
+
+def project_kernel(order, values, weight, *outs):
+    rows = outs[0].shape[0]
+    picked = jnp.concatenate(
+        [values[pl.ds(pl.multiple_of(order[at] * rows, rows), rows), :] for at in range(len(outs))], axis=0
+    )
+    result = jnp.dot(picked, weight[...], preferred_element_type=jnp.float32).astype(outs[0].dtype)
+    for at, out in enumerate(outs):
+        out[...] = result[at * rows : (at + 1) * rows]
+
+
+def project_blocks(order, values, weight, count):
+    rows, inner = values.shape
+    width = weight.shape[1]
+    block, tile = rows // count, 896
+    return pl.pallas_call(
+        project_kernel,
+        grid_spec=pltpu.PrefetchScalarGridSpec(
+            num_scalar_prefetch=1,
+            grid=(width // tile,),
+            in_specs=[
+                pl.BlockSpec((rows, inner), lambda n, s: (0, 0)),
+                pl.BlockSpec((inner, tile), lambda n, s: (0, n)),
+            ],
+            out_specs=[pl.BlockSpec((block, tile), lambda n, s: (0, n))] * count,
+        ),
+        out_shape=[jax.ShapeDtypeStruct((block, width), jnp.bfloat16)] * count,
+        compiler_params=pltpu.CompilerParams(vmem_limit_bytes=32 * 1024 * 1024),
+        cost_estimate=pl.CostEstimate(
+            flops=2 * rows * inner * width, bytes_accessed=2 * (inner + rows) * width, transcendentals=0
+        ),
+        name="project",
+    )(order, values, weight)
+
+
+def hidden_kernel(here, *refs, blocks, counts, experts):
+    rows = refs[:blocks]
+    pieces = refs[blocks : blocks + sum(counts)]
+    hidden, energy_bins, scale, row_data, held, sems = refs[blocks + sum(counts) :]
+    copies, at = [], 0
+    for part, count in enumerate(counts):
+        mine, first = [], 0
+        for piece in pieces[at : at + count]:
+            mine.append(
+                pltpu.make_async_copy(piece, held.at[part, pl.ds(first, piece.shape[0])], sems.at[at + len(mine)])
+            )
+            mine[-1].start()
+            first += piece.shape[0]
+        at += count
+        copies.append(mine)
+    inner, units, each = held.shape[1], held.shape[2] // 2, rows[0].shape[0]
+    for at, row in enumerate(rows):
+        row_data[at * each : (at + 1) * each, :] = row[:, :inner]
+    table = jnp.concatenate([row[:, inner:] for row in rows], axis=0).astype(jnp.float32)
+    lane = lax.broadcasted_iota(jnp.int32, table.shape, 1)
+
+    def column(first):
+        return jnp.sum(jnp.where(lane == first + here[0], table, 0.0), axis=1, keepdims=True)
+
+    levels = jnp.sum(jnp.where(lane < experts, table, 0.0), axis=1, keepdims=True)
+    scale[...] = column(0) / levels
+    squares = 0.0
+    for part, mine in enumerate(copies):
+        for copy in mine:
+            copy.wait()
+        both = jnp.dot(row_data[...], held[part], preferred_element_type=jnp.float32)
+        gate_part, up_part = both[:, :units], both[:, units:]
+        activation = gate_part / (1.0 + jnp.exp(-gate_part)) * up_part
+        hidden[:, part * units : (part + 1) * units] = activation.astype(hidden.dtype)
+        squares = squares + jnp.sum(activation * activation, axis=1, keepdims=True)
+    place = lane.astype(jnp.float32)
+    high = jnp.where(place == column(experts), squares * (1.0 / HID), 0.0)
+    low = jnp.where(place == column(2 * experts), 1.0, 0.0)
+    counted = jnp.dot(high.T, low, precision=lax.Precision.HIGHEST, preferred_element_type=jnp.float32)
+    energy_bins[...] = counted[: energy_bins.shape[0], :]
+
+
+def hidden_rows(rows, weights, experts):
+    blocks, parts = len(rows), len(weights)
+    both = weights[0][0].shape[1]
+    inner = sum(piece.shape[0] for piece in weights[0])
+    count = blocks * rows[0].shape[0]
+    counts = tuple(len(pieces) for pieces in weights)
+    whole = pl.BlockSpec(memory_space=pltpu.VMEM)
+    return pl.pallas_call(
+        functools.partial(hidden_kernel, blocks=blocks, counts=counts, experts=experts),
+        in_specs=[pl.BlockSpec(memory_space=pltpu.SMEM)]
+        + [whole] * blocks
+        + [pl.BlockSpec(memory_space=pl.ANY)] * sum(counts),
+        out_specs=[whole] * 3,
+        out_shape=[
+            jax.ShapeDtypeStruct((count, parts * both // 2), jnp.bfloat16),
+            jax.ShapeDtypeStruct((NBINS // 128, 128), jnp.float32),
+            jax.ShapeDtypeStruct((count, 1), jnp.float32),
+        ],
+        scratch_shapes=[
+            pltpu.VMEM((count, inner), jnp.bfloat16),
+            pltpu.VMEM((parts, inner, both), jnp.bfloat16),
+            pltpu.SemaphoreType.DMA((sum(counts),)),
+        ],
+        compiler_params=pltpu.CompilerParams(vmem_limit_bytes=VMEM_BYTES),
+        cost_estimate=pl.CostEstimate(
+            flops=2 * count * inner * parts * both,
+            bytes_accessed=2 * inner * (count + parts * both),
+            transcendentals=count * parts * both // 2,
+        ),
+        name="hidden",
+    )(lax.axis_index("exp").astype(jnp.int32).reshape(1), *rows, *[piece for pieces in weights for piece in pieces])
+
+
+def down_kernel(hidden, scale, *refs, parts, tile):
+    weights = refs[:parts]
+    outs, held, sems = refs[parts:-2], refs[-2], refs[-1]
+    rows, units = outs[0].shape[0], weights[0].shape[0]
+    tiles = outs[0].shape[1] // tile
+    copies = [
+        [
+            pltpu.make_async_copy(
+                weight.at[:, pl.ds(at * tile, tile)],
+                held.at[at, pl.ds(part * units, units)],
+                sems.at[at * parts + part],
+            )
+            for part, weight in enumerate(weights)
+        ]
+        for at in range(tiles)
+    ]
+    for group in copies:
+        for copy in group:
+            copy.start()
+    for at, group in enumerate(copies):
+        for copy in group:
+            copy.wait()
+        total = jnp.dot(hidden[...], held[at], preferred_element_type=jnp.float32)
+        total = (total * scale[...]).astype(outs[0].dtype)
+        for block, out in enumerate(outs):
+            out[:, at * tile : (at + 1) * tile] = total[block * rows : (block + 1) * rows]
+
+
+def down_blocks(hidden, weights, scale, count):
+    parts, tile = len(weights), 896
+    rows, inner = hidden.shape
+    units, width = weights[0].shape
+    whole = pl.BlockSpec(memory_space=pltpu.VMEM)
+    return pl.pallas_call(
+        functools.partial(down_kernel, parts=parts, tile=tile),
+        in_specs=[whole] * 2 + [pl.BlockSpec(memory_space=pl.ANY)] * parts,
+        out_specs=[whole] * count,
+        out_shape=[jax.ShapeDtypeStruct((rows // count, width), jnp.bfloat16)] * count,
+        scratch_shapes=[
+            pltpu.VMEM((width // tile, inner, tile), jnp.bfloat16),
+            pltpu.SemaphoreType.DMA((width // tile * parts,)),
+        ],
+        compiler_params=pltpu.CompilerParams(vmem_limit_bytes=VMEM_BYTES),
+        cost_estimate=pl.CostEstimate(
+            flops=2 * rows * inner * width, bytes_accessed=2 * width * (inner + rows), transcendentals=0
+        ),
+        name="down",
+    )(hidden, scale, *weights)
+
+
+def spread_bins(counts):
+    counts = counts.reshape(2, 2, NBINS // 4)
+    ctx_here = lax.axis_index("ctx")
+    for at, bit in ((ctx_here // 2, 2), (ctx_here % 2, 1)):
+        counts = lax.dynamic_index_in_dim(counts, at, 0, keepdims=False) + swap_ctx(
+            lax.dynamic_index_in_dim(counts, 1 - at, 0, keepdims=False), bit
+        )
+    return counts[None, :]
+
+
+def dense_device(
+    residual_in,
+    norm_gain,
+    q_nope,
+    q_rope,
+    latent,
+    k_rope,
+    doc_ids,
+    uv_weight,
+    out_weight,
+    expert_ids,
+    gate_levels,
+    bin_ids,
+    gate_weight,
+    up_weight,
+    down_weight,
+):
+    exp_devices, ctx_devices = lax.axis_size("exp"), lax.axis_size("ctx")
+    ctx_here, exp_here = lax.axis_index("ctx"), lax.axis_index("exp")
+    token_count = residual_in.shape[0]
+    block_len, head_count, lat_width = q_nope.shape
+    rope_width = k_rope.shape[1]
+    order = relative_order(exp_devices)
+
+    spare = 128 - rope_width - 1
+    own = jnp.concatenate(
+        [latent, k_rope, doc_ids.astype(jnp.bfloat16)[:, None], jnp.zeros((block_len, spare), jnp.bfloat16)], axis=1
+    )
+    half = block_len // 2
+    sent = lax.dynamic_slice_in_dim(own, (exp_here % 2) * half, half, 0)
+    far_half = lax.ppermute(sent, "ctx", [(c, c + 2) for c in range(ctx_devices - 2)])
+    far = jnp.concatenate([far_half, swap_exp(far_half)], axis=0)
+    near = lax.ppermute(own, "ctx", [(c, c + 1) for c in range(0, ctx_devices, 2)])
+    near = near + lax.ppermute(far, "ctx", [(3, 2)])
+
+    w_down = down_weight[0]
+    near_both = jnp.concatenate([gate_weight[0], up_weight[0]], axis=1)
+
+    def from_far(first, end, earlier):
+        return swap_ctx(after(lax.slice_in_dim(near_both, first, end, axis=0), earlier), 2)
+
+    part_a, part_b = FIRST_ROWS
+    both_a = from_far(0, part_a, far_half)
+    own = after(own, both_a)
+    both_b = from_far(part_a, part_b, own)
+    values = attend(
+        ctx_here, q_nope.reshape(block_len, head_count * lat_width), q_rope, own, near, far, uv_weight, rope_width
+    )
+    values = after(values, both_b)
+    both_c = from_far(part_b, near_both.shape[0], values)
+    partial = project_blocks(order, values, out_weight, exp_devices)
+    attended = one_step(reduce_exp, *partial)
+    attended = after(attended, both_c)
+    far_down = swap_ctx(after(w_down, attended), 2)
+    stream_state = residual_in.astype(jnp.float32) + attended
+    normed = (
+        stream_state
+        * lax.rsqrt(jnp.mean(stream_state * stream_state, axis=1, keepdims=True) + norm_eps)
+        * norm_gain
+    ).astype(jnp.bfloat16)
+
+    named = expert_ids[:, :, None] == jnp.arange(exp_devices, dtype=jnp.int32)[None, None, :]
+    table = jnp.concatenate(
+        [
+            jnp.sum(jnp.where(named, what[:, :, None], 0), axis=1)
+            for what in (gate_levels, bin_ids // 128, bin_ids % 128)
+        ]
+        + [jnp.zeros((token_count, 128 - 3 * exp_devices), jnp.int32)],
+        axis=1,
+    ).astype(jnp.bfloat16)
+    block = jnp.concatenate([normed, table], axis=1)
+    found = [block] + after(one_step(gather_exp, block), far_down)
+    far_both = [both_a, both_b, both_c]
+    weights = [[near_both], [swap_ctx(near_both, 1)], far_both, [swap_ctx(piece, 1) for piece in far_both]]
+    downs = [w_down, swap_ctx(w_down, 1), far_down, swap_ctx(far_down, 1)]
+    hidden, bins, row_scale = hidden_rows(found, weights, exp_devices)
+    mixture = reduce_exp(*down_blocks(hidden, downs, row_scale, exp_devices))
+    layer_out = (stream_state + mixture).astype(jnp.bfloat16)
+    histogram = spread_bins(bins)
+    return (layer_out, histogram)
+
+
 def solution(mesh):
+    sizes = mesh.shape
+
+    def on_device(*arrays):
+        named_experts = arrays[9].shape[1]
+        dense = sizes["exp"] == 8 and sizes["ctx"] == 4 and named_experts == sizes["exp"]
+        return (dense_device if dense else routed_device)(*arrays)
+
     return jax.shard_map(
         on_device,
         mesh=mesh,

time: 677 us -> 251 us (0.37); the launches traced: 668 us -> 251 us
  waiting for transfers between devices: 392 us -> 156 us
  blocking collectives: 104 us -> 0 us
  matrix products: 73 us -> 0 us
  Pallas kernels: 0 us -> 36.7 us
  local copies, waits for them, and re-layouts: 32.4 us -> 5.36 us
  other arithmetic: 33 us -> 14.5 us
  starting transfers between devices: 20.5 us -> 37.4 us
  between operations: 14.2 us -> 1.07 us
    reduce_scatter x2 -> x0, waiting for transfers between devices: 228 us -> none  [the longest x1 130 us: on_device(): lax.psum_scatter(head_rows(jnp.int32(0), token_count * lax.axis_size('exp...]
    ppermute x0 -> x37, waiting for transfers between devices: none -> 156 us  [the longest x9 76.9 us: ring_z(): lax.ppermute(value, 'exp', [(e, (e + 2) % exp_devices) for e in range(exp...]
    all_gather x2 -> x0, waiting for transfers between devices: 105 us -> none  [the longest x1 93.2 us: on_device(): lax.all_gather(incoming, 'ctx', axis=1, tiled=True)]
    all_to_all x1 -> x0, blocking collectives: 85.7 us -> none  [on_device(): lax.all_to_all(outgoing, 'exp', split_axis=0, concat_axis=1, tiled=True)]
    dot_general x9 -> x0, matrix products: 58.3 us -> none  [the longest x1 11.7 us: expert_hidden(): up_part = jnp.dot(row_data, w_up, preferred_element_type=jnp.float32)]
    ppermute x0 -> x37, starting transfers between devices: none -> 37.4 us  [the longest x13 17.9 us: swap_exp(): lax.ppermute(value, 'exp', [(e, e ^ bit) for e in range(lax.axis_size('ex...]
    pallas_call x0 -> x4, Pallas kernels: none -> 36.7 us  [the longest x1 13.8 us: hidden_rows(): pl.pallas_call(functools.partial(hidden_kernel, blocks=blocks, counts=cou...]
    all_to_all x2 -> x0, waiting for transfers between devices: 33.7 us -> none  [the longest x1 33.7 us: on_device(): lax.all_to_all(expert_out[None], 'exp', split_axis=1, concat_axis=0, tile...]
  transfers between devices with their start and end apart: 7 -> 37, of which waited for: 6 -> 25; matrix products, arithmetic and copies ran while one was open for 10% -> 5% of each run, Pallas kernels for 0% -> 11%
where the time goes in v2:
time: 251 us
  waiting for transfers between devices  156 us (62%)
  starting transfers between devices  37.4 us (15%)
  Pallas kernels  36.7 us (15%)
  other arithmetic  14.5 us (6%)
  local copies, waits for them, and re-layouts  5.36 us (2%)
    ppermute x9, waiting for transfers between devices, ring_z(): lax.ppermute(value, 'exp', [(e, (e + 2) % exp_devices) for e in range(exp...  76.9 us
    ppermute x13, waiting for transfers between devices, swap_exp(): lax.ppermute(value, 'exp', [(e, e ^ bit) for e in range(lax.axis_size('ex...  56.1 us
    ppermute x13, starting transfers between devices, swap_exp(): lax.ppermute(value, 'exp', [(e, e ^ bit) for e in range(lax.axis_size('ex...  17.9 us
    ppermute x12, waiting for transfers between devices, swap_ctx(): lax.ppermute(value, 'ctx', [(c, c ^ bit) for c in range(lax.axis_size('ct...  15.9 us
    pallas_call x1, Pallas kernels, hidden_rows(): pl.pallas_call(functools.partial(hidden_kernel, blocks=blocks, counts=cou...  13.8 us
    pallas_call x1, Pallas kernels, attend(): pl.pallas_call(functools.partial(attend_kernel, heads=heads, rope_width=r...  10.4 us
    pallas_call x1, Pallas kernels, down_blocks(): pl.pallas_call(functools.partial(down_kernel, parts=parts, tile=tile), in...  9.6 us
    ppermute x12, starting transfers between devices, swap_ctx(): lax.ppermute(value, 'ctx', [(c, c ^ bit) for c in range(lax.axis_size('ct...  8.98 us
  transfers between devices with their start and end apart: 37, of which 25 were waited for; matrix products, arithmetic and copies ran while one was open for 5% of the time, Pallas kernels for 11%

profile of v2, /device:TPU:0, one launch (start us, length us, event | category | flops | bytes accessed | tf_op | source)
XLA Modules:
  0.0 251.0 jit_solution(8221329208275495851)
XLA Ops:
  3.9 4.9 %collective-permute-start.14 = (bf16[256,640]{1,0:T(8,128)(2,1)S(1)}, bf16[256,640]{1,0:T(8,128)(2,1)S(1)}, u32[]{:S(2)}, u32[]{:S(2)}) collective-permute-start(bf16[256,640]{1,0:T(8,128)(2,1)S(1)} %constant_dynamic-slice_fusion.2), channel_id=1, source_target_pairs={{0,16},{8,24},{1,17},{9,25},{2,18},{10,26},{3,19},{11,27},{4,20},{... | collective-permute-start | bytes 983048 | tf_op jit(solution)/shard_map/ppermute | solution.py:524
  8.8 6.9 %collective-permute-done.14 = bf16[256,640]{1,0:T(8,128)(2,1)S(1)} collective-permute-done((bf16[256,640]{1,0:T(8,128)(2,1)S(1)}, bf16[256,640]{1,0:T(8,128)(2,1)S(1)}, u32[]{:S(2)}, u32[]{:S(2)}) %collective-permute-start.14) | collective-permute-done | bytes 327712 | tf_op jit(solution)/shard_map/ppermute | solution.py:524
  27.0 3.3 %collective-permute-done.15.refs_10_ = bf16[448,512]{1,0:T(8,128)(2,1)S(1)} collective-permute-done((bf16[448,512]{1,0:T(8,128)(2,1)S(1)}, bf16[448,512]{1,0:T(8,128)(2,1)S(1)}, u32[]{:S(2)}, u32[]{:S(2)}) %collective-permute-start.15) | collective-permute-done | bytes 458784 | tf_op jit(solution)/shard_map/ppermute | solution.py:207
  37.7 10.4 %attend.1.values = bf16[512,256]{1,0:T(8,128)(2,1)S(1)} custom-call(s32[1]{0:T(128)} %bitcast.8.scalars, bf16[512,1024]{1,0:T(8,128)(2,1)S(1)} %bitcast.22, bf16[512,128]{1,0:T(8,128)(2,1)S(1)} %copy-done.2, bf16[512,640]{1,0:T(8,128)(2,1)S(1)} %maximum_maximum_fusion.own, bf16[512,640]{1,0:T(8,128)(2,1)S(1)} %add.188.near, ...), custom_call_target="tpu_custom_call" | custom-call | flops 3623878656 | bytes 3276800 | tf_op jit(solution)/shard_map/attend/pallas_call | solution.py:299
  58.2 52.6 %conditional.2 = (f32[64,3584]{1,0:T(8,128)S(1)}) conditional(s32[]{:T(128)} %convert_element_type.102, () %tuple.32, (bf16[64,3584]{1,0:T(8,128)(2,1)S(1)}, bf16[64,3584]{1,0:T(8,128)(2,1)S(1)}, bf16[64,3584]{1,0:T(8,128)(2,1)S(1)}, bf16[64,3584]{1,0:T(8,128)(2,1)S(1)}, bf16[64,3584]{1,0:T(8,128)(2,1)S(1)}, ...), branch_computations={%region_0.1_spmd, %region_1.2_spmd} | conditional | flops 4816896 | bytes 20185376 | solution.py:220
  60.3 11.3 %collective-permute-done.10 = bf16[64,3584]{1,0:T(8,128)(2,1)S(1)} collective-permute-done((bf16[64,3584]{1,0:T(8,128)(2,1)S(1)}, bf16[64,3584]{1,0:T(8,128)(2,1)S(1)}, u32[]{:S(2)}, u32[]{:S(2)}) %collective-permute-start.10) | collective-permute-done | bytes 458784 | tf_op jit(solution)/shard_map/cond/branch_1_fun/ppermute | solution.py:198
  74.8 6.6 %collective-permute-done.9 = bf16[64,3584]{1,0:T(8,128)(2,1)S(1)} collective-permute-done((bf16[64,3584]{1,0:T(8,128)(2,1)S(1)}, bf16[64,3584]{1,0:T(8,128)(2,1)S(1)}, u32[]{:S(2)}, u32[]{:S(2)}) %collective-permute-start.9) | collective-permute-done | bytes 458784 | tf_op jit(solution)/shard_map/cond/branch_1_fun/ppermute | solution.py:198
  81.4 4.1 %collective-permute-done.11 = bf16[64,3584]{1,0:T(8,128)(2,1)S(1)} collective-permute-done((bf16[64,3584]{1,0:T(8,128)(2,1)S(1)}, bf16[64,3584]{1,0:T(8,128)(2,1)S(1)}, u32[]{:S(2)}, u32[]{:S(2)}) %collective-permute-start.11) | collective-permute-done | bytes 458784 | tf_op jit(solution)/shard_map/cond/branch_1_fun/ppermute | solution.py:203
  87.3 4.0 %collective-permute-done.8 = bf16[64,3584]{1,0:T(8,128)(2,1)S(1)} collective-permute-done((bf16[64,3584]{1,0:T(8,128)(2,1)S(1)}, bf16[64,3584]{1,0:T(8,128)(2,1)S(1)}, u32[]{:S(2)}, u32[]{:S(2)}) %collective-permute-start.8) | collective-permute-done | bytes 458784 | tf_op jit(solution)/shard_map/cond/branch_1_fun/ppermute | solution.py:198
  91.3 7.3 %collective-permute-done.12 = bf16[64,3584]{1,0:T(8,128)(2,1)S(1)} collective-permute-done((bf16[64,3584]{1,0:T(8,128)(2,1)S(1)}, bf16[64,3584]{1,0:T(8,128)(2,1)S(1)}, u32[]{:S(2)}, u32[]{:S(2)}) %collective-permute-start.12) | collective-permute-done | bytes 458784 | tf_op jit(solution)/shard_map/cond/branch_1_fun/ppermute | solution.py:203
  100.7 9.9 %collective-permute-done.13 = bf16[64,3584]{1,0:T(8,128)(2,1)S(1)} collective-permute-done((bf16[64,3584]{1,0:T(8,128)(2,1)S(1)}, bf16[64,3584]{1,0:T(8,128)(2,1)S(1)}, u32[]{:S(2)}, u32[]{:S(2)}) %collective-permute-start.13) | collective-permute-done | bytes 458784 | tf_op jit(solution)/shard_map/cond/branch_1_fun/ppermute | solution.py:203
  112.2 54.5 %conditional.3 = (bf16[64,3712]{1,0:T(8,128)(2,1)}, bf16[64,3712]{1,0:T(8,128)(2,1)}, bf16[64,3712]{1,0:T(8,128)(2,1)}, bf16[64,3712]{1,0:T(8,128)(2,1)}, bf16[6...) conditional(s32[]{:T(128)} %convert_element_type.102, () %tuple.40, ...), branch_computations={%region_6.7_spmd, %region_7.8_spmd} | conditional | bytes 13304144 | solution.py:220
  113.8 13.6 %collective-permute-done.1 = bf16[64,3712]{1,0:T(8,128)(2,1)} collective-permute-done((bf16[64,3712]{1,0:T(8,128)(2,1)S(1)}, bf16[64,3712]{1,0:T(8,128)(2,1)}, u32[]{:S(2)}, u32[]{:S(2)}) %collective-permute-start.1) | collective-permute-done | bytes 475168 | tf_op jit(solution)/shard_map/cond/branch_1_fun/ppermute | solution.py:203
  128.9 13.1 %collective-permute-done.3 = bf16[64,3712]{1,0:T(8,128)(2,1)} collective-permute-done((bf16[64,3712]{1,0:T(8,128)(2,1)}, bf16[64,3712]{1,0:T(8,128)(2,1)}, u32[]{:S(2)}, u32[]{:S(2)}) %collective-permute-start.3) | collective-permute-done | bytes 475168 | tf_op jit(solution)/shard_map/cond/branch_1_fun/ppermute | solution.py:203
  143.5 12.2 %collective-permute-done.5 = bf16[64,3712]{1,0:T(8,128)(2,1)} collective-permute-done((bf16[64,3712]{1,0:T(8,128)(2,1)}, bf16[64,3712]{1,0:T(8,128)(2,1)}, u32[]{:S(2)}, u32[]{:S(2)}) %collective-permute-start.5) | collective-permute-done | bytes 475168 | tf_op jit(solution)/shard_map/cond/branch_1_fun/ppermute | solution.py:203
  157.2 9.5 %collective-permute-done.6 = bf16[64,3712]{1,0:T(8,128)(2,1)} collective-permute-done((bf16[64,3712]{1,0:T(8,128)(2,1)}, bf16[64,3712]{1,0:T(8,128)(2,1)}, u32[]{:S(2)}, u32[]{:S(2)}) %collective-permute-start.6) | collective-permute-done | bytes 475168 | tf_op jit(solution)/shard_map/cond/branch_1_fun/ppermute | solution.py:198
  169.3 4.5 %collective-permute-done.24.refs_14_ = bf16[832,512]{1,0:T(8,128)(2,1)S(1)} collective-permute-done((bf16[832,512]{1,0:T(8,128)(2,1)}, bf16[832,512]{1,0:T(8,128)(2,1)S(1)}, u32[]{:S(2)}, u32[]{:S(2)}) %collective-permute-start.24) | collective-permute-done | bytes 852000 | tf_op jit(solution)/shard_map/ppermute | solution.py:207
  174.7 13.8 %hidden.1 = (bf16[512,1024]{1,0:T(8,128)(2,1)}, f32[16,128]{1,0:T(8,128)}, f32[512,1]{1,0:T(8,128)}) custom-call(s32[1]{0:T(128)} %bitcast.11.here, bf16[64,3712]{1,0:T(8,128)(2,1)S(1)} %concatenate.21.refs_0_, bf16[64,3712]{1,0:T(8,128)(2,1)} %get-tuple-element.94.refs_1_, bf16[64,3712]{1,0:T(8,128)(2,1)} %get-tuple-element.95.refs_2_, ...), custom_call_target="tpu_custom_call" | custom-call | flops 7516192768 | bytes 18350080 | tf_op jit(solution)/shard_map/hidden/pallas_call | solution.py:408
  188.6 9.6 %down.1 = (bf16[64,3584]{1,0:T(8,128)(2,1)}, bf16[64,3584]{1,0:T(8,128)(2,1)}, bf16[64,3584]{1,0:T(8,128)(2,1)}, bf16[64,3584]{1,0:T(8,128)(2,1)}, bf16[64,3584]...) custom-call(bf16[512,1024]{1,0:T(8,128)(2,1)} %get-tuple-element.101.hidden, ...), custom_call_target="tpu_custom_call" | custom-call | flops 3758096384 | bytes 11010048 | tf_op jit(solution)/shard_map/down/pallas_call | solution.py:467
  200.3 11.5 %collective-permute-done.31 = bf16[64,3584]{1,0:T(8,128)(2,1)S(1)} collective-permute-done((bf16[64,3584]{1,0:T(8,128)(2,1)}, bf16[64,3584]{1,0:T(8,128)(2,1)S(1)}, u32[]{:S(2)}, u32[]{:S(2)}) %collective-permute-start.31) | collective-permute-done | bytes 458784 | tf_op jit(solution)/shard_map/ppermute | solution.py:198
  214.6 7.1 %collective-permute-done.30 = bf16[64,3584]{1,0:T(8,128)(2,1)S(1)} collective-permute-done((bf16[64,3584]{1,0:T(8,128)(2,1)}, bf16[64,3584]{1,0:T(8,128)(2,1)S(1)}, u32[]{:S(2)}, u32[]{:S(2)}) %collective-permute-start.30) | collective-permute-done | bytes 458784 | tf_op jit(solution)/shard_map/ppermute | solution.py:198
  221.7 4.1 %collective-permute-done.32 = bf16[64,3584]{1,0:T(8,128)(2,1)S(1)} collective-permute-done((bf16[64,3584]{1,0:T(8,128)(2,1)S(1)}, bf16[64,3584]{1,0:T(8,128)(2,1)S(1)}, u32[]{:S(2)}, u32[]{:S(2)}) %collective-permute-start.32) | collective-permute-done | bytes 458784 | tf_op jit(solution)/shard_map/ppermute | solution.py:203
  231.5 7.4 %collective-permute-done.33 = bf16[64,3584]{1,0:T(8,128)(2,1)S(1)} collective-permute-done((bf16[64,3584]{1,0:T(8,128)(2,1)S(1)}, bf16[64,3584]{1,0:T(8,128)(2,1)S(1)}, u32[]{:S(2)}, u32[]{:S(2)}) %collective-permute-start.33) | collective-permute-done | bytes 458784 | tf_op jit(solution)/shard_map/ppermute | solution.py:203
  244.6 5.3 %collective-permute-done.34 = bf16[64,3584]{1,0:T(8,128)(2,1)S(1)} collective-permute-done((bf16[64,3584]{1,0:T(8,128)(2,1)S(1)}, bf16[64,3584]{1,0:T(8,128)(2,1)S(1)}, u32[]{:S(2)}, u32[]{:S(2)}) %collective-permute-start.34) | collective-permute-done | bytes 458784 | tf_op jit(solution)/shard_map/ppermute | solution.py:203
  (136 shorter events, 69.4 us)
Async XLA Ops:
  20.9 15.3 %collective-permute-start.16 = (bf16[512,640]{1,0:T(8,128)(2,1)S(1)}, bf16[512,640]{1,0:T(8,128)(2,1)}, u32[]{:S(2)}, u32[]{:S(2)}) collective-permute-start(bf16[512,640]{1,0:T(8,128)(2,1)S(1)} %maximum_maximum_fusion.own), channel_id=1, source_target_pairs={{0,8},{16,24},{1,9},{17,25},{2,10},{18,26},{3,11},{19,27},{4,12},{... | collective-permute-start | bytes 1966088 | tf_op jit(solution)/shard_map/ppermute | solution.py:526
  31.1 20.3 %collective-permute-start.19 = (bf16[832,512]{1,0:T(8,128)(2,1)}, bf16[832,512]{1,0:T(8,128)(2,1)}, u32[]{:S(2)}, u32[]{:S(2)}) collective-permute-start(bf16[832,512]{1,0:T(8,128)(2,1)} %fusion.1), channel_id=1, source_target_pairs={{0,16},{8,24},{16,0},{24,8},{1,17},{9,25},{17,1},{25,9},{2,18},{10... | collective-permute-start | bytes 2555912 | tf_op jit(solution)/shard_map/ppermute | solution.py:207
  51.4 59.4 %collective-permute-start.20 = (bf16[2304,512]{1,0:T(8,128)(2,1)}, bf16[2304,512]{1,0:T(8,128)(2,1)}, u32[]{:S(2)}, u32[]{:S(2)}) collective-permute-start(bf16[2304,512]{1,0:T(8,128)(2,1)} %fusion), channel_id=1, source_target_pairs={{0,16},{8,24},{16,0},{24,8},{1,17},{9,25},{17,1},{25,9},{2,18},{10... | collective-permute-start | bytes 7077896 | tf_op jit(solution)/shard_map/ppermute | solution.py:207
  55.2 118.6 %collective-permute-start.22 = (bf16[3584,512]{1,0:T(8,128)(2,1)}, bf16[3584,512]{1,0:T(8,128)(2,1)}, u32[]{:S(2)}, u32[]{:S(2)}) collective-permute-start(bf16[3584,512]{1,0:T(8,128)(2,1)} %pad_maximum_fusion.refs_8_), channel_id=1, source_target_pairs={{0,8},{8,0},{16,24},{24,16},{1,9},{9,1},{17,25},{25,17},{2,10},{10... | collective-permute-start | bytes 11010056 | tf_op jit(solution)/shard_map/ppermute | solution.py:207
  58.2 13.4 %collective-permute-start.10 = (bf16[64,3584]{1,0:T(8,128)(2,1)S(1)}, bf16[64,3584]{1,0:T(8,128)(2,1)S(1)}, u32[]{:S(2)}, u32[]{:S(2)}) collective-permute-start(bf16[64,3584]{1,0:T(8,128)(2,1)S(1)} %get-tuple-element.27), channel_id=1, source_target_pairs={{0,1},{1,0},{2,3},{3,2},{4,5},{5,4},{6,7},{7,6},{8,9},{9,8},{10,11... | collective-permute-start | bytes 1376264 | tf_op jit(solution)/shard_map/cond/branch_1_fun/ppermute | solution.py:198
  59.8 21.7 %collective-permute-start.9 = (bf16[64,3584]{1,0:T(8,128)(2,1)S(1)}, bf16[64,3584]{1,0:T(8,128)(2,1)S(1)}, u32[]{:S(2)}, u32[]{:S(2)}) collective-permute-start(bf16[64,3584]{1,0:T(8,128)(2,1)S(1)} %get-tuple-element.25), channel_id=1, source_target_pairs={{0,1},{1,0},{2,3},{3,2},{4,5},{5,4},{6,7},{7,6},{8,9},{9,8},{10,11... | collective-permute-start | bytes 1376264 | tf_op jit(solution)/shard_map/cond/branch_1_fun/ppermute | solution.py:198
  71.7 13.8 %collective-permute-start.11 = (bf16[64,3584]{1,0:T(8,128)(2,1)S(1)}, bf16[64,3584]{1,0:T(8,128)(2,1)S(1)}, u32[]{:S(2)}, u32[]{:S(2)}) collective-permute-start(bf16[64,3584]{1,0:T(8,128)(2,1)S(1)} %add_convert_fusion.2), channel_id=1, source_target_pairs={{0,2},{1,3},{2,4},{3,5},{4,6},{5,7},{6,0},{7,1},{8,10},{9,11},{10,... | collective-permute-start | bytes 1376264 | tf_op jit(solution)/shard_map/cond/branch_1_fun/ppermute | solution.py:203
  73.3 17.9 %collective-permute-start.8 = (bf16[64,3584]{1,0:T(8,128)(2,1)S(1)}, bf16[64,3584]{1,0:T(8,128)(2,1)S(1)}, u32[]{:S(2)}, u32[]{:S(2)}) collective-permute-start(bf16[64,3584]{1,0:T(8,128)(2,1)S(1)} %get-tuple-element.23), channel_id=1, source_target_pairs={{0,1},{1,0},{2,3},{3,2},{4,5},{5,4},{6,7},{7,6},{8,9},{9,8},{10,11... | collective-permute-start | bytes 1376264 | tf_op jit(solution)/shard_map/cond/branch_1_fun/ppermute | solution.py:198
  85.7 12.9 %collective-permute-start.12 = (bf16[64,3584]{1,0:T(8,128)(2,1)S(1)}, bf16[64,3584]{1,0:T(8,128)(2,1)S(1)}, u32[]{:S(2)}, u32[]{:S(2)}) collective-permute-start(bf16[64,3584]{1,0:T(8,128)(2,1)S(1)} %add_convert_fusion.1), channel_id=1, source_target_pairs={{0,2},{1,3},{2,4},{3,5},{4,6},{5,7},{6,0},{7,1},{8,10},{9,11},{10,... | collective-permute-start | bytes 1376264 | tf_op jit(solution)/shard_map/cond/branch_1_fun/ppermute | solution.py:203
  85.7 15.0 %collective-permute-start.7 = (bf16[64,3584]{1,0:T(8,128)(2,1)S(1)}, bf16[64,3584]{1,0:T(8,128)(2,1)S(1)}, u32[]{:S(2)}, u32[]{:S(2)}) collective-permute-start(bf16[64,3584]{1,0:T(8,128)(2,1)S(1)} %get-tuple-element.21), channel_id=1, source_target_pairs={{0,1},{1,0},{2,3},{3,2},{4,5},{5,4},{6,7},{7,6},{8,9},{9,8},{10,11... | collective-permute-start | bytes 1376264 | tf_op jit(solution)/shard_map/cond/branch_1_fun/ppermute | solution.py:198
  110.8 56.4 %collective-permute-start.21 = (bf16[256,3584]{1,0:T(8,128)(2,1)}, bf16[256,3584]{1,0:T(8,128)(2,1)}, u32[]{:S(2)}, u32[]{:S(2)}) collective-permute-start(bf16[256,3584]{1,0:T(8,128)(2,1)} %bitcast.35), channel_id=1, source_target_pairs={{0,16},{8,24},{16,0},{24,8},{1,17},{9,25},{17,1},{25,9},{2,18},{10... | collective-permute-start | bytes 5505032 | tf_op jit(solution)/shard_map/ppermute | solution.py:207
  111.5 62.3 %collective-permute-start.25 = (bf16[2304,512]{1,0:T(8,128)(2,1)}, bf16[2304,512]{1,0:T(8,128)(2,1)}, u32[]{:S(2)}, u32[]{:S(2)}) collective-permute-start(bf16[2304,512]{1,0:T(8,128)(2,1)} %collective-permute-done.20.refs_12_), channel_id=1, source_target_pairs={{0,8},{8,0},{16,24},{24,16},{1,9},{9,1},{17,25},{25,17},{2,10},{10... | collective-permute-start | bytes 7077896 | tf_op jit(solution)/shard_map/ppermute | solution.py:207
  112.2 15.2 %collective-permute-start.1 = (bf16[64,3712]{1,0:T(8,128)(2,1)S(1)}, bf16[64,3712]{1,0:T(8,128)(2,1)}, u32[]{:S(2)}, u32[]{:S(2)}) collective-permute-start(bf16[64,3712]{1,0:T(8,128)(2,1)S(1)} %param.3), channel_id=1, source_target_pairs={{0,2},{1,3},{2,4},{3,5},{4,6},{5,7},{6,0},{7,1},{8,10},{9,11},{10,... | collective-permute-start | bytes 1425416 | tf_op jit(solution)/shard_map/cond/branch_1_fun/ppermute | solution.py:203
  112.3 15.2 %collective-permute-start = (bf16[64,3712]{1,0:T(8,128)(2,1)S(1)}, bf16[64,3712]{1,0:T(8,128)(2,1)}, u32[]{:S(2)}, u32[]{:S(2)}) collective-permute-start(bf16[64,3712]{1,0:T(8,128)(2,1)S(1)} %param.3), channel_id=1, source_target_pairs={{0,1},{1,0},{2,3},{3,2},{4,5},{5,4},{6,7},{7,6},{8,9},{9,8},{10,11... | collective-permute-start | bytes 1425416 | tf_op jit(solution)/shard_map/cond/branch_1_fun/ppermute | solution.py:198
  127.4 14.6 %collective-permute-start.3 = (bf16[64,3712]{1,0:T(8,128)(2,1)}, bf16[64,3712]{1,0:T(8,128)(2,1)}, u32[]{:S(2)}, u32[]{:S(2)}) collective-permute-start(bf16[64,3712]{1,0:T(8,128)(2,1)} %collective-permute-done.1), channel_id=1, source_target_pairs={{0,2},{1,3},{2,4},{3,5},{4,6},{5,7},{6,0},{7,1},{8,10},{9,11},{10,... | collective-permute-start | bytes 1425416 | tf_op jit(solution)/shard_map/cond/branch_1_fun/ppermute | solution.py:203
  127.4 14.6 %collective-permute-start.2 = (bf16[64,3712]{1,0:T(8,128)(2,1)}, bf16[64,3712]{1,0:T(8,128)(2,1)}, u32[]{:S(2)}, u32[]{:S(2)}) collective-permute-start(bf16[64,3712]{1,0:T(8,128)(2,1)} %collective-permute-done.1), channel_id=1, source_target_pairs={{0,1},{1,0},{2,3},{3,2},{4,5},{5,4},{6,7},{7,6},{8,9},{9,8},{10,11... | collective-permute-start | bytes 1425416 | tf_op jit(solution)/shard_map/cond/branch_1_fun/ppermute | solution.py:198
  142.0 13.7 %collective-permute-start.5 = (bf16[64,3712]{1,0:T(8,128)(2,1)}, bf16[64,3712]{1,0:T(8,128)(2,1)}, u32[]{:S(2)}, u32[]{:S(2)}) collective-permute-start(bf16[64,3712]{1,0:T(8,128)(2,1)} %collective-permute-done.3), channel_id=1, source_target_pairs={{0,2},{1,3},{2,4},{3,5},{4,6},{5,7},{6,0},{7,1},{8,10},{9,11},{10,... | collective-permute-start | bytes 1425416 | tf_op jit(solution)/shard_map/cond/branch_1_fun/ppermute | solution.py:203
  142.0 15.2 %collective-permute-start.4 = (bf16[64,3712]{1,0:T(8,128)(2,1)}, bf16[64,3712]{1,0:T(8,128)(2,1)}, u32[]{:S(2)}, u32[]{:S(2)}) collective-permute-start(bf16[64,3712]{1,0:T(8,128)(2,1)} %collective-permute-done.3), channel_id=1, source_target_pairs={{0,1},{1,0},{2,3},{3,2},{4,5},{5,4},{6,7},{7,6},{8,9},{9,8},{10,11... | collective-permute-start | bytes 1425416 | tf_op jit(solution)/shard_map/cond/branch_1_fun/ppermute | solution.py:198
  166.7 21.8 %collective-permute-start.26 = (bf16[256,3584]{1,0:T(8,128)(2,1)}, bf16[256,3584]{1,0:T(8,128)(2,1)}, u32[]{:S(2)}, u32[]{:S(2)}) collective-permute-start(bf16[256,3584]{1,0:T(8,128)(2,1)} %bitcast.36), channel_id=1, source_target_pairs={{0,8},{8,0},{16,24},{24,16},{1,9},{9,1},{17,25},{25,17},{2,10},{10... | collective-permute-start | bytes 5505032 | tf_op jit(solution)/shard_map/ppermute | solution.py:207
  167.2 21.3 %collective-permute-start.27 = (bf16[256,3584]{1,0:T(8,128)(2,1)}, bf16[256,3584]{1,0:T(8,128)(2,1)}, u32[]{:S(2)}, u32[]{:S(2)}) collective-permute-start(bf16[256,3584]{1,0:T(8,128)(2,1)} %collective-permute-done.21.refs_2_), channel_id=1, source_target_pairs={{0,8},{8,0},{16,24},{24,16},{1,9},{9,1},{17,25},{25,17},{2,10},{10... | collective-permute-start | bytes 5505032 | tf_op jit(solution)/shard_map/ppermute | solution.py:207
  198.2 13.6 %collective-permute-start.31 = (bf16[64,3584]{1,0:T(8,128)(2,1)}, bf16[64,3584]{1,0:T(8,128)(2,1)S(1)}, u32[]{:S(2)}, u32[]{:S(2)}) collective-permute-start(bf16[64,3584]{1,0:T(8,128)(2,1)} %get-tuple-element.110), channel_id=1, source_target_pairs={{0,1},{1,0},{2,3},{3,2},{4,5},{5,4},{6,7},{7,6},{8,9},{9,8},{10,11... | collective-permute-start | bytes 1376264 | tf_op jit(solution)/shard_map/ppermute | solution.py:198
  199.7 21.9 %collective-permute-start.30 = (bf16[64,3584]{1,0:T(8,128)(2,1)}, bf16[64,3584]{1,0:T(8,128)(2,1)S(1)}, u32[]{:S(2)}, u32[]{:S(2)}) collective-permute-start(bf16[64,3584]{1,0:T(8,128)(2,1)} %get-tuple-element.108), channel_id=1, source_target_pairs={{0,1},{1,0},{2,3},{3,2},{4,5},{5,4},{6,7},{7,6},{8,9},{9,8},{10,11... | collective-permute-start | bytes 1376264 | tf_op jit(solution)/shard_map/ppermute | solution.py:198
  213.0 18.5 %collective-permute-start.29 = (bf16[64,3584]{1,0:T(8,128)(2,1)}, bf16[64,3584]{1,0:T(8,128)(2,1)S(1)}, u32[]{:S(2)}, u32[]{:S(2)}) collective-permute-start(bf16[64,3584]{1,0:T(8,128)(2,1)} %get-tuple-element.106), channel_id=1, source_target_pairs={{0,1},{1,0},{2,3},{3,2},{4,5},{5,4},{6,7},{7,6},{8,9},{9,8},{10,11... | collective-permute-start | bytes 1376264 | tf_op jit(solution)/shard_map/ppermute | solution.py:198
  227.0 17.6 %collective-permute-start.28 = (bf16[64,3584]{1,0:T(8,128)(2,1)}, bf16[64,3584]{1,0:T(8,128)(2,1)S(1)}, u32[]{:S(2)}, u32[]{:S(2)}) collective-permute-start(bf16[64,3584]{1,0:T(8,128)(2,1)} %get-tuple-element.104), channel_id=1, source_target_pairs={{0,1},{1,0},{2,3},{3,2},{4,5},{5,4},{6,7},{7,6},{8,9},{9,8},{10,11... | collective-permute-start | bytes 1376264 | tf_op jit(solution)/shard_map/ppermute | solution.py:198
  (32 other events, 572.6 us)

commit v3 on v0

--- a/solution.py
+++ b/solution.py
@@ -1,6 +1,11 @@
+import functools
+import math
+
 import jax
 import jax.numpy as jnp
 from jax import lax
+from jax.experimental import pallas as pl
+from jax.experimental.pallas import tpu as pltpu
 from jax.sharding import PartitionSpec as P
 
 HID = 1024
@@ -10,6 +15,9 @@
 softmax_scale = 192.0 ** (-0.5)
 norm_eps = 1e-06
 masked_score = -1e30
+LOG2_E = math.log2(math.e)
+FIRST_ROWS = (256, 896)
+VMEM_BYTES = 14 * 1024 * 1024
 
 
 def route_slots(expert_ids, experts, capacity):
@@ -74,7 +82,7 @@
     return jnp.dot(energy[None, :], onehot, precision=lax.Precision.HIGHEST)[0]
 
 
-def on_device(
+def routed_device(
     residual_in,
     norm_gain,
     q_nope,
@@ -173,7 +181,542 @@
     return (layer_out, histogram)
 
 
+def turn(place):
+    return place ^ (place // 2)
+
+
+def positions(exp_devices):
+    ctx_here, here = lax.axis_index("ctx"), lax.axis_index("exp")
+    rows = exp_devices // 2
+    z_at, x_at = here // 2, here % 2
+    order = [
+        turn((turn(z_at) - step + rows) % rows) * 2 + (x_at if side == 0 else 1 - x_at)
+        for step in range(rows)
+        for side in range(2)
+    ]
+    return jnp.stack([x_at, ctx_here, here, *order]).astype(jnp.int32)
+
+
+def swap_exp(value, bit=1):
+    return lax.ppermute(value, "exp", [(e, e ^ bit) for e in range(lax.axis_size("exp"))])
+
+
+def ring_z(value):
+    rows = lax.axis_size("exp") // 2
+    steps = [(turn(at), turn((at + 1) % rows)) for at in range(rows)]
+    return lax.ppermute(value, "exp", [(2 * a + x, 2 * b + x) for a, b in steps for x in range(2)])
+
+
+def swap_ctx(value, bit):
+    return lax.ppermute(value, "ctx", [(c, c ^ bit) for c in range(lax.axis_size("ctx"))])
+
+
+def after(value, earlier):
+    return lax.optimization_barrier((value, earlier))[0]
+
+
+def one_step(work, *inputs):
+    taken = lax.axis_index("ctx") // lax.axis_size("ctx") == 0
+
+    def blank(*arrays):
+        return jax.tree.map(lambda leaf: jnp.zeros(leaf.shape, leaf.dtype), jax.eval_shape(work, *arrays))
+
+    return lax.cond(taken, work, blank, *inputs)
+
+
+def reduce_exp(*blocks):
+    rows, across = len(blocks) // 2, {}
+    for step in list(range(1, rows)) + [0]:
+        across[step] = blocks[2 * step], swap_exp(blocks[2 * step + 1])
+    total = sum(term.astype(jnp.float32) for term in across[1])
+    for step in range(2, rows):
+        moved = ring_z(total.astype(jnp.bfloat16))
+        total = moved.astype(jnp.float32) + sum(term.astype(jnp.float32) for term in across[step])
+    return ring_z(total.astype(jnp.bfloat16)), *across[0]
+
+
+def norm_kernel(moved, mine, across, residual, gain, table, stream, out):
+    width = stream.shape[1]
+    state = residual[...].astype(jnp.float32) + (
+        moved[...].astype(jnp.float32) + (mine[...].astype(jnp.float32) + across[...].astype(jnp.float32))
+    )
+    stream[...] = state
+    mean = jnp.sum(state * state, axis=1, keepdims=True) * (1.0 / width)
+    out[:, :width] = (state * lax.rsqrt(mean + norm_eps) * gain[...]).astype(out.dtype)
+    out[:, width:] = table[...]
+
+
+def norm_rows(moved, mine, across, residual, gain, table):
+    rows, width = residual.shape
+    whole = pl.BlockSpec(memory_space=pltpu.VMEM)
+    return pl.pallas_call(
+        norm_kernel,
+        in_specs=[whole] * 6,
+        out_specs=[whole] * 2,
+        out_shape=[
+            jax.ShapeDtypeStruct((rows, width), jnp.float32),
+            pltpu.VMEM((rows, width + table.shape[1]), jnp.bfloat16),
+        ],
+        compiler_params=pltpu.CompilerParams(vmem_limit_bytes=VMEM_BYTES),
+        cost_estimate=pl.CostEstimate(flops=8 * rows * width, bytes_accessed=14 * rows * width, transcendentals=rows),
+        name="norm",
+    )(moved, mine, across, residual, gain[None, :], table)
+
+
+def gather_exp(block):
+    found = []
+    for step in range(lax.axis_size("exp") // 2):
+        if step:
+            block = ring_z(after(block, found[-3]) if step > 1 else block)
+            found.append(block)
+        found.append(swap_exp(block))
+    return found
+
+
+def pack_kernel(here, latent, k_rope, docs, own, sent):
+    keys, lat_width, rope_width = latent.shape[0], latent.shape[1], k_rope.shape[1]
+    own[:, :lat_width] = latent[...]
+    row = lax.broadcasted_iota(jnp.int32, (128, 128), 0)
+    lane = lax.broadcasted_iota(jnp.int32, (128, 128), 1)
+    for at in range(keys // 128):
+        wide = jnp.broadcast_to(docs[at : at + 1, :], (128, 128))
+        column = jnp.sum(jnp.where(row == lane, wide, 0), axis=1, keepdims=True)
+        ropes = jnp.concatenate(
+            [k_rope[at * 128 : (at + 1) * 128, :].astype(jnp.float32), jnp.zeros((128, 128 - rope_width), jnp.float32)],
+            axis=1,
+        )
+        own[at * 128 : (at + 1) * 128, lat_width:] = jnp.where(
+            lane == rope_width, column.astype(jnp.float32), ropes
+        ).astype(jnp.bfloat16)
+    half = sent.shape[0]
+    sent[...] = own[pl.ds(pl.multiple_of(here[0] * half, half), half), :]
+
+
+def pack_keys(here, latent, k_rope, doc_ids):
+    keys, width = latent.shape[0], latent.shape[1] + 128
+    whole = pl.BlockSpec(memory_space=pltpu.VMEM)
+    return pl.pallas_call(
+        pack_kernel,
+        in_specs=[pl.BlockSpec(memory_space=pltpu.SMEM)] + [whole] * 3,
+        out_specs=[whole] * 2,
+        out_shape=[
+            jax.ShapeDtypeStruct((keys, width), jnp.bfloat16),
+            jax.ShapeDtypeStruct((keys // 2, width), jnp.bfloat16),
+        ],
+        cost_estimate=pl.CostEstimate(flops=0, bytes_accessed=6 * keys * width, transcendentals=0),
+        compiler_params=pltpu.CompilerParams(vmem_limit_bytes=8 * 1024 * 1024),
+        name="pack",
+    )(here, latent, k_rope, doc_ids.reshape(keys // 128, 128))
+
+
+def join_kernel(left, right, *refs):
+    outs, sems = refs[:-1], refs[-1]
+    width, first, copies = left.shape[1], 0, []
+    for out in outs:
+        for side, weight in enumerate((left, right)):
+            copies.append(
+                pltpu.make_async_copy(
+                    weight.at[pl.ds(first, out.shape[0])],
+                    out.at[:, pl.ds(side * width, width)],
+                    sems.at[len(copies)],
+                )
+            )
+            copies[-1].start()
+        first += out.shape[0]
+    for copy in copies:
+        copy.wait()
+
+
+def join_weights(left, right, ends):
+    width = left.shape[1]
+    counts = [end - first for first, end in zip((0, *ends[:-1]), ends)]
+    anywhere = pl.BlockSpec(memory_space=pl.ANY)
+    return pl.pallas_call(
+        join_kernel,
+        in_specs=[anywhere] * 2,
+        out_specs=[anywhere] * len(ends),
+        out_shape=[jax.ShapeDtypeStruct((count, 2 * width), left.dtype) for count in counts],
+        scratch_shapes=[pltpu.SemaphoreType.DMA((2 * len(ends),))],
+        compiler_params=pltpu.CompilerParams(vmem_limit_bytes=1024 * 1024),
+        cost_estimate=pl.CostEstimate(flops=0, bytes_accessed=8 * left.size, transcendentals=0),
+        name="join",
+    )(left, right)
+
+
+def route_kernel(ids, levels, bins, out, *, experts):
+    lane = lax.broadcasted_iota(jnp.int32, out.shape, 1)
+    table = jnp.zeros(out.shape, jnp.int32)
+    for at, what in enumerate((levels[...], bins[...] // 128, bins[...] % 128)):
+        for expert in range(experts):
+            column = jnp.sum(jnp.where(ids[...] == expert, what, 0), axis=1, keepdims=True)
+            table = jnp.where(lane == at * experts + expert, column, table)
+    out[...] = table.astype(jnp.float32).astype(out.dtype)
+
+
+def route_table(expert_ids, gate_levels, bin_ids, experts):
+    whole = pl.BlockSpec(memory_space=pltpu.VMEM)
+    return pl.pallas_call(
+        functools.partial(route_kernel, experts=experts),
+        in_specs=[whole] * 3,
+        out_specs=whole,
+        out_shape=jax.ShapeDtypeStruct((expert_ids.shape[0], 128), jnp.bfloat16),
+        compiler_params=pltpu.CompilerParams(vmem_limit_bytes=4 * 1024 * 1024),
+        name="route",
+    )(expert_ids, gate_levels, bin_ids)
+
+
+def attend_kernel(scalars, q_nope, q_rope, *refs, heads, rope_width):
+    own, near_even, near_a, near_b, far_a, far_b, uv, out, keys, more, sems = refs
+    tile, block_len, half = out.shape[0], own.shape[0], far_a.shape[0]
+    lat_width = uv.shape[1]
+    first = pl.program_id(0) * tile
+    places = [
+        (own, keys, 0),
+        (near_even, keys, block_len),
+        (near_a, more, 0),
+        (near_b, more, half),
+        (far_a, keys, 2 * block_len),
+        (far_b, keys, 2 * block_len + half),
+    ]
+    copies = [
+        pltpu.make_async_copy(piece, into.at[pl.ds(at, piece.shape[0])], sems.at[number])
+        for number, (piece, into, at) in enumerate(places)
+    ]
+
+    @pl.when(pl.program_id(0) == 0)
+    def _():
+        for copy in copies:
+            copy.start()
+        for copy in copies:
+            copy.wait()
+        keys[block_len : 2 * block_len, :] = keys[block_len : 2 * block_len, :] + more[...]
+
+    doc_at = lat_width + rope_width
+    pick = (lax.broadcasted_iota(jnp.int32, (8, 128), 1) == rope_width).astype(jnp.bfloat16)
+    query_docs = keys[pl.ds(pl.multiple_of(first, tile), tile), lat_width:][:, rope_width : rope_width + 1].astype(jnp.float32)
+    over = (((1,), (1,)), ((), ()))
+    docs = lax.dot_general(pick, keys[:, lat_width:], over, preferred_element_type=jnp.float32)[0:1, :]
+    key_at = lax.broadcasted_iota(jnp.int32, (1, keys.shape[0]), 1)
+    docs = jnp.where(key_at < (scalars[1] + 1) * block_len, docs, -1.0)
+    spare = jnp.zeros((tile, keys.shape[1] - doc_at), jnp.bfloat16)
+    query = jnp.concatenate(
+        [
+            jnp.concatenate(
+                [
+                    q_nope[:, head * lat_width : (head + 1) * lat_width],
+                    q_rope[:, head * rope_width : (head + 1) * rope_width],
+                    spare,
+                ],
+                axis=1,
+            )
+            for head in range(heads)
+        ],
+        axis=0,
+    )
+    scores, top = [], None
+    for block in range(keys.shape[0] // block_len):
+        at = slice(block * block_len, (block + 1) * block_len)
+        same = docs[:, at] == query_docs
+        if block == 0:
+            within = lax.broadcasted_iota(jnp.int32, (tile, block_len), 1)
+            same = same & (within <= lax.broadcasted_iota(jnp.int32, (tile, block_len), 0) + first)
+        raw = lax.dot_general(query, keys[at, :], over, preferred_element_type=jnp.float32)
+        same = jnp.concatenate([same] * heads, axis=0)
+        scores.append(jnp.where(same, raw * (softmax_scale * LOG2_E), masked_score))
+        most = jnp.max(scores[-1], axis=1, keepdims=True)
+        top = most if top is None else jnp.maximum(top, most)
+    total, accum = 0.0, 0.0
+    for block, score in enumerate(scores):
+        probs = jnp.exp2(score - top)
+        total = total + jnp.sum(probs, axis=1, keepdims=True)
+        accum = accum + jnp.dot(
+            probs.astype(jnp.bfloat16),
+            keys[block * block_len : (block + 1) * block_len, :lat_width],
+            preferred_element_type=jnp.float32,
+        )
+    context = (accum / total).astype(jnp.bfloat16)
+    width = uv.shape[2]
+    for head in range(heads):
+        value = jnp.dot(context[head * tile : (head + 1) * tile], uv[head], preferred_element_type=jnp.float32)
+        out[:, head * width : (head + 1) * width] = value.astype(out.dtype)
+
+
+def attend(here, q_nope, q_rope, pieces, uv_weight, rope_width):
+    queries, (block_len, width) = q_nope.shape[0], pieces[0].shape
+    heads, lat_width, value_width = uv_weight.shape
+    tile = 256
+    return pl.pallas_call(
+        functools.partial(attend_kernel, heads=heads, rope_width=rope_width),
+        grid_spec=pltpu.PrefetchScalarGridSpec(
+            num_scalar_prefetch=1,
+            grid=(queries // tile,),
+            in_specs=[
+                pl.BlockSpec((tile, heads * lat_width), lambda i, s: (i, 0)),
+                pl.BlockSpec((tile, heads * rope_width), lambda i, s: (i, 0)),
+                *[pl.BlockSpec(memory_space=pltpu.HBM) for _ in pieces],
+                pl.BlockSpec(uv_weight.shape, lambda i, s: (0, 0, 0)),
+            ],
+            out_specs=pl.BlockSpec((tile, heads * value_width), lambda i, s: (i, 0)),
+            scratch_shapes=[
+                pltpu.VMEM((3 * block_len, width), jnp.bfloat16),
+                pltpu.VMEM((block_len, width), jnp.bfloat16),
+                pltpu.SemaphoreType.DMA((len(pieces),)),
+            ],
+        ),
+        out_shape=jax.ShapeDtypeStruct((queries, heads * value_width), jnp.bfloat16),
+        compiler_params=pltpu.CompilerParams(vmem_limit_bytes=24 * 1024 * 1024),
+        cost_estimate=pl.CostEstimate(
+            flops=6 * heads * queries * block_len * (width + lat_width),
+            bytes_accessed=2 * (q_nope.size + 4 * block_len * width + uv_weight.size),
+            transcendentals=3 * heads * queries * block_len,
+        ),
+        name="attend",
+    )(here, q_nope, q_rope, *pieces, uv_weight)
+
+
+def project_kernel(order, values, weight, *outs):
+    rows = outs[0].shape[0]
+    picked = jnp.concatenate(
+        [values[pl.ds(pl.multiple_of(order[3 + at] * rows, rows), rows), :] for at in range(len(outs))], axis=0
+    )
+    result = jnp.dot(picked, weight[...], preferred_element_type=jnp.float32).astype(outs[0].dtype)
+    for at, out in enumerate(outs):
+        out[...] = result[at * rows : (at + 1) * rows]
+
+
+def project_blocks(here, values, weight, count):
+    rows, inner = values.shape
+    width = weight.shape[1]
+    block, tile = rows // count, 896
+    return pl.pallas_call(
+        project_kernel,
+        grid_spec=pltpu.PrefetchScalarGridSpec(
+            num_scalar_prefetch=1,
+            grid=(width // tile,),
+            in_specs=[
+                pl.BlockSpec((rows, inner), lambda n, s: (0, 0)),
+                pl.BlockSpec((inner, tile), lambda n, s: (0, n)),
+            ],
+            out_specs=[pl.BlockSpec((block, tile), lambda n, s: (0, n))] * count,
+        ),
+        out_shape=[pltpu.VMEM((block, width), jnp.bfloat16)] * count,
+        compiler_params=pltpu.CompilerParams(vmem_limit_bytes=32 * 1024 * 1024),
+        cost_estimate=pl.CostEstimate(
+            flops=2 * rows * inner * width, bytes_accessed=2 * (inner + rows) * width, transcendentals=0
+        ),
+        name="project",
+    )(here, values, weight)
+
+
+def hidden_kernel(here, *refs, blocks, counts, experts):
+    rows, rest = refs[:blocks], refs[blocks:]
+    copies = []
+    if counts:
+        pieces, (hidden, energy_bins, scale, held, row_data, sems) = rest[: sum(counts)], rest[sum(counts) :]
+        at = 0
+        for part, count in enumerate(counts):
+            copies.append([])
+            first = 0
+            for piece in pieces[at : at + count]:
+                into = held.at[part, pl.ds(first, piece.shape[0])]
+                copies[-1].append(pltpu.make_async_copy(piece, into, sems.at[at]))
+                copies[-1][-1].start()
+                first += piece.shape[0]
+                at += 1
+    else:
+        held, hidden, energy_bins, scale, row_data = rest
+    parts, inner, units, each = held.shape[0], held.shape[1], held.shape[2] // 2, rows[0].shape[0]
+    for at, row in enumerate(rows):
+        row_data[at * each : (at + 1) * each, :] = row[:, :inner]
+    table = jnp.concatenate([row[:, inner:] for row in rows], axis=0).astype(jnp.float32)
+    lane = lax.broadcasted_iota(jnp.int32, table.shape, 1)
+
+    def column(first):
+        return jnp.sum(jnp.where(lane == first + here[2], table, 0.0), axis=1, keepdims=True)
+
+    levels = jnp.sum(jnp.where(lane < experts, table, 0.0), axis=1, keepdims=True)
+    scale[...] = column(0) / levels
+    squares = 0.0
+    for part in range(parts):
+        for copy in copies[part] if counts else ():
+            copy.wait()
+        both = jnp.dot(row_data[...], held[part], preferred_element_type=jnp.float32)
+        gate_part, up_part = both[:, :units], both[:, units:]
+        activation = gate_part / (1.0 + jnp.exp(-gate_part)) * up_part
+        hidden[:, part * units : (part + 1) * units] = activation.astype(hidden.dtype)
+        squares = squares + jnp.sum(activation * activation, axis=1, keepdims=True)
+    place = lane.astype(jnp.float32)
+    high = jnp.where(place == column(experts), squares * (1.0 / HID), 0.0)
+    low = jnp.where(place == column(2 * experts), 1.0, 0.0)
+    counted = jnp.dot(high.T, low, precision=lax.Precision.HIGHEST, preferred_element_type=jnp.float32)
+    energy_bins[...] = counted[: energy_bins.shape[0], :]
+
+
+def hidden_rows(here, rows, weights, experts):
+    first = isinstance(weights, list)
+    whole = pl.BlockSpec(memory_space=pltpu.VMEM)
+    if first:
+        counts = tuple(len(pieces) for pieces in weights)
+        parts, both = len(weights), weights[0][0].shape[1]
+        inner = sum(piece.shape[0] for piece in weights[0])
+        operands = [piece for pieces in weights for piece in pieces]
+    else:
+        counts, (parts, inner, both), operands = None, weights.shape, [weights]
+    count = len(rows) * rows[0].shape[0]
+    kept = [pltpu.VMEM((parts, inner, both), jnp.bfloat16)] if first else []
+    return pl.pallas_call(
+        functools.partial(hidden_kernel, blocks=len(rows), counts=counts, experts=experts),
+        in_specs=[pl.BlockSpec(memory_space=pltpu.SMEM)]
+        + [whole] * len(rows)
+        + [pl.BlockSpec(memory_space=pltpu.HBM) if first else whole] * len(operands),
+        out_specs=[whole] * (3 + len(kept)),
+        out_shape=[
+            jax.ShapeDtypeStruct((count, parts * both // 2), jnp.bfloat16),
+            jax.ShapeDtypeStruct((NBINS // 128, 128), jnp.float32),
+            jax.ShapeDtypeStruct((count, 1), jnp.float32),
+            *kept,
+        ],
+        scratch_shapes=[pltpu.VMEM((count, inner), jnp.bfloat16)]
+        + ([pltpu.SemaphoreType.DMA((len(operands),))] if first else []),
+        compiler_params=pltpu.CompilerParams(vmem_limit_bytes=VMEM_BYTES),
+        cost_estimate=pl.CostEstimate(
+            flops=2 * count * inner * parts * both,
+            bytes_accessed=2 * inner * (count + parts * both),
+            transcendentals=count * parts * both // 2,
+        ),
+        name="hidden",
+    )(here, *rows, *operands)
+
+
+def down_kernel(*refs, pieces, parts, tile):
+    hidden, scales, weights = refs[:pieces], refs[pieces : 2 * pieces], refs[2 * pieces : 2 * pieces + parts]
+    outs = refs[2 * pieces + parts :]
+    rows, units = outs[0].shape[0], weights[0].shape[0]
+    each = hidden[0].shape[0]
+    for piece in range(pieces):
+        for at in range(outs[0].shape[1] // tile):
+            columns = slice(at * tile, (at + 1) * tile)
+            total = 0.0
+            for part, weight in enumerate(weights):
+                total = total + jnp.dot(
+                    hidden[piece][:, part * units : (part + 1) * units],
+                    weight[:, columns],
+                    preferred_element_type=jnp.float32,
+                )
+            total = (total * scales[piece][...]).astype(outs[0].dtype)
+            for block in range(each // rows):
+                outs[piece * (each // rows) + block][:, columns] = total[block * rows : (block + 1) * rows]
+
+
+def down_blocks(hidden, scales, weights, count):
+    pieces, parts, tile = len(hidden), len(weights), 512
+    each, inner = hidden[0].shape
+    units, width = weights[0].shape
+    whole = pl.BlockSpec(memory_space=pltpu.VMEM)
+    return pl.pallas_call(
+        functools.partial(down_kernel, pieces=pieces, parts=parts, tile=tile),
+        in_specs=[whole] * (2 * pieces + parts),
+        out_specs=[whole] * count,
+        out_shape=[pltpu.VMEM((pieces * each // count, width), jnp.bfloat16)] * count,
+        compiler_params=pltpu.CompilerParams(vmem_limit_bytes=VMEM_BYTES),
+        cost_estimate=pl.CostEstimate(
+            flops=2 * pieces * each * inner * width,
+            bytes_accessed=2 * width * (inner + pieces * each),
+            transcendentals=0,
+        ),
+        name="down",
+    )(*hidden, *scales, *weights)
+
+
+def spread_bins(counts):
+    counts = counts.reshape(2, 2, NBINS // 4)
+    ctx_here = lax.axis_index("ctx")
+    for at, bit in ((ctx_here // 2, 2), (ctx_here % 2, 1)):
+        counts = lax.dynamic_index_in_dim(counts, at, 0, keepdims=False) + swap_ctx(
+            lax.dynamic_index_in_dim(counts, 1 - at, 0, keepdims=False), bit
+        )
+    return counts[None, :]
+
+
+def dense_device(
+    residual_in,
+    norm_gain,
+    q_nope,
+    q_rope,
+    latent,
+    k_rope,
+    doc_ids,
+    uv_weight,
+    out_weight,
+    expert_ids,
+    gate_levels,
+    bin_ids,
+    gate_weight,
+    up_weight,
+    down_weight,
+):
+    exp_devices, ctx_devices = lax.axis_size("exp"), lax.axis_size("ctx")
+    block_len, head_count, lat_width = q_nope.shape
+    rope_width = k_rope.shape[1]
+    here = positions(exp_devices)
+
+    own, sent = pack_keys(here, latent, k_rope, doc_ids)
+    table = route_table(expert_ids, gate_levels, bin_ids, exp_devices)
+    far_a = lax.ppermute(sent, "ctx", [(c, c + 2) for c in range(ctx_devices - 2)])
+    near_even = lax.ppermute(own, "ctx", [(c, c + 1) for c in range(0, ctx_devices, 2)])
+    flat_q = q_nope.reshape(block_len, head_count * lat_width)
+    w_gate, w_up, w_down = gate_weight[0], up_weight[0], down_weight[0]
+    part_a, part_b = FIRST_ROWS
+    own_both = join_weights(w_gate, w_up, (part_a, part_b, w_gate.shape[0]))
+    far_b = swap_exp(after(far_a, (flat_q, own_both, table)))
+    near_a = lax.ppermute(far_a, "ctx", [(3, 2)])
+    near_b = lax.ppermute(far_b, "ctx", [(3, 2)])
+
+    both_a = swap_ctx(after(own_both[0], far_a), 2)
+    there_both = [swap_ctx(piece, 1) for piece in own_both]
+    own = after(own, both_a)
+    both_b = swap_ctx(after(own_both[1], own), 2)
+    key_pieces = [own, near_even, near_a, near_b, far_a, far_b]
+    values = attend(here, flat_q, q_rope, key_pieces, uv_weight, rope_width)
+    values = after(values, both_b)
+    both_c = swap_ctx(after(own_both[2], values), 2)
+    partial = project_blocks(here, values, out_weight, exp_devices)
+    def sum_and_norm(partial, *rest):
+        return norm_rows(*reduce_exp(*partial), *rest)
+
+    swapped = [swap_ctx(both_a, 1), swap_ctx(both_b, 1)]
+    stream_state, block = after(
+        one_step(sum_and_norm, partial, residual_in, norm_gain, table), (both_c, swapped, there_both)
+    )
+    far_down = swap_ctx(after(w_down, block), 2)
+
+    def gather_and_hide(block, here, own_both, there_both, far_both, swapped):
+        weights = [own_both, there_both, far_both, [*swapped, swap_ctx(far_both[-1], 1)]]
+        found = [block, *gather_exp(block)]
+        half = len(found) // 2
+        *first, held = hidden_rows(here, found[:half], weights, exp_devices)
+        last = hidden_rows(here, found[half:], held, exp_devices)
+        return [*zip(first, last)]
+
+    hidden, bins, scales = after(
+        one_step(gather_and_hide, block, here, own_both, there_both, [both_a, both_b, both_c], swapped), far_down
+    )
+    downs = [w_down, swap_ctx(w_down, 1), far_down, swap_ctx(after(far_down, hidden), 1)]
+    expert_out = down_blocks(hidden, scales, downs, exp_devices)
+    mixture = reduce_exp(*expert_out)
+    layer_out = (stream_state + sum(term.astype(jnp.float32) for term in mixture)).astype(jnp.bfloat16)
+    histogram = spread_bins(after(bins[0] + bins[1], expert_out[0]))
+    return (layer_out, histogram)
+
+
 def solution(mesh):
+    sizes = mesh.shape
+
+    def on_device(*arrays):
+        named_experts = arrays[9].shape[1]
+        dense = sizes["exp"] == 8 and sizes["ctx"] == 4 and named_experts == sizes["exp"]
+        return (dense_device if dense else routed_device)(*arrays)
+
     return jax.shard_map(
         on_device,
         mesh=mesh,

time: 677 us -> 223 us (0.33); the launches traced: 668 us -> 222 us
  waiting for transfers between devices: 392 us -> 125 us
  blocking collectives: 104 us -> 0 us
  matrix products: 73 us -> 0 us
  Pallas kernels: 0 us -> 34.6 us
  other arithmetic: 33 us -> 2.43 us
  starting transfers between devices: 20.5 us -> 50.8 us
  local copies, waits for them, and re-layouts: 32.4 us -> 8.52 us
  between operations: 14.2 us -> 1.13 us
    reduce_scatter x2 -> x0, waiting for transfers between devices: 228 us -> none  [the longest x1 130 us: on_device(): lax.psum_scatter(head_rows(jnp.int32(0), token_count * lax.axis_size('exp...]
    ppermute x0 -> x40, waiting for transfers between devices: none -> 125 us  [the longest x13 73.2 us: swap_exp(): lax.ppermute(value, 'exp', [(e, e ^ bit) for e in range(lax.axis_size('ex...]
    all_gather x2 -> x0, waiting for transfers between devices: 105 us -> none  [the longest x1 93.2 us: on_device(): lax.all_gather(incoming, 'ctx', axis=1, tiled=True)]
    all_to_all x1 -> x0, blocking collectives: 85.7 us -> none  [on_device(): lax.all_to_all(outgoing, 'exp', split_axis=0, concat_axis=1, tiled=True)]
    dot_general x9 -> x0, matrix products: 58.3 us -> none  [the longest x1 11.7 us: expert_hidden(): up_part = jnp.dot(row_data, w_up, preferred_element_type=jnp.float32)]
    ppermute x0 -> x40, starting transfers between devices: none -> 50.8 us  [the longest x13 16.7 us: swap_exp(): lax.ppermute(value, 'exp', [(e, e ^ bit) for e in range(lax.axis_size('ex...]
    pallas_call x0 -> x9, Pallas kernels: none -> 34.6 us  [the longest x2 12.7 us: hidden_rows(): pl.pallas_call(functools.partial(hidden_kernel, blocks=len(rows), counts=...]
    all_to_all x2 -> x0, waiting for transfers between devices: 33.7 us -> none  [the longest x1 33.7 us: on_device(): lax.all_to_all(expert_out[None], 'exp', split_axis=1, concat_axis=0, tile...]
  transfers between devices with their start and end apart: 7 -> 40, of which waited for: 6 -> 27; matrix products, arithmetic and copies ran while one was open for 10% -> 1% of each run, Pallas kernels for 0% -> 12%
where the time goes in v3:
time: 223 us; the launch traced here: 222 us
  waiting for transfers between devices  125 us (56%)
  starting transfers between devices  50.8 us (23%)
  Pallas kernels  34.6 us (16%)
  local copies, waits for them, and re-layouts  8.52 us (4%)
  other arithmetic  2.43 us (1%)
    ppermute x13, waiting for transfers between devices, swap_exp(): lax.ppermute(value, 'exp', [(e, e ^ bit) for e in range(lax.axis_size('ex...  73.2 us
    ppermute x9, waiting for transfers between devices, ring_z(): lax.ppermute(value, 'exp', [(2 * a + x, 2 * b + x) for a, b in steps for...  27.9 us
    ppermute x14, waiting for transfers between devices, swap_ctx(): lax.ppermute(value, 'ctx', [(c, c ^ bit) for c in range(lax.axis_size('ct...  23.4 us
    ppermute x13, starting transfers between devices, swap_exp(): lax.ppermute(value, 'exp', [(e, e ^ bit) for e in range(lax.axis_size('ex...  16.7 us
    ppermute x9, starting transfers between devices, ring_z(): lax.ppermute(value, 'exp', [(2 * a + x, 2 * b + x) for a, b in steps for...  14.3 us
    pallas_call x2, Pallas kernels, hidden_rows(): pl.pallas_call(functools.partial(hidden_kernel, blocks=len(rows), counts=...  12.7 us
    ppermute x14, starting transfers between devices, swap_ctx(): lax.ppermute(value, 'ctx', [(c, c ^ bit) for c in range(lax.axis_size('ct...  11.2 us
    unnamed x41, local copies, waits for them, and re-layouts  8.38 us
  transfers between devices with their start and end apart: 40, of which 27 were waited for; matrix products, arithmetic and copies ran while one was open for 1% of the time, Pallas kernels for 12%

profile of v3, /device:TPU:0, one launch (start us, length us, event | category | flops | bytes accessed | tf_op | source)
XLA Modules:
  0.0 222.3 jit_solution(425801492025951797)
XLA Ops:
  5.4 4.9 %collective-permute-start.15 = (bf16[256,640]{1,0:T(8,128)(2,1)}, bf16[256,640]{1,0:T(8,128)(2,1)S(1)}, u32[]{:S(2)}, u32[]{:S(2)}) collective-permute-start(bf16[256,640]{1,0:T(8,128)(2,1)} %get-tuple-element.131), channel_id=1, source_target_pairs={{0,16},{8,24},{1,17},{9,25},{2,18},{10,26},{3,19},{11,27},{4,20},{... | collective-permute-start | bytes 983048 | tf_op jit(solution)/shard_map/ppermute | solution.py:665
  22.1 4.2 %collective-permute-done.19.refs_5_ = bf16[256,640]{1,0:T(8,128)(2,1)S(1)} collective-permute-done((bf16[256,640]{1,0:T(8,128)(2,1)S(1)}, bf16[256,640]{1,0:T(8,128)(2,1)S(1)}, u32[]{:S(2)}, u32[]{:S(2)}) %collective-permute-start.19) | collective-permute-done | bytes 327712 | tf_op jit(solution)/shard_map/ppermute | solution.py:201
  30.8 7.9 %attend.1.values = bf16[512,256]{1,0:T(8,128)(2,1)S(1)} custom-call(s32[11]{0:T(128)S(1)} %stack.47.here.scalars.order, bf16[512,1024]{1,0:T(8,128)(2,1)S(1)} %bitcast.26, bf16[512,128]{1,0:T(8,128)(2,1)S(1)} %copy-done.7, bf16[512,640]{1,0:T(8,128)(2,1)} %get-tuple-element.133.refs_0_, bf16[512,640]{1,0:T(8,128)(2,1)} %collective-permute-done.17.refs_1_, ...), custom_call_target="tpu_custom_call" | custom-call | flops 3623878656 | bytes 3932160 | tf_op jit(solution)/shard_map/attend/pallas_call | solution.py:448
  38.7 6.4 %collective-permute-done.21 = bf16[640,512]{1,0:T(8,128)(2,1)S(1)} collective-permute-done((bf16[640,512]{1,0:T(8,128)(2,1)S(1)}, bf16[640,512]{1,0:T(8,128)(2,1)S(1)}, u32[]{:S(2)}, u32[]{:S(2)}) %collective-permute-start.21) | collective-permute-done | bytes 655392 | tf_op jit(solution)/shard_map/ppermute | solution.py:211
  52.5 46.6 %conditional.2 = ((f32[64,3584]{1,0:T(8,128)}, bf16[64,3712]{1,0:T(8,128)(2,1)S(1)})) conditional(s32[]{:T(128)} %convert_element_type.82, () %tuple.36, (bf16[64,3584]{1,0:T(8,128)(2,1)S(1)}, bf16[64,3584]{1,0:T(8,128)(2,1)S(1)}, bf16[64,3584]{1,0:T(8,128)(2,1)S(1)}, bf16[64,3584]{1,0:T(8,128)(2,1)S(1)}, bf16[64,3584]{1,0:T(8,128)(2,1)S(1)}, ...), branch_computations={%region_0.1_spmd, %region_1.2_spmd} | conditional | flops 5505024 | bytes 22966588 | solution.py:224
  54.6 11.4 %collective-permute-done.8 = bf16[64,3584]{1,0:T(8,128)(2,1)S(1)} collective-permute-done((bf16[64,3584]{1,0:T(8,128)(2,1)S(1)}, bf16[64,3584]{1,0:T(8,128)(2,1)S(1)}, u32[]{:S(2)}, u32[]{:S(2)}) %collective-permute-start.8) | collective-permute-done | bytes 458784 | tf_op jit(solution)/shard_map/cond/branch_1_fun/ppermute | solution.py:201
  69.2 6.6 %collective-permute-done.10 = bf16[64,3584]{1,0:T(8,128)(2,1)S(1)} collective-permute-done((bf16[64,3584]{1,0:T(8,128)(2,1)S(1)}, bf16[64,3584]{1,0:T(8,128)(2,1)S(1)}, u32[]{:S(2)}, u32[]{:S(2)}) %collective-permute-start.10) | collective-permute-done | bytes 458784 | tf_op jit(solution)/shard_map/cond/branch_1_fun/ppermute | solution.py:201
  79.9 5.8 %collective-permute-done.12 = bf16[64,3584]{1,0:T(8,128)(2,1)S(1)} collective-permute-done((bf16[64,3584]{1,0:T(8,128)(2,1)S(1)}, bf16[64,3584]{1,0:T(8,128)(2,1)S(1)}, u32[]{:S(2)}, u32[]{:S(2)}) %collective-permute-start.12) | collective-permute-done | bytes 458784 | tf_op jit(solution)/shard_map/cond/branch_1_fun/ppermute | solution.py:201
  89.1 5.2 %collective-permute-done.14.across = bf16[64,3584]{1,0:T(8,128)(2,1)S(1)} collective-permute-done((bf16[64,3584]{1,0:T(8,128)(2,1)S(1)}, bf16[64,3584]{1,0:T(8,128)(2,1)S(1)}, u32[]{:S(2)}, u32[]{:S(2)}) %collective-permute-start.14) | collective-permute-done | bytes 458784 | tf_op jit(solution)/shard_map/cond/branch_1_fun/ppermute | solution.py:201
  94.4 3.4 %collective-permute-done.13.moved = bf16[64,3584]{1,0:T(8,128)(2,1)S(1)} collective-permute-done((bf16[64,3584]{1,0:T(8,128)(2,1)S(1)}, bf16[64,3584]{1,0:T(8,128)(2,1)S(1)}, u32[]{:S(2)}, u32[]{:S(2)}) %collective-permute-start.13) | collective-permute-done | bytes 458784 | tf_op jit(solution)/shard_map/cond/branch_1_fun/ppermute | solution.py:207
  104.5 3.9 %collective-permute-done.22 = bf16[2688,512]{1,0:T(8,128)(2,1)} collective-permute-done((bf16[2688,512]{1,0:T(8,128)(2,1)}, bf16[2688,512]{1,0:T(8,128)(2,1)}, u32[]{:S(2)}, u32[]{:S(2)}) %collective-permute-start.22) | collective-permute-done | bytes 2752544 | tf_op jit(solution)/shard_map/ppermute | solution.py:211
  110.2 54.4 %conditional.3 = (bf16[256,1024]{1,0:T(8,128)(2,1)S(1)}, bf16[256,1024]{1,0:T(8,128)(2,1)S(1)}, f32[16,128]{1,0:T(8,128)S(1)}, f32[16,128]{1,0:T(8,128)S(1)}, f3...) conditional(s32[]{:T(128)} %convert_element_type.82, () %tuple.45, (bf16[64,3712]{1,0:T(8,128)(2,1)S(1)}, ...), branch_computations={%region_2.3_spmd, %region_3.4_spmd} | conditional | flops 7516192768 | bytes 57344368 | solution.py:224
  113.8 9.7 %collective-permute-done.refs_1_ = bf16[64,3712]{1,0:T(8,128)(2,1)S(1)} collective-permute-done((bf16[64,3712]{1,0:T(8,128)(2,1)S(1)}, bf16[64,3712]{1,0:T(8,128)(2,1)S(1)}, u32[]{:S(2)}, u32[]{:S(2)}) %collective-permute-start) | collective-permute-done | bytes 475168 | tf_op jit(solution)/shard_map/cond/branch_1_fun/ppermute | solution.py:201
  126.9 10.3 %collective-permute-done.2.refs_3_ = bf16[64,3712]{1,0:T(8,128)(2,1)S(1)} collective-permute-done((bf16[64,3712]{1,0:T(8,128)(2,1)S(1)}, bf16[64,3712]{1,0:T(8,128)(2,1)S(1)}, u32[]{:S(2)}, u32[]{:S(2)}) %collective-permute-start.2) | collective-permute-done | bytes 475168 | tf_op jit(solution)/shard_map/cond/branch_1_fun/ppermute | solution.py:201
  140.6 9.0 %collective-permute-done.6.refs_2_ = bf16[64,3712]{1,0:T(8,128)(2,1)S(1)} collective-permute-done((bf16[64,3712]{1,0:T(8,128)(2,1)S(1)}, bf16[64,3712]{1,0:T(8,128)(2,1)S(1)}, u32[]{:S(2)}, u32[]{:S(2)}) %collective-permute-start.6) | collective-permute-done | bytes 475168 | tf_op jit(solution)/shard_map/cond/branch_1_fun/ppermute | solution.py:207
  151.1 7.8 %hidden.2 = (bf16[256,1024]{1,0:T(8,128)(2,1)S(1)}, f32[16,128]{1,0:T(8,128)S(1)}, f32[256,1]{1,0:T(8,128)S(1)}, bf16[4,3584,512]{2,1,0:T(8,128)(2,1)S(1)}) custom-call(s32[11]{0:T(128)S(1)} %get-tuple-element.59.here, bf16[64,3712]{1,0:T(8,128)(2,1)S(1)} %get-tuple-element.60.refs_0_, bf16[64,3712]{1,0:T(8,128)(2,1)S(1)} %collective-permute-done.refs_1_, ...), custom_call_target="tpu_custom_call" | custom-call | flops 3758096384 | bytes 16515072 | tf_op jit(solution)/shard_map/cond/branch_1_fun/hidden/pallas_call | solution.py:567
  159.4 4.9 %hidden.3 = (bf16[256,1024]{1,0:T(8,128)(2,1)S(1)}, f32[16,128]{1,0:T(8,128)S(1)}, f32[256,1]{1,0:T(8,128)S(1)}) custom-call(s32[11]{0:T(128)S(1)} %get-tuple-element.59.here, bf16[64,3712]{1,0:T(8,128)(2,1)S(1)} %collective-permute-done.4.refs_0_, bf16[64,3712]{1,0:T(8,128)(2,1)S(1)} %collective-permute-done.5.refs_1_, ...), custom_call_target="tpu_custom_call" | custom-call | flops 3758096384 | bytes 16515072 | tf_op jit(solution)/shard_map/cond/branch_1_fun/hidden/pallas_call | solution.py:567
  164.6 4.0 %collective-permute-done.30.refs_7_ = bf16[256,3584]{1,0:T(8,128)(2,1)S(1)} collective-permute-done((bf16[256,3584]{1,0:T(8,128)(2,1)}, bf16[256,3584]{1,0:T(8,128)(2,1)S(1)}, u32[]{:S(2)}, u32[]{:S(2)}) %collective-permute-start.30) | collective-permute-done | bytes 1835040 | tf_op jit(solution)/shard_map/ppermute | solution.py:211
  168.6 6.0 %down.1 = (bf16[64,3584]{1,0:T(8,128)(2,1)S(1)}, bf16[64,3584]{1,0:T(8,128)(2,1)S(1)}, bf16[64,3584]{1,0:T(8,128)(2,1)S(1)}, bf16[64,3584]{1,0:T(8,128)(2,1)S(1)...) custom-call(bf16[256,1024]{1,0:T(8,128)(2,1)S(1)} %get-tuple-element, ...), custom_call_target="tpu_custom_call" | custom-call | flops 3758096384 | bytes 11010048 | tf_op jit(solution)/shard_map/down/pallas_call | solution.py:616
  176.7 11.3 %collective-permute-done.31 = bf16[64,3584]{1,0:T(8,128)(2,1)S(1)} collective-permute-done((bf16[64,3584]{1,0:T(8,128)(2,1)S(1)}, bf16[64,3584]{1,0:T(8,128)(2,1)S(1)}, u32[]{:S(2)}, u32[]{:S(2)}) %collective-permute-start.31) | collective-permute-done | bytes 458784 | tf_op jit(solution)/shard_map/ppermute | solution.py:201
  188.2 3.4 %collective-permute-start.32 = (bf16[64,3584]{1,0:T(8,128)(2,1)S(1)}, bf16[64,3584]{1,0:T(8,128)(2,1)S(1)}, u32[]{:S(2)}, u32[]{:S(2)}) collective-permute-start(bf16[64,3584]{1,0:T(8,128)(2,1)S(1)} %add_convert_fusion.6), channel_id=1, source_target_pairs={{0,2},{1,3},{2,6},{3,7},{6,4},{7,5},{4,0},{5,1},{8,10},{9,11},{10,... | collective-permute-start | bytes 1376264 | tf_op jit(solution)/shard_map/ppermute | solution.py:207
  193.1 4.8 %collective-permute-done.33 = bf16[64,3584]{1,0:T(8,128)(2,1)S(1)} collective-permute-done((bf16[64,3584]{1,0:T(8,128)(2,1)S(1)}, bf16[64,3584]{1,0:T(8,128)(2,1)S(1)}, u32[]{:S(2)}, u32[]{:S(2)}) %collective-permute-start.33) | collective-permute-done | bytes 458784 | tf_op jit(solution)/shard_map/ppermute | solution.py:201
  204.2 3.5 %collective-permute-done.35 = bf16[64,3584]{1,0:T(8,128)(2,1)S(1)} collective-permute-done((bf16[64,3584]{1,0:T(8,128)(2,1)S(1)}, bf16[64,3584]{1,0:T(8,128)(2,1)S(1)}, u32[]{:S(2)}, u32[]{:S(2)}) %collective-permute-start.35) | collective-permute-done | bytes 458784 | tf_op jit(solution)/shard_map/ppermute | solution.py:201
  207.7 3.4 %collective-permute-done.34 = bf16[64,3584]{1,0:T(8,128)(2,1)S(1)} collective-permute-done((bf16[64,3584]{1,0:T(8,128)(2,1)S(1)}, bf16[64,3584]{1,0:T(8,128)(2,1)S(1)}, u32[]{:S(2)}, u32[]{:S(2)}) %collective-permute-start.34) | collective-permute-done | bytes 458784 | tf_op jit(solution)/shard_map/ppermute | solution.py:207
  (125 shorter events, 83.1 us)
Async XLA Ops:
  5.4 12.6 %collective-permute-start.15 = (bf16[256,640]{1,0:T(8,128)(2,1)}, bf16[256,640]{1,0:T(8,128)(2,1)S(1)}, u32[]{:S(2)}, u32[]{:S(2)}) collective-permute-start(bf16[256,640]{1,0:T(8,128)(2,1)} %get-tuple-element.131), channel_id=1, source_target_pairs={{0,16},{8,24},{1,17},{9,25},{2,18},{10,26},{3,19},{11,27},{4,20},{... | collective-permute-start | bytes 983048 | tf_op jit(solution)/shard_map/ppermute | solution.py:665
  10.3 20.4 %collective-permute-start.17 = (bf16[512,640]{1,0:T(8,128)(2,1)}, bf16[512,640]{1,0:T(8,128)(2,1)}, u32[]{:S(2)}, u32[]{:S(2)}) collective-permute-start(bf16[512,640]{1,0:T(8,128)(2,1)} %get-tuple-element.133.refs_0_), channel_id=1, source_target_pairs={{0,8},{16,24},{1,9},{17,25},{2,10},{18,26},{3,11},{19,27},{4,12},{... | collective-permute-start | bytes 1966088 | tf_op jit(solution)/shard_map/ppermute | solution.py:666
  27.0 18.1 %collective-permute-start.21 = (bf16[640,512]{1,0:T(8,128)(2,1)S(1)}, bf16[640,512]{1,0:T(8,128)(2,1)S(1)}, u32[]{:S(2)}, u32[]{:S(2)}) collective-permute-start(bf16[640,512]{1,0:T(8,128)(2,1)S(1)} %get-tuple-element.137), channel_id=1, source_target_pairs={{0,16},{8,24},{16,0},{24,8},{1,17},{9,25},{17,1},{25,9},{2,18},{10... | collective-permute-start | bytes 1966088 | tf_op jit(solution)/shard_map/ppermute | solution.py:211
  29.9 74.6 %collective-permute-start.27 = (bf16[2688,512]{1,0:T(8,128)(2,1)}, bf16[2688,512]{1,0:T(8,128)(2,1)}, u32[]{:S(2)}, u32[]{:S(2)}) collective-permute-start(bf16[2688,512]{1,0:T(8,128)(2,1)} %get-tuple-element.149), channel_id=1, source_target_pairs={{0,8},{8,0},{16,24},{24,16},{1,9},{9,1},{17,25},{25,17},{2,10},{10... | collective-permute-start | bytes 8257544 | tf_op jit(solution)/shard_map/ppermute | solution.py:211
  45.9 62.5 %collective-permute-start.22 = (bf16[2688,512]{1,0:T(8,128)(2,1)}, bf16[2688,512]{1,0:T(8,128)(2,1)}, u32[]{:S(2)}, u32[]{:S(2)}) collective-permute-start(bf16[2688,512]{1,0:T(8,128)(2,1)} %get-tuple-element.149), channel_id=1, source_target_pairs={{0,16},{8,24},{16,0},{24,8},{1,17},{9,25},{17,1},{25,9},{2,18},{10... | collective-permute-start | bytes 8257544 | tf_op jit(solution)/shard_map/ppermute | solution.py:211
  52.5 13.5 %collective-permute-start.8 = (bf16[64,3584]{1,0:T(8,128)(2,1)S(1)}, bf16[64,3584]{1,0:T(8,128)(2,1)S(1)}, u32[]{:S(2)}, u32[]{:S(2)}) collective-permute-start(bf16[64,3584]{1,0:T(8,128)(2,1)S(1)} %get-tuple-element.49), channel_id=1, source_target_pairs={{0,1},{1,0},{2,3},{3,2},{4,5},{5,4},{6,7},{7,6},{8,9},{9,8},{10,11... | collective-permute-start | bytes 1376264 | tf_op jit(solution)/shard_map/cond/branch_1_fun/ppermute | solution.py:201
  54.1 21.7 %collective-permute-start.10 = (bf16[64,3584]{1,0:T(8,128)(2,1)S(1)}, bf16[64,3584]{1,0:T(8,128)(2,1)S(1)}, u32[]{:S(2)}, u32[]{:S(2)}) collective-permute-start(bf16[64,3584]{1,0:T(8,128)(2,1)S(1)} %get-tuple-element.51), channel_id=1, source_target_pairs={{0,1},{1,0},{2,3},{3,2},{4,5},{5,4},{6,7},{7,6},{8,9},{9,8},{10,11... | collective-permute-start | bytes 1376264 | tf_op jit(solution)/shard_map/cond/branch_1_fun/ppermute | solution.py:201
  66.1 11.3 %collective-permute-start.9 = (bf16[64,3584]{1,0:T(8,128)(2,1)S(1)}, bf16[64,3584]{1,0:T(8,128)(2,1)S(1)}, u32[]{:S(2)}, u32[]{:S(2)}) collective-permute-start(bf16[64,3584]{1,0:T(8,128)(2,1)S(1)} %add_convert_fusion.2), channel_id=1, source_target_pairs={{0,2},{1,3},{2,6},{3,7},{6,4},{7,5},{4,0},{5,1},{8,10},{9,11},{10,... | collective-permute-start | bytes 1376264 | tf_op jit(solution)/shard_map/cond/branch_1_fun/ppermute | solution.py:207
  67.8 17.9 %collective-permute-start.12 = (bf16[64,3584]{1,0:T(8,128)(2,1)S(1)}, bf16[64,3584]{1,0:T(8,128)(2,1)S(1)}, u32[]{:S(2)}, u32[]{:S(2)}) collective-permute-start(bf16[64,3584]{1,0:T(8,128)(2,1)S(1)} %get-tuple-element.53), channel_id=1, source_target_pairs={{0,1},{1,0},{2,3},{3,2},{4,5},{5,4},{6,7},{7,6},{8,9},{9,8},{10,11... | collective-permute-start | bytes 1376264 | tf_op jit(solution)/shard_map/cond/branch_1_fun/ppermute | solution.py:201
  78.4 15.9 %collective-permute-start.14 = (bf16[64,3584]{1,0:T(8,128)(2,1)S(1)}, bf16[64,3584]{1,0:T(8,128)(2,1)S(1)}, u32[]{:S(2)}, u32[]{:S(2)}) collective-permute-start(bf16[64,3584]{1,0:T(8,128)(2,1)S(1)} %get-tuple-element.55), channel_id=1, source_target_pairs={{0,1},{1,0},{2,3},{3,2},{4,5},{5,4},{6,7},{7,6},{8,9},{9,8},{10,11... | collective-permute-start | bytes 1376264 | tf_op jit(solution)/shard_map/cond/branch_1_fun/ppermute | solution.py:201
  108.4 56.1 %collective-permute-start.28 = (bf16[256,3584]{1,0:T(8,128)(2,1)S(1)}, bf16[256,3584]{1,0:T(8,128)(2,1)}, u32[]{:S(2)}, u32[]{:S(2)}) collective-permute-start(bf16[256,3584]{1,0:T(8,128)(2,1)S(1)} %bitcast.28), channel_id=1, source_target_pairs={{0,16},{8,24},{16,0},{24,8},{1,17},{9,25},{17,1},{25,9},{2,18},{10... | collective-permute-start | bytes 5505032 | tf_op jit(solution)/shard_map/ppermute | solution.py:211
  110.2 54.5 %collective-permute-start.29 = (bf16[256,3584]{1,0:T(8,128)(2,1)S(1)}, bf16[256,3584]{1,0:T(8,128)(2,1)}, u32[]{:S(2)}, u32[]{:S(2)}) collective-permute-start(bf16[256,3584]{1,0:T(8,128)(2,1)S(1)} %bitcast.29), channel_id=1, source_target_pairs={{0,8},{8,0},{16,24},{24,16},{1,9},{9,1},{17,25},{25,17},{2,10},{10... | collective-permute-start | bytes 5505032 | tf_op jit(solution)/shard_map/ppermute | solution.py:211
  110.2 41.0 %collective-permute-start.3 = (bf16[2688,512]{1,0:T(8,128)(2,1)}, bf16[2688,512]{1,0:T(8,128)(2,1)S(1)}, u32[]{:S(2)}, u32[]{:S(2)}) collective-permute-start(bf16[2688,512]{1,0:T(8,128)(2,1)} %get-tuple-element.69.refs_12_), channel_id=1, source_target_pairs={{0,8},{8,0},{16,24},{24,16},{1,9},{9,1},{17,25},{25,17},{2,10},{10... | collective-permute-start | bytes 8257544 | tf_op jit(solution)/shard_map/cond/branch_1_fun/ppermute | solution.py:211
  110.7 12.8 %collective-permute-start = (bf16[64,3712]{1,0:T(8,128)(2,1)S(1)}, bf16[64,3712]{1,0:T(8,128)(2,1)S(1)}, u32[]{:S(2)}, u32[]{:S(2)}) collective-permute-start(bf16[64,3712]{1,0:T(8,128)(2,1)S(1)} %get-tuple-element.60.refs_0_), channel_id=1, source_target_pairs={{0,1},{1,0},{2,3},{3,2},{4,5},{5,4},{6,7},{7,6},{8,9},{9,8},{10,11... | collective-permute-start | bytes 1425416 | tf_op jit(solution)/shard_map/cond/branch_1_fun/ppermute | solution.py:201
  112.2 13.4 %collective-permute-start.1 = (bf16[64,3712]{1,0:T(8,128)(2,1)S(1)}, bf16[64,3712]{1,0:T(8,128)(2,1)S(1)}, u32[]{:S(2)}, u32[]{:S(2)}) collective-permute-start(bf16[64,3712]{1,0:T(8,128)(2,1)S(1)} %get-tuple-element.60.refs_0_), channel_id=1, source_target_pairs={{0,2},{1,3},{2,6},{3,7},{6,4},{7,5},{4,0},{5,1},{8,10},{9,11},{10,... | collective-permute-start | bytes 1425416 | tf_op jit(solution)/shard_map/cond/branch_1_fun/ppermute | solution.py:207
  125.6 11.6 %collective-permute-start.2 = (bf16[64,3712]{1,0:T(8,128)(2,1)S(1)}, bf16[64,3712]{1,0:T(8,128)(2,1)S(1)}, u32[]{:S(2)}, u32[]{:S(2)}) collective-permute-start(bf16[64,3712]{1,0:T(8,128)(2,1)S(1)} %collective-permute-done.1.refs_2_), channel_id=1, source_target_pairs={{0,1},{1,0},{2,3},{3,2},{4,5},{5,4},{6,7},{7,6},{8,9},{9,8},{10,11... | collective-permute-start | bytes 1425416 | tf_op jit(solution)/shard_map/cond/branch_1_fun/ppermute | solution.py:201
  126.1 12.2 %collective-permute-start.4 = (bf16[64,3712]{1,0:T(8,128)(2,1)S(1)}, bf16[64,3712]{1,0:T(8,128)(2,1)S(1)}, u32[]{:S(2)}, u32[]{:S(2)}) collective-permute-start(bf16[64,3712]{1,0:T(8,128)(2,1)S(1)} %collective-permute-done.1.refs_2_), channel_id=1, source_target_pairs={{0,2},{1,3},{2,6},{3,7},{6,4},{7,5},{4,0},{5,1},{8,10},{9,11},{10,... | collective-permute-start | bytes 1425416 | tf_op jit(solution)/shard_map/cond/branch_1_fun/ppermute | solution.py:207
  138.3 11.3 %collective-permute-start.6 = (bf16[64,3712]{1,0:T(8,128)(2,1)S(1)}, bf16[64,3712]{1,0:T(8,128)(2,1)S(1)}, u32[]{:S(2)}, u32[]{:S(2)}) collective-permute-start(bf16[64,3712]{1,0:T(8,128)(2,1)S(1)} %collective-permute-done.4.refs_0_), channel_id=1, source_target_pairs={{0,2},{1,3},{2,6},{3,7},{6,4},{7,5},{4,0},{5,1},{8,10},{9,11},{10,... | collective-permute-start | bytes 1425416 | tf_op jit(solution)/shard_map/cond/branch_1_fun/ppermute | solution.py:207
  139.1 19.8 %collective-permute-start.5 = (bf16[64,3712]{1,0:T(8,128)(2,1)S(1)}, bf16[64,3712]{1,0:T(8,128)(2,1)S(1)}, u32[]{:S(2)}, u32[]{:S(2)}) collective-permute-start(bf16[64,3712]{1,0:T(8,128)(2,1)S(1)} %collective-permute-done.4.refs_0_), channel_id=1, source_target_pairs={{0,1},{1,0},{2,3},{3,2},{4,5},{5,4},{6,7},{7,6},{8,9},{9,8},{10,11... | collective-permute-start | bytes 1425416 | tf_op jit(solution)/shard_map/cond/branch_1_fun/ppermute | solution.py:201
  174.6 13.4 %collective-permute-start.31 = (bf16[64,3584]{1,0:T(8,128)(2,1)S(1)}, bf16[64,3584]{1,0:T(8,128)(2,1)S(1)}, u32[]{:S(2)}, u32[]{:S(2)}) collective-permute-start(bf16[64,3584]{1,0:T(8,128)(2,1)S(1)} %get-tuple-element.165), channel_id=1, source_target_pairs={{0,1},{1,0},{2,3},{3,2},{4,5},{5,4},{6,7},{7,6},{8,9},{9,8},{10,11... | collective-permute-start | bytes 1376264 | tf_op jit(solution)/shard_map/ppermute | solution.py:201
  176.2 21.7 %collective-permute-start.33 = (bf16[64,3584]{1,0:T(8,128)(2,1)S(1)}, bf16[64,3584]{1,0:T(8,128)(2,1)S(1)}, u32[]{:S(2)}, u32[]{:S(2)}) collective-permute-start(bf16[64,3584]{1,0:T(8,128)(2,1)S(1)} %get-tuple-element.167), channel_id=1, source_target_pairs={{0,1},{1,0},{2,3},{3,2},{4,5},{5,4},{6,7},{7,6},{8,9},{9,8},{10,11... | collective-permute-start | bytes 1376264 | tf_op jit(solution)/shard_map/ppermute | solution.py:201
  188.2 11.9 %collective-permute-start.32 = (bf16[64,3584]{1,0:T(8,128)(2,1)S(1)}, bf16[64,3584]{1,0:T(8,128)(2,1)S(1)}, u32[]{:S(2)}, u32[]{:S(2)}) collective-permute-start(bf16[64,3584]{1,0:T(8,128)(2,1)S(1)} %add_convert_fusion.6), channel_id=1, source_target_pairs={{0,2},{1,3},{2,6},{3,7},{6,4},{7,5},{4,0},{5,1},{8,10},{9,11},{10,... | collective-permute-start | bytes 1376264 | tf_op jit(solution)/shard_map/ppermute | solution.py:207
  191.6 16.1 %collective-permute-start.35 = (bf16[64,3584]{1,0:T(8,128)(2,1)S(1)}, bf16[64,3584]{1,0:T(8,128)(2,1)S(1)}, u32[]{:S(2)}, u32[]{:S(2)}) collective-permute-start(bf16[64,3584]{1,0:T(8,128)(2,1)S(1)} %get-tuple-element.169), channel_id=1, source_target_pairs={{0,1},{1,0},{2,3},{3,2},{4,5},{5,4},{6,7},{7,6},{8,9},{9,8},{10,11... | collective-permute-start | bytes 1376264 | tf_op jit(solution)/shard_map/ppermute | solution.py:201
  202.7 16.0 %collective-permute-start.37 = (bf16[64,3584]{1,0:T(8,128)(2,1)S(1)}, bf16[64,3584]{1,0:T(8,128)(2,1)S(1)}, u32[]{:S(2)}, u32[]{:S(2)}) collective-permute-start(bf16[64,3584]{1,0:T(8,128)(2,1)S(1)} %get-tuple-element.171), channel_id=1, source_target_pairs={{0,1},{1,0},{2,3},{3,2},{4,5},{5,4},{6,7},{7,6},{8,9},{9,8},{10,11... | collective-permute-start | bytes 1376264 | tf_op jit(solution)/shard_map/ppermute | solution.py:201
  (35 other events, 387.9 us)

commit v4 on v3

--- a/solution.py
+++ b/solution.py
@@ -16,7 +16,7 @@
 norm_eps = 1e-06
 masked_score = -1e30
 LOG2_E = math.log2(math.e)
-FIRST_ROWS = (256, 896)
+FIRST_ROWS = 960
 VMEM_BYTES = 14 * 1024 * 1024
 
 
@@ -224,15 +224,28 @@
     return lax.cond(taken, work, blank, *inputs)
 
 
-def reduce_exp(*blocks):
-    rows, across = len(blocks) // 2, {}
-    for step in list(range(1, rows)) + [0]:
-        across[step] = blocks[2 * step], swap_exp(blocks[2 * step + 1])
-    total = sum(term.astype(jnp.float32) for term in across[1])
-    for step in range(2, rows):
-        moved = ring_z(total.astype(jnp.bfloat16))
-        total = moved.astype(jnp.float32) + sum(term.astype(jnp.float32) for term in across[step])
-    return ring_z(total.astype(jnp.bfloat16)), *across[0]
+def reduce_exp(own, own_across, first, first_a, first_b, second, second_across, third, third_across):
+    def summed(*terms):
+        return sum(term.astype(jnp.float32) for term in terms).astype(jnp.bfloat16)
+
+    got_a, moved_b = swap_exp(first_a), ring_z(first_b)
+    total = summed(first, jnp.concatenate([got_a, jnp.zeros_like(first_b)], axis=1))
+    second_across = summed(second_across, jnp.concatenate([jnp.zeros_like(first_a), moved_b], axis=1))
+    got_second = swap_exp(second_across)
+    got_third = swap_exp(after(third_across, second_across))
+    total = summed(ring_z(total), second, got_second)
+    got_own = swap_exp(after(own_across, got_second))
+    total = summed(ring_z(total), third, got_third)
+    return ring_z(total), own, got_own
+
+
+def split_outs(count, rows, width):
+    half = width // 2
+    places = []
+    for at in range(count):
+        for columns in ((0, half), (half, width)) if at == 3 else ((0, width),):
+            places.append((at * rows, columns))
+    return places
 
 
 def norm_kernel(moved, mine, across, residual, gain, table, stream, out):
@@ -264,12 +277,10 @@
 
 
 def gather_exp(block):
-    found = []
-    for step in range(lax.axis_size("exp") // 2):
-        if step:
-            block = ring_z(after(block, found[-3]) if step > 1 else block)
-            found.append(block)
-        found.append(swap_exp(block))
+    found = [block, swap_exp(block)]
+    for step in range(2, lax.axis_size("exp") // 2):
+        block = ring_z(after(block, found[-3]) if len(found) > 2 else block)
+        found += [block, swap_exp(block)]
     return found
 
 
@@ -474,22 +485,32 @@
     )(here, q_nope, q_rope, *pieces, uv_weight)
 
 
-def project_kernel(order, values, weight, *outs):
+def project_kernel(order, values, weight, *outs, places):
     rows = outs[0].shape[0]
     picked = jnp.concatenate(
-        [values[pl.ds(pl.multiple_of(order[3 + at] * rows, rows), rows), :] for at in range(len(outs))], axis=0
+        [values[pl.ds(pl.multiple_of(order[3 + at] * rows, rows), rows), :] for at in range(values.shape[0] // rows)], axis=0
     )
     result = jnp.dot(picked, weight[...], preferred_element_type=jnp.float32).astype(outs[0].dtype)
-    for at, out in enumerate(outs):
-        out[...] = result[at * rows : (at + 1) * rows]
+    tile, step = weight.shape[1], pl.program_id(0)
+    for (first, (start, end)), out in zip(places, outs):
+
+        @pl.when((step >= start // tile) & (step < end // tile))
+        def _(first=first, out=out):
+            out[...] = result[first : first + rows]
 
 
 def project_blocks(here, values, weight, count):
     rows, inner = values.shape
     width = weight.shape[1]
     block, tile = rows // count, 896
+    places = split_outs(count, block, width)
+
+    def out_spec(columns):
+        first, last = columns[0] // tile, columns[1] // tile - 1
+        return pl.BlockSpec((block, tile), lambda n, s: (0, jnp.clip(n, first, last) - first))
+
     return pl.pallas_call(
-        project_kernel,
+        functools.partial(project_kernel, places=places),
         grid_spec=pltpu.PrefetchScalarGridSpec(
             num_scalar_prefetch=1,
             grid=(width // tile,),
@@ -497,9 +518,9 @@
                 pl.BlockSpec((rows, inner), lambda n, s: (0, 0)),
                 pl.BlockSpec((inner, tile), lambda n, s: (0, n)),
             ],
-            out_specs=[pl.BlockSpec((block, tile), lambda n, s: (0, n))] * count,
+            out_specs=[out_spec(columns) for _, columns in places],
         ),
-        out_shape=[pltpu.VMEM((block, width), jnp.bfloat16)] * count,
+        out_shape=[pltpu.VMEM((block, end - start), jnp.bfloat16) for _, (start, end) in places],
         compiler_params=pltpu.CompilerParams(vmem_limit_bytes=32 * 1024 * 1024),
         cost_estimate=pl.CostEstimate(
             flops=2 * rows * inner * width, bytes_accessed=2 * (inner + rows) * width, transcendentals=0
@@ -588,13 +609,13 @@
     )(here, *rows, *operands)
 
 
-def down_kernel(*refs, pieces, parts, tile):
+def down_kernel(*refs, pieces, parts, tile, places):
     hidden, scales, weights = refs[:pieces], refs[pieces : 2 * pieces], refs[2 * pieces : 2 * pieces + parts]
     outs = refs[2 * pieces + parts :]
     rows, units = outs[0].shape[0], weights[0].shape[0]
     each = hidden[0].shape[0]
     for piece in range(pieces):
-        for at in range(outs[0].shape[1] // tile):
+        for at in range(weights[0].shape[1] // tile):
             columns = slice(at * tile, (at + 1) * tile)
             total = 0.0
             for part, weight in enumerate(weights):
@@ -604,20 +625,22 @@
                     preferred_element_type=jnp.float32,
                 )
             total = (total * scales[piece][...]).astype(outs[0].dtype)
-            for block in range(each // rows):
-                outs[piece * (each // rows) + block][:, columns] = total[block * rows : (block + 1) * rows]
+            for (first, (start, end)), out in zip(places, outs):
+                if piece * each <= first < (piece + 1) * each and start <= at * tile < end:
+                    out[:, at * tile - start : (at + 1) * tile - start] = total[first - piece * each :][:rows]
 
 
 def down_blocks(hidden, scales, weights, count):
-    pieces, parts, tile = len(hidden), len(weights), 512
+    pieces, parts, tile = len(hidden), len(weights), 896
     each, inner = hidden[0].shape
     units, width = weights[0].shape
     whole = pl.BlockSpec(memory_space=pltpu.VMEM)
+    places = split_outs(count, pieces * each // count, width)
     return pl.pallas_call(
-        functools.partial(down_kernel, pieces=pieces, parts=parts, tile=tile),
+        functools.partial(down_kernel, pieces=pieces, parts=parts, tile=tile, places=places),
         in_specs=[whole] * (2 * pieces + parts),
-        out_specs=[whole] * count,
-        out_shape=[pltpu.VMEM((pieces * each // count, width), jnp.bfloat16)] * count,
+        out_specs=[whole] * len(places),
+        out_shape=[pltpu.VMEM((pieces * each // count, end - start), jnp.bfloat16) for _, (start, end) in places],
         compiler_params=pltpu.CompilerParams(vmem_limit_bytes=VMEM_BYTES),
         cost_estimate=pl.CostEstimate(
             flops=2 * pieces * each * inner * width,
@@ -661,45 +684,45 @@
     here = positions(exp_devices)
 
     own, sent = pack_keys(here, latent, k_rope, doc_ids)
-    table = route_table(expert_ids, gate_levels, bin_ids, exp_devices)
-    far_a = lax.ppermute(sent, "ctx", [(c, c + 2) for c in range(ctx_devices - 2)])
-    near_even = lax.ppermute(own, "ctx", [(c, c + 1) for c in range(0, ctx_devices, 2)])
+    far = lax.ppermute(sent, "ctx", [(c, c + 2) for c in range(ctx_devices - 2)])
     flat_q = q_nope.reshape(block_len, head_count * lat_width)
     w_gate, w_up, w_down = gate_weight[0], up_weight[0], down_weight[0]
-    part_a, part_b = FIRST_ROWS
-    own_both = join_weights(w_gate, w_up, (part_a, part_b, w_gate.shape[0]))
-    far_b = swap_exp(after(far_a, (flat_q, own_both, table)))
-    near_a = lax.ppermute(far_a, "ctx", [(3, 2)])
-    near_b = lax.ppermute(far_b, "ctx", [(3, 2)])
-
-    both_a = swap_ctx(after(own_both[0], far_a), 2)
+    own_both = join_weights(w_gate, w_up, (FIRST_ROWS, w_gate.shape[0]))
+    far = after(far, own_both)
+    both_a = swap_ctx(after(own_both[0], far), 2)
+
+    def attend_and_project(here, flat_q, q_rope, own, far, uv_weight, out_weight, expert_ids, gate_levels, bin_ids):
+        far_across = swap_exp(far)
+        near = lax.ppermute(own, "ctx", [(c, c + 1) for c in range(0, ctx_devices, 2)])
+        table = route_table(expert_ids, gate_levels, bin_ids, exp_devices)
+        early = after(far, (flat_q, table))
+        key_pieces = [own, near, *[lax.ppermute(piece, "ctx", [(3, 2)]) for piece in (early, far_across)], far, far_across]
+        values = attend(here, flat_q, q_rope, key_pieces, uv_weight, rope_width)
+        return project_blocks(here, values, out_weight, exp_devices), table
+
     there_both = [swap_ctx(piece, 1) for piece in own_both]
-    own = after(own, both_a)
-    both_b = swap_ctx(after(own_both[1], own), 2)
-    key_pieces = [own, near_even, near_a, near_b, far_a, far_b]
-    values = attend(here, flat_q, q_rope, key_pieces, uv_weight, rope_width)
-    values = after(values, both_b)
-    both_c = swap_ctx(after(own_both[2], values), 2)
-    partial = project_blocks(here, values, out_weight, exp_devices)
+    inputs = here, flat_q, q_rope, own, far, uv_weight, out_weight, expert_ids, gate_levels, bin_ids
+    partial, table = after(one_step(attend_and_project, *inputs), both_a)
+    both_c = swap_ctx(after(own_both[1], (partial[0], both_a)), 2)
+
     def sum_and_norm(partial, *rest):
         return norm_rows(*reduce_exp(*partial), *rest)
 
-    swapped = [swap_ctx(both_a, 1), swap_ctx(both_b, 1)]
-    stream_state, block = after(
-        one_step(sum_and_norm, partial, residual_in, norm_gain, table), (both_c, swapped, there_both)
-    )
-    far_down = swap_ctx(after(w_down, block), 2)
-
-    def gather_and_hide(block, here, own_both, there_both, far_both, swapped):
-        weights = [own_both, there_both, far_both, [*swapped, swap_ctx(far_both[-1], 1)]]
-        found = [block, *gather_exp(block)]
+    stream_state, block = one_step(sum_and_norm, partial, residual_in, norm_gain, table)
+    swapped = swap_ctx(both_a, 1)
+    across, back = after(one_step(lambda value: (swap_exp(value), ring_z(value)), block), (both_c, swapped))
+    far_down = swap_ctx(after(w_down, (both_c, back)), 2)
+
+    def gather_and_hide(block, across, back, here, own_both, there_both, far_both, swapped):
+        weights = [own_both, there_both, far_both, [swapped, swap_ctx(far_both[-1], 1)]]
+        found = [block, across, *gather_exp(back)]
         half = len(found) // 2
         *first, held = hidden_rows(here, found[:half], weights, exp_devices)
         last = hidden_rows(here, found[half:], held, exp_devices)
         return [*zip(first, last)]
 
     hidden, bins, scales = after(
-        one_step(gather_and_hide, block, here, own_both, there_both, [both_a, both_b, both_c], swapped), far_down
+        one_step(gather_and_hide, block, across, back, here, own_both, there_both, [both_a, both_c], swapped), far_down
     )
     downs = [w_down, swap_ctx(w_down, 1), far_down, swap_ctx(after(far_down, hidden), 1)]
     expert_out = down_blocks(hidden, scales, downs, exp_devices)

time: 223 us -> 218 us (0.978)
  starting transfers between devices: 50.8 us -> 42.4 us
  waiting for transfers between devices: 125 us -> 121 us
  Pallas kernels: 34.6 us -> 37.9 us
  local copies, waits for them, and re-layouts: 8.52 us -> 10.9 us
    ppermute x14 -> x11, waiting for transfers between devices: 23.4 us -> 9.61 us  [swap_ctx(): lax.ppermute(value, 'ctx', [(c, c ^ bit) for c in range(lax.axis_size('ct...]
    ppermute x9 -> x11, waiting for transfers between devices: 27.9 us -> 41.5 us  [ring_z(): lax.ppermute(value, 'exp', [(2 * a + x, 2 * b + x) for a, b in steps for...]
    ppermute x13, waiting for transfers between devices: 73.2 us -> 67.6 us  [swap_exp(): lax.ppermute(value, 'exp', [(e, e ^ bit) for e in range(lax.axis_size('ex...]
    ppermute x13, starting transfers between devices: 16.7 us -> 12.5 us  [swap_exp(): lax.ppermute(value, 'exp', [(e, e ^ bit) for e in range(lax.axis_size('ex...]
    cond x2 -> x14, local copies, waits for them, and re-layouts: 0.01 us -> 2.52 us
    ppermute x14 -> x11, starting transfers between devices: 11.2 us -> 9.21 us  [swap_ctx(): lax.ppermute(value, 'ctx', [(c, c ^ bit) for c in range(lax.axis_size('ct...]
    ppermute x9 -> x11, starting transfers between devices: 14.3 us -> 13 us  [ring_z(): lax.ppermute(value, 'exp', [(2 * a + x, 2 * b + x) for a, b in steps for...]
    unnamed x41 -> x23, local copies, waits for them, and re-layouts: 8.38 us -> 7.98 us
  transfers between devices with their start and end apart: 40 -> 39, of which waited for: 27 -> 25; matrix products, arithmetic and copies ran while one was open for 1% -> 2% of each run, Pallas kernels for 12% -> 14%
where the time goes in v4:
time: 218 us; the launch traced here: 217 us
  waiting for transfers between devices  121 us (56%)
  starting transfers between devices  42.4 us (19%)
  Pallas kernels  37.9 us (17%)
  local copies, waits for them, and re-layouts  10.9 us (5%)
  other arithmetic  3.64 us (2%)
    ppermute x13, waiting for transfers between devices, swap_exp(): lax.ppermute(value, 'exp', [(e, e ^ bit) for e in range(lax.axis_size('ex...  67.6 us
    ppermute x11, waiting for transfers between devices, ring_z(): lax.ppermute(value, 'exp', [(2 * a + x, 2 * b + x) for a, b in steps for...  41.5 us
    pallas_call x2, Pallas kernels, hidden_rows(): pl.pallas_call(functools.partial(hidden_kernel, blocks=len(rows), counts=...  13.6 us
    ppermute x11, starting transfers between devices, ring_z(): lax.ppermute(value, 'exp', [(2 * a + x, 2 * b + x) for a, b in steps for...  13 us
    ppermute x13, starting transfers between devices, swap_exp(): lax.ppermute(value, 'exp', [(e, e ^ bit) for e in range(lax.axis_size('ex...  12.5 us
    ppermute x11, waiting for transfers between devices, swap_ctx(): lax.ppermute(value, 'ctx', [(c, c ^ bit) for c in range(lax.axis_size('ct...  9.61 us
    ppermute x11, starting transfers between devices, swap_ctx(): lax.ppermute(value, 'ctx', [(c, c ^ bit) for c in range(lax.axis_size('ct...  9.21 us
    pallas_call x1, Pallas kernels, attend(): pl.pallas_call(functools.partial(attend_kernel, heads=heads, rope_width=r...  8.27 us
  transfers between devices with their start and end apart: 39, of which 25 were waited for; matrix products, arithmetic and copies ran while one was open for 2% of the time, Pallas kernels for 14%

profile of v4, /device:TPU:0, one launch (start us, length us, event | category | flops | bytes accessed | tf_op | source)
XLA Modules:
  0.0 217.1 jit_solution(12426566792393439205)
XLA Ops:
  5.2 4.9 %collective-permute-start.20 = (bf16[256,640]{1,0:T(8,128)(2,1)S(1)}, bf16[256,640]{1,0:T(8,128)(2,1)S(1)}, u32[]{:S(2)}, u32[]{:S(2)}) collective-permute-start(bf16[256,640]{1,0:T(8,128)(2,1)S(1)} %get-tuple-element.189), channel_id=1, source_target_pairs={{0,16},{8,24},{1,17},{9,25},{2,18},{10,26},{3,19},{11,27},{4,20},{... | collective-permute-start | bytes 983048 | tf_op jit(solution)/shard_map/ppermute | solution.py:687
  20.2 23.1 %conditional.4 = (bf16[64,3584]{1,0:T(8,128)(2,1)S(1)}, bf16[64,3584]{1,0:T(8,128)(2,1)S(1)}, bf16[64,3584]{1,0:T(8,128)(2,1)S(1)}, bf16[64,1792]{1,0:T(8,128)(2...) conditional(s32[]{:T(128)} %convert_element_type.102, () %tuple.60, ...), branch_computations={%region_0.1_spmd, %region_1.2_spmd} | conditional | flops 4563402752 | bytes 30421344 | solution.py:224
  26.2 4.1 %collective-permute-done.2.refs_5_ = bf16[256,640]{1,0:T(8,128)(2,1)S(1)} collective-permute-done((bf16[256,640]{1,0:T(8,128)(2,1)}, bf16[256,640]{1,0:T(8,128)(2,1)S(1)}, u32[]{:S(2)}, u32[]{:S(2)}) %collective-permute-start.2) | collective-permute-done | bytes 327712 | tf_op jit(solution)/shard_map/cond/branch_1_fun/ppermute | solution.py:201
  31.0 8.3 %attend.1.values = bf16[512,256]{1,0:T(8,128)(2,1)S(1)} custom-call(s32[11]{0:T(128)S(1)} %get-tuple-element.71.scalars.order, bf16[512,1024]{1,0:T(8,128)(2,1)S(1)} %bitcast.26, bf16[512,128]{1,0:T(8,128)(2,1)} %get-tuple-element.259.q_rope, bf16[512,640]{1,0:T(8,128)(2,1)S(1)} %copy-done.13, bf16[512,640]{1,0:T(8,128)(2,1)S(1)} %collective-permute-done.refs_1_, ...), custom_call_target="tpu_custom_call" | custom-call | flops 3623878656 | bytes 3932160 | tf_op jit(solution)/shard_map/cond/branch_1_fun/attend/pallas_call | solution.py:459
  39.3 4.1 %project.1 = (bf16[64,3584]{1,0:T(8,128)(2,1)S(1)}, bf16[64,3584]{1,0:T(8,128)(2,1)S(1)}, bf16[64,3584]{1,0:T(8,128)(2,1)S(1)}, bf16[64,1792]{1,0:T(8,128)(2,1)S...) custom-call(s32[11]{0:T(128)S(1)} %get-tuple-element.71.scalars.orde, ...), custom_call_target="tpu_custom_call" | custom-call | flops 939524096 | bytes 5505024 | tf_op jit(solution)/shard_map/cond/branch_1_fun/project/pallas_call | solution.py:512
  46.5 49.4 %conditional.5 = (f32[64,3584]{1,0:T(8,128)}, bf16[64,3712]{1,0:T(8,128)(2,1)}, bf16[64,3712]{1,0:T(8,128)(2,1)S(1)}) conditional(s32[]{:T(128)} %convert_element_type.102, () %tuple.59, (bf16[64,3584]{1,0:T(8,128)(2,1)S(1)}, bf16[64,1792]{1,0:T(8,128)(2,1)S(1)}, bf16[64,3584]{1,0:T(8,128)(2,1)S(1)}, bf16[64,3584]{1,0:T(8,128)(2,1)S(1)}, ...), branch_computations={%region_2.3_spmd, %region_3.4_spmd} | conditional | flops 6422528 | bytes 24834420 | solution.py:224
  49.6 6.0 %collective-permute-done.14 = bf16[64,1792]{1,0:T(8,128)(2,1)S(1)} collective-permute-done((bf16[64,1792]{1,0:T(8,128)(2,1)}, bf16[64,1792]{1,0:T(8,128)(2,1)S(1)}, u32[]{:S(2)}, u32[]{:S(2)}) %collective-permute-start.14) | collective-permute-done | bytes 229408 | tf_op jit(solution)/shard_map/cond/branch_1_fun/ppermute | solution.py:207
  60.0 9.2 %collective-permute-done.15 = bf16[64,3584]{1,0:T(8,128)(2,1)S(1)} collective-permute-done((bf16[64,3584]{1,0:T(8,128)(2,1)S(1)}, bf16[64,3584]{1,0:T(8,128)(2,1)S(1)}, u32[]{:S(2)}, u32[]{:S(2)}) %collective-permute-start.15) | collective-permute-done | bytes 458784 | tf_op jit(solution)/shard_map/cond/branch_1_fun/ppermute | solution.py:201
  72.2 6.8 %collective-permute-done.17 = bf16[64,3584]{1,0:T(8,128)(2,1)S(1)} collective-permute-done((bf16[64,3584]{1,0:T(8,128)(2,1)S(1)}, bf16[64,3584]{1,0:T(8,128)(2,1)S(1)}, u32[]{:S(2)}, u32[]{:S(2)}) %collective-permute-start.17) | collective-permute-done | bytes 458784 | tf_op jit(solution)/shard_map/cond/branch_1_fun/ppermute | solution.py:201
  83.2 4.3 %collective-permute-done.19.across = bf16[64,3584]{1,0:T(8,128)(2,1)S(1)} collective-permute-done((bf16[64,3584]{1,0:T(8,128)(2,1)S(1)}, bf16[64,3584]{1,0:T(8,128)(2,1)S(1)}, u32[]{:S(2)}, u32[]{:S(2)}) %collective-permute-start.19) | collective-permute-done | bytes 458784 | tf_op jit(solution)/shard_map/cond/branch_1_fun/ppermute | solution.py:201
  87.6 5.8 %collective-permute-done.18.moved = bf16[64,3584]{1,0:T(8,128)(2,1)S(1)} collective-permute-done((bf16[64,3584]{1,0:T(8,128)(2,1)S(1)}, bf16[64,3584]{1,0:T(8,128)(2,1)S(1)}, u32[]{:S(2)}, u32[]{:S(2)}) %collective-permute-start.18) | collective-permute-done | bytes 458784 | tf_op jit(solution)/shard_map/cond/branch_1_fun/ppermute | solution.py:207
  95.9 14.5 %conditional.6 = (bf16[64,3712]{1,0:T(8,128)(2,1)}, bf16[64,3712]{1,0:T(8,128)(2,1)}) conditional(s32[]{:T(128)} %convert_element_type.102, () %tuple.67, bf16[64,3712]{1,0:T(8,128)(2,1)S(1)} %get-tuple-element.215), branch_computations={%region_4.5_spmd, %region_5.6_spmd} | conditional | bytes 3801184 | solution.py:224
  97.2 12.1 %collective-permute-done.4 = bf16[64,3712]{1,0:T(8,128)(2,1)} collective-permute-done((bf16[64,3712]{1,0:T(8,128)(2,1)S(1)}, bf16[64,3712]{1,0:T(8,128)(2,1)}, u32[]{:S(2)}, u32[]{:S(2)}) %collective-permute-start.4) | collective-permute-done | bytes 475168 | tf_op jit(solution)/shard_map/cond/branch_1_fun/ppermute | solution.py:201
  115.5 44.9 %conditional.7 = (bf16[256,1024]{1,0:T(8,128)(2,1)S(1)}, bf16[256,1024]{1,0:T(8,128)(2,1)S(1)}, f32[16,128]{1,0:T(8,128)S(1)}, f32[16,128]{1,0:T(8,128)S(1)}, f3...) conditional(s32[]{:T(128)} %convert_element_type.102, () %tuple.66, (bf16[64,3712]{1,0:T(8,128)(2,1)}, ...), branch_computations={%region_6.7_spmd, %region_7.8_spmd} | conditional | flops 7516192768 | bytes 53281260 | solution.py:224
  117.8 11.2 %collective-permute-done.6.refs_3_ = bf16[64,3712]{1,0:T(8,128)(2,1)S(1)} collective-permute-done((bf16[64,3712]{1,0:T(8,128)(2,1)}, bf16[64,3712]{1,0:T(8,128)(2,1)S(1)}, u32[]{:S(2)}, u32[]{:S(2)}) %collective-permute-start.6) | collective-permute-done | bytes 475168 | tf_op jit(solution)/shard_map/cond/branch_1_fun/ppermute | solution.py:201
  132.5 11.5 %collective-permute-done.10.refs_2_ = bf16[64,3712]{1,0:T(8,128)(2,1)S(1)} collective-permute-done((bf16[64,3712]{1,0:T(8,128)(2,1)S(1)}, bf16[64,3712]{1,0:T(8,128)(2,1)S(1)}, u32[]{:S(2)}, u32[]{:S(2)}) %collective-permute-start.10) | collective-permute-done | bytes 475168 | tf_op jit(solution)/shard_map/cond/branch_1_fun/ppermute | solution.py:207
  144.5 8.6 %hidden.2 = (bf16[256,1024]{1,0:T(8,128)(2,1)S(1)}, f32[16,128]{1,0:T(8,128)S(1)}, f32[256,1]{1,0:T(8,128)S(1)}, bf16[4,3584,512]{2,1,0:T(8,128)(2,1)S(1)}) custom-call(s32[11]{0:T(128)S(1)} %get-tuple-element.107.here, bf16[64,3712]{1,0:T(8,128)(2,1)} %get-tuple-element.108.refs_0_, bf16[64,3712]{1,0:T(8,128)(2,1)} %get-tuple-element.109.refs_1_, ...), custom_call_target="tpu_custom_call" | custom-call | flops 3758096384 | bytes 16515072 | tf_op jit(solution)/shard_map/cond/branch_1_fun/hidden/pallas_call | solution.py:588
  155.1 5.0 %hidden.3 = (bf16[256,1024]{1,0:T(8,128)(2,1)S(1)}, f32[16,128]{1,0:T(8,128)S(1)}, f32[256,1]{1,0:T(8,128)S(1)}) custom-call(s32[11]{0:T(128)} %copy-done.8, bf16[64,3712]{1,0:T(8,128)(2,1)S(1)} %collective-permute-done.8.refs_0_, bf16[64,3712]{1,0:T(8,128)(2,1)S(1)} %collective-permute-done.9.refs_1_, bf16[64,3712]{1,0:T(8,128)(2,1)S(1)} %collective-permute-done.10.refs_2_, ...), custom_call_target="tpu_custom_call" | custom-call | flops 3758096384 | bytes 16515072 | tf_op jit(solution)/shard_map/cond/branch_1_fun/hidden/pallas_call | solution.py:588
  160.4 4.0 %collective-permute-done.28.refs_7_ = bf16[256,3584]{1,0:T(8,128)(2,1)S(1)} collective-permute-done((bf16[256,3584]{1,0:T(8,128)(2,1)}, bf16[256,3584]{1,0:T(8,128)(2,1)S(1)}, u32[]{:S(2)}, u32[]{:S(2)}) %collective-permute-start.28) | collective-permute-done | bytes 1835040 | tf_op jit(solution)/shard_map/ppermute | solution.py:211
  164.4 6.6 %down.1 = (bf16[64,3584]{1,0:T(8,128)(2,1)S(1)}, bf16[64,3584]{1,0:T(8,128)(2,1)S(1)}, bf16[64,3584]{1,0:T(8,128)(2,1)S(1)}, bf16[64,1792]{1,0:T(8,128)(2,1)S(1)...) custom-call(bf16[256,1024]{1,0:T(8,128)(2,1)S(1)} %get-tuple-element, ...), custom_call_target="tpu_custom_call" | custom-call | flops 3758096384 | bytes 11010048 | tf_op jit(solution)/shard_map/down/pallas_call | solution.py:639
  173.6 5.9 %collective-permute-done.31 = bf16[64,1792]{1,0:T(8,128)(2,1)S(1)} collective-permute-done((bf16[64,1792]{1,0:T(8,128)(2,1)S(1)}, bf16[64,1792]{1,0:T(8,128)(2,1)S(1)}, u32[]{:S(2)}, u32[]{:S(2)}) %collective-permute-start.31) | collective-permute-done | bytes 229408 | tf_op jit(solution)/shard_map/ppermute | solution.py:207
  183.2 10.0 %collective-permute-done.32 = bf16[64,3584]{1,0:T(8,128)(2,1)S(1)} collective-permute-done((bf16[64,3584]{1,0:T(8,128)(2,1)S(1)}, bf16[64,3584]{1,0:T(8,128)(2,1)S(1)}, u32[]{:S(2)}, u32[]{:S(2)}) %collective-permute-start.32) | collective-permute-done | bytes 458784 | tf_op jit(solution)/shard_map/ppermute | solution.py:201
  195.2 7.8 %collective-permute-done.34 = bf16[64,3584]{1,0:T(8,128)(2,1)S(1)} collective-permute-done((bf16[64,3584]{1,0:T(8,128)(2,1)S(1)}, bf16[64,3584]{1,0:T(8,128)(2,1)S(1)}, u32[]{:S(2)}, u32[]{:S(2)}) %collective-permute-start.34) | collective-permute-done | bytes 458784 | tf_op jit(solution)/shard_map/ppermute | solution.py:201
  211.6 3.3 %collective-permute-done.35 = bf16[64,3584]{1,0:T(8,128)(2,1)S(1)} collective-permute-done((bf16[64,3584]{1,0:T(8,128)(2,1)S(1)}, bf16[64,3584]{1,0:T(8,128)(2,1)S(1)}, u32[]{:S(2)}, u32[]{:S(2)}) %collective-permute-start.35) | collective-permute-done | bytes 458784 | tf_op jit(solution)/shard_map/ppermute | solution.py:207
  (124 shorter events, 76.2 us)
Async XLA Ops:
  5.2 11.8 %collective-permute-start.20 = (bf16[256,640]{1,0:T(8,128)(2,1)S(1)}, bf16[256,640]{1,0:T(8,128)(2,1)S(1)}, u32[]{:S(2)}, u32[]{:S(2)}) collective-permute-start(bf16[256,640]{1,0:T(8,128)(2,1)S(1)} %get-tuple-element.189), channel_id=1, source_target_pairs={{0,16},{8,24},{1,17},{9,25},{2,18},{10,26},{3,19},{11,27},{4,20},{... | collective-permute-start | bytes 983048 | tf_op jit(solution)/shard_map/ppermute | solution.py:687
  17.7 25.6 %collective-permute-start.21 = (bf16[960,512]{1,0:T(8,128)(2,1)}, bf16[960,512]{1,0:T(8,128)(2,1)}, u32[]{:S(2)}, u32[]{:S(2)}) collective-permute-start(bf16[960,512]{1,0:T(8,128)(2,1)} %get-tuple-element.203), channel_id=1, source_target_pairs={{0,16},{8,24},{16,0},{24,8},{1,17},{9,25},{17,1},{25,9},{2,18},{10... | collective-permute-start | bytes 2949128 | tf_op jit(solution)/shard_map/ppermute | solution.py:211
  43.4 67.0 %collective-permute-start.22 = (bf16[2624,512]{1,0:T(8,128)(2,1)}, bf16[2624,512]{1,0:T(8,128)(2,1)}, u32[]{:S(2)}, u32[]{:S(2)}) collective-permute-start(bf16[2624,512]{1,0:T(8,128)(2,1)} %get-tuple-element.218), channel_id=1, source_target_pairs={{0,16},{8,24},{16,0},{24,8},{1,17},{9,25},{17,1},{25,9},{2,18},{10... | collective-permute-start | bytes 8060936 | tf_op jit(solution)/shard_map/ppermute | solution.py:211
  46.5 63.9 %collective-permute-start.23 = (bf16[960,512]{1,0:T(8,128)(2,1)}, bf16[960,512]{1,0:T(8,128)(2,1)}, u32[]{:S(2)}, u32[]{:S(2)}) collective-permute-start(bf16[960,512]{1,0:T(8,128)(2,1)} %collective-permute-done.21), channel_id=1, source_target_pairs={{0,8},{8,0},{16,24},{24,16},{1,9},{9,1},{17,25},{25,17},{2,10},{10... | collective-permute-start | bytes 2949128 | tf_op jit(solution)/shard_map/ppermute | solution.py:211
  55.7 13.5 %collective-permute-start.15 = (bf16[64,3584]{1,0:T(8,128)(2,1)S(1)}, bf16[64,3584]{1,0:T(8,128)(2,1)S(1)}, u32[]{:S(2)}, u32[]{:S(2)}) collective-permute-start(bf16[64,3584]{1,0:T(8,128)(2,1)S(1)} %add_convert_fusion.2), channel_id=1, source_target_pairs={{0,1},{1,0},{2,3},{3,2},{4,5},{5,4},{6,7},{7,6},{8,9},{9,8},{10,11... | collective-permute-start | bytes 1376264 | tf_op jit(solution)/shard_map/cond/branch_1_fun/ppermute | solution.py:201
  57.3 12.8 %collective-permute-start.13 = (bf16[64,3584]{1,0:T(8,128)(2,1)S(1)}, bf16[64,3584]{1,0:T(8,128)(2,1)S(1)}, u32[]{:S(2)}, u32[]{:S(2)}) collective-permute-start(bf16[64,3584]{1,0:T(8,128)(2,1)S(1)} %add_convert_fusion.3), channel_id=1, source_target_pairs={{0,2},{1,3},{2,6},{3,7},{6,4},{7,5},{4,0},{5,1},{8,10},{9,11},{10,... | collective-permute-start | bytes 1376264 | tf_op jit(solution)/shard_map/cond/branch_1_fun/ppermute | solution.py:207
  58.5 20.5 %collective-permute-start.17 = (bf16[64,3584]{1,0:T(8,128)(2,1)S(1)}, bf16[64,3584]{1,0:T(8,128)(2,1)S(1)}, u32[]{:S(2)}, u32[]{:S(2)}) collective-permute-start(bf16[64,3584]{1,0:T(8,128)(2,1)S(1)} %get-tuple-element.98), channel_id=1, source_target_pairs={{0,1},{1,0},{2,3},{3,2},{4,5},{5,4},{6,7},{7,6},{8,9},{9,8},{10,11... | collective-permute-start | bytes 1376264 | tf_op jit(solution)/shard_map/cond/branch_1_fun/ppermute | solution.py:201
  70.3 11.9 %collective-permute-start.16 = (bf16[64,3584]{1,0:T(8,128)(2,1)S(1)}, bf16[64,3584]{1,0:T(8,128)(2,1)S(1)}, u32[]{:S(2)}, u32[]{:S(2)}) collective-permute-start(bf16[64,3584]{1,0:T(8,128)(2,1)S(1)} %add_convert_fusion.1), channel_id=1, source_target_pairs={{0,2},{1,3},{2,6},{3,7},{6,4},{7,5},{4,0},{5,1},{8,10},{9,11},{10,... | collective-permute-start | bytes 1376264 | tf_op jit(solution)/shard_map/cond/branch_1_fun/ppermute | solution.py:207
  71.2 16.4 %collective-permute-start.19 = (bf16[64,3584]{1,0:T(8,128)(2,1)S(1)}, bf16[64,3584]{1,0:T(8,128)(2,1)S(1)}, u32[]{:S(2)}, u32[]{:S(2)}) collective-permute-start(bf16[64,3584]{1,0:T(8,128)(2,1)S(1)} %get-tuple-element.101), channel_id=1, source_target_pairs={{0,1},{1,0},{2,3},{3,2},{4,5},{5,4},{6,7},{7,6},{8,9},{9,8},{10,11... | collective-permute-start | bytes 1376264 | tf_op jit(solution)/shard_map/cond/branch_1_fun/ppermute | solution.py:201
  95.9 18.0 %collective-permute-start.25 = (bf16[2624,512]{1,0:T(8,128)(2,1)}, bf16[2624,512]{1,0:T(8,128)(2,1)S(1)}, u32[]{:S(2)}, u32[]{:S(2)}) collective-permute-start(bf16[2624,512]{1,0:T(8,128)(2,1)} %get-tuple-element.218), channel_id=1, source_target_pairs={{0,8},{8,0},{16,24},{24,16},{1,9},{9,1},{17,25},{25,17},{2,10},{10... | collective-permute-start | bytes 8060936 | tf_op jit(solution)/shard_map/ppermute | solution.py:211
  95.9 13.4 %collective-permute-start.4 = (bf16[64,3712]{1,0:T(8,128)(2,1)S(1)}, bf16[64,3712]{1,0:T(8,128)(2,1)}, u32[]{:S(2)}, u32[]{:S(2)}) collective-permute-start(bf16[64,3712]{1,0:T(8,128)(2,1)S(1)} %param.5), channel_id=1, source_target_pairs={{0,1},{1,0},{2,3},{3,2},{4,5},{5,4},{6,7},{7,6},{8,9},{9,8},{10,11... | collective-permute-start | bytes 1425416 | tf_op jit(solution)/shard_map/cond/branch_1_fun/ppermute | solution.py:201
  96.4 14.0 %collective-permute-start.5 = (bf16[64,3712]{1,0:T(8,128)(2,1)S(1)}, bf16[64,3712]{1,0:T(8,128)(2,1)}, u32[]{:S(2)}, u32[]{:S(2)}) collective-permute-start(bf16[64,3712]{1,0:T(8,128)(2,1)S(1)} %param.5), channel_id=1, source_target_pairs={{0,2},{1,3},{2,6},{3,7},{6,4},{7,5},{4,0},{5,1},{8,10},{9,11},{10,... | collective-permute-start | bytes 1425416 | tf_op jit(solution)/shard_map/cond/branch_1_fun/ppermute | solution.py:207
  110.4 49.9 %collective-permute-start.26 = (bf16[256,3584]{1,0:T(8,128)(2,1)}, bf16[256,3584]{1,0:T(8,128)(2,1)}, u32[]{:S(2)}, u32[]{:S(2)}) collective-permute-start(bf16[256,3584]{1,0:T(8,128)(2,1)} %bitcast.28), channel_id=1, source_target_pairs={{0,16},{8,24},{16,0},{24,8},{1,17},{9,25},{17,1},{25,9},{2,18},{10... | collective-permute-start | bytes 5505032 | tf_op jit(solution)/shard_map/ppermute | solution.py:211
  110.5 49.9 %collective-permute-start.27 = (bf16[256,3584]{1,0:T(8,128)(2,1)}, bf16[256,3584]{1,0:T(8,128)(2,1)}, u32[]{:S(2)}, u32[]{:S(2)}) collective-permute-start(bf16[256,3584]{1,0:T(8,128)(2,1)} %bitcast.29), channel_id=1, source_target_pairs={{0,8},{8,0},{16,24},{24,16},{1,9},{9,1},{17,25},{25,17},{2,10},{10... | collective-permute-start | bytes 5505032 | tf_op jit(solution)/shard_map/ppermute | solution.py:211
  115.5 29.1 %collective-permute-start.7 = (bf16[2624,512]{1,0:T(8,128)(2,1)}, bf16[2624,512]{1,0:T(8,128)(2,1)S(1)}, u32[]{:S(2)}, u32[]{:S(2)}) collective-permute-start(bf16[2624,512]{1,0:T(8,128)(2,1)} %get-tuple-element.116.refs_9_), channel_id=1, source_target_pairs={{0,8},{8,0},{16,24},{24,16},{1,9},{9,1},{17,25},{25,17},{2,10},{10... | collective-permute-start | bytes 8060936 | tf_op jit(solution)/shard_map/cond/branch_1_fun/ppermute | solution.py:211
  115.6 13.4 %collective-permute-start.6 = (bf16[64,3712]{1,0:T(8,128)(2,1)}, bf16[64,3712]{1,0:T(8,128)(2,1)S(1)}, u32[]{:S(2)}, u32[]{:S(2)}) collective-permute-start(bf16[64,3712]{1,0:T(8,128)(2,1)} %get-tuple-element.110.refs_2_), channel_id=1, source_target_pairs={{0,1},{1,0},{2,3},{3,2},{4,5},{5,4},{6,7},{7,6},{8,9},{9,8},{10,11... | collective-permute-start | bytes 1425416 | tf_op jit(solution)/shard_map/cond/branch_1_fun/ppermute | solution.py:201
  117.1 14.0 %collective-permute-start.8 = (bf16[64,3712]{1,0:T(8,128)(2,1)}, bf16[64,3712]{1,0:T(8,128)(2,1)S(1)}, u32[]{:S(2)}, u32[]{:S(2)}) collective-permute-start(bf16[64,3712]{1,0:T(8,128)(2,1)} %get-tuple-element.110.refs_2_), channel_id=1, source_target_pairs={{0,2},{1,3},{2,6},{3,7},{6,4},{7,5},{4,0},{5,1},{8,10},{9,11},{10,... | collective-permute-start | bytes 1425416 | tf_op jit(solution)/shard_map/cond/branch_1_fun/ppermute | solution.py:207
  131.1 12.9 %collective-permute-start.10 = (bf16[64,3712]{1,0:T(8,128)(2,1)S(1)}, bf16[64,3712]{1,0:T(8,128)(2,1)S(1)}, u32[]{:S(2)}, u32[]{:S(2)}) collective-permute-start(bf16[64,3712]{1,0:T(8,128)(2,1)S(1)} %collective-permute-done.8.refs_0_), channel_id=1, source_target_pairs={{0,2},{1,3},{2,6},{3,7},{6,4},{7,5},{4,0},{5,1},{8,10},{9,11},{10,... | collective-permute-start | bytes 1425416 | tf_op jit(solution)/shard_map/cond/branch_1_fun/ppermute | solution.py:207
  132.0 21.2 %collective-permute-start.9 = (bf16[64,3712]{1,0:T(8,128)(2,1)S(1)}, bf16[64,3712]{1,0:T(8,128)(2,1)S(1)}, u32[]{:S(2)}, u32[]{:S(2)}) collective-permute-start(bf16[64,3712]{1,0:T(8,128)(2,1)S(1)} %collective-permute-done.8.refs_0_), channel_id=1, source_target_pairs={{0,1},{1,0},{2,3},{3,2},{4,5},{5,4},{6,7},{7,6},{8,9},{9,8},{10,11... | collective-permute-start | bytes 1425416 | tf_op jit(solution)/shard_map/cond/branch_1_fun/ppermute | solution.py:201
  179.7 13.5 %collective-permute-start.32 = (bf16[64,3584]{1,0:T(8,128)(2,1)S(1)}, bf16[64,3584]{1,0:T(8,128)(2,1)S(1)}, u32[]{:S(2)}, u32[]{:S(2)}) collective-permute-start(bf16[64,3584]{1,0:T(8,128)(2,1)S(1)} %add_convert_fusion.7), channel_id=1, source_target_pairs={{0,1},{1,0},{2,3},{3,2},{4,5},{5,4},{6,7},{7,6},{8,9},{9,8},{10,11... | collective-permute-start | bytes 1376264 | tf_op jit(solution)/shard_map/ppermute | solution.py:201
  180.5 12.6 %collective-permute-start.30 = (bf16[64,3584]{1,0:T(8,128)(2,1)S(1)}, bf16[64,3584]{1,0:T(8,128)(2,1)S(1)}, u32[]{:S(2)}, u32[]{:S(2)}) collective-permute-start(bf16[64,3584]{1,0:T(8,128)(2,1)S(1)} %add_convert_fusion.8), channel_id=1, source_target_pairs={{0,2},{1,3},{2,6},{3,7},{6,4},{7,5},{4,0},{5,1},{8,10},{9,11},{10,... | collective-permute-start | bytes 1376264 | tf_op jit(solution)/shard_map/ppermute | solution.py:207
  182.7 20.3 %collective-permute-start.34 = (bf16[64,3584]{1,0:T(8,128)(2,1)S(1)}, bf16[64,3584]{1,0:T(8,128)(2,1)S(1)}, u32[]{:S(2)}, u32[]{:S(2)}) collective-permute-start(bf16[64,3584]{1,0:T(8,128)(2,1)S(1)} %get-tuple-element.241), channel_id=1, source_target_pairs={{0,1},{1,0},{2,3},{3,2},{4,5},{5,4},{6,7},{7,6},{8,9},{9,8},{10,11... | collective-permute-start | bytes 1376264 | tf_op jit(solution)/shard_map/ppermute | solution.py:201
  193.4 11.2 %collective-permute-start.33 = (bf16[64,3584]{1,0:T(8,128)(2,1)S(1)}, bf16[64,3584]{1,0:T(8,128)(2,1)S(1)}, u32[]{:S(2)}, u32[]{:S(2)}) collective-permute-start(bf16[64,3584]{1,0:T(8,128)(2,1)S(1)} %add_convert_fusion.6), channel_id=1, source_target_pairs={{0,2},{1,3},{2,6},{3,7},{6,4},{7,5},{4,0},{5,1},{8,10},{9,11},{10,... | collective-permute-start | bytes 1376264 | tf_op jit(solution)/shard_map/ppermute | solution.py:207
  194.6 17.0 %collective-permute-start.36 = (bf16[64,3584]{1,0:T(8,128)(2,1)S(1)}, bf16[64,3584]{1,0:T(8,128)(2,1)S(1)}, u32[]{:S(2)}, u32[]{:S(2)}) collective-permute-start(bf16[64,3584]{1,0:T(8,128)(2,1)S(1)} %get-tuple-element.244), channel_id=1, source_target_pairs={{0,1},{1,0},{2,3},{3,2},{4,5},{5,4},{6,7},{7,6},{8,9},{9,8},{10,11... | collective-permute-start | bytes 1376264 | tf_op jit(solution)/shard_map/ppermute | solution.py:201
  (32 other events, 304.7 us)

commit v5 on v4

--- a/solution.py
+++ b/solution.py
@@ -267,7 +267,7 @@
         in_specs=[whole] * 6,
         out_specs=[whole] * 2,
         out_shape=[
-            jax.ShapeDtypeStruct((rows, width), jnp.float32),
+            pltpu.VMEM((rows, width), jnp.float32),
             pltpu.VMEM((rows, width + table.shape[1]), jnp.bfloat16),
         ],
         compiler_params=pltpu.CompilerParams(vmem_limit_bytes=VMEM_BYTES),
@@ -709,12 +709,20 @@
         return norm_rows(*reduce_exp(*partial), *rest)
 
     stream_state, block = one_step(sum_and_norm, partial, residual_in, norm_gain, table)
-    swapped = swap_ctx(both_a, 1)
-    across, back = after(one_step(lambda value: (swap_exp(value), ring_z(value)), block), (both_c, swapped))
+    across, back, there_c, near_down = after(
+        one_step(
+            lambda value, *weights: (swap_exp(value), ring_z(value), *[swap_ctx(weight, 1) for weight in weights]),
+            block,
+            own_both[1],
+            w_down,
+        ),
+        both_c,
+    )
+    there_both = [there_both[0], there_c]
     far_down = swap_ctx(after(w_down, (both_c, back)), 2)
 
-    def gather_and_hide(block, across, back, here, own_both, there_both, far_both, swapped):
-        weights = [own_both, there_both, far_both, [swapped, swap_ctx(far_both[-1], 1)]]
+    def gather_and_hide(block, across, back, here, own_both, there_both, far_both):
+        weights = [own_both, there_both, far_both, [swap_ctx(piece, 1) for piece in far_both]]
         found = [block, across, *gather_exp(back)]
         half = len(found) // 2
         *first, held = hidden_rows(here, found[:half], weights, exp_devices)
@@ -722,9 +730,9 @@
         return [*zip(first, last)]
 
     hidden, bins, scales = after(
-        one_step(gather_and_hide, block, across, back, here, own_both, there_both, [both_a, both_c], swapped), far_down
-    )
-    downs = [w_down, swap_ctx(w_down, 1), far_down, swap_ctx(after(far_down, hidden), 1)]
+        one_step(gather_and_hide, block, across, back, here, own_both, there_both, [both_a, both_c]), far_down
+    )
+    downs = [w_down, near_down, far_down, swap_ctx(after(far_down, hidden), 1)]
     expert_out = down_blocks(hidden, scales, downs, exp_devices)
     mixture = reduce_exp(*expert_out)
     layer_out = (stream_state + sum(term.astype(jnp.float32) for term in mixture)).astype(jnp.bfloat16)

time: 218 us -> 212 us (0.972)
  local copies, waits for them, and re-layouts: 10.9 us -> 7.85 us
    ppermute x11, waiting for transfers between devices: 41.5 us -> 37.1 us  [ring_z(): lax.ppermute(value, 'exp', [(2 * a + x, 2 * b + x) for a, b in steps for...]
    unnamed x23 -> x21, local copies, waits for them, and re-layouts: 7.98 us -> 6.44 us
  transfers between devices with their start and end apart: 39 -> 39, of which waited for: 25 -> 27; matrix products, arithmetic and copies ran while one was open for 2% -> 1% of each run, Pallas kernels for 14% -> 14%
where the time goes in v5:
time: 212 us; the launch traced here: 211 us
  waiting for transfers between devices  119 us (56%)
  starting transfers between devices  43 us (20%)
  Pallas kernels  37.4 us (18%)
  local copies, waits for them, and re-layouts  7.85 us (4%)
  other arithmetic  2.47 us (1%)
    ppermute x13, waiting for transfers between devices, swap_exp(): lax.ppermute(value, 'exp', [(e, e ^ bit) for e in range(lax.axis_size('ex...  69 us
    ppermute x11, waiting for transfers between devices, ring_z(): lax.ppermute(value, 'exp', [(2 * a + x, 2 * b + x) for a, b in steps for...  37.1 us
    ppermute x11, starting transfers between devices, ring_z(): lax.ppermute(value, 'exp', [(2 * a + x, 2 * b + x) for a, b in steps for...  14.3 us
    pallas_call x2, Pallas kernels, hidden_rows(): pl.pallas_call(functools.partial(hidden_kernel, blocks=len(rows), counts=...  13.4 us
    ppermute x13, starting transfers between devices, swap_exp(): lax.ppermute(value, 'exp', [(e, e ^ bit) for e in range(lax.axis_size('ex...  12.4 us
    ppermute x11, waiting for transfers between devices, swap_ctx(): lax.ppermute(value, 'ctx', [(c, c ^ bit) for c in range(lax.axis_size('ct...  11.1 us
    pallas_call x1, Pallas kernels, attend(): pl.pallas_call(functools.partial(attend_kernel, heads=heads, rope_width=r...  8.98 us
    ppermute x11, starting transfers between devices, swap_ctx(): lax.ppermute(value, 'ctx', [(c, c ^ bit) for c in range(lax.axis_size('ct...  8.57 us
  transfers between devices with their start and end apart: 39, of which 27 were waited for; matrix products, arithmetic and copies ran while one was open for 1% of the time, Pallas kernels for 14%

profile of v5, /device:TPU:0, one launch (start us, length us, event | category | flops | bytes accessed | tf_op | source)
XLA Modules:
  0.0 211.4 jit_solution(9741695298253508663)
XLA Ops:
  5.2 4.9 %collective-permute-start.23 = (bf16[256,640]{1,0:T(8,128)(2,1)S(1)}, bf16[256,640]{1,0:T(8,128)(2,1)S(1)}, u32[]{:S(2)}, u32[]{:S(2)}) collective-permute-start(bf16[256,640]{1,0:T(8,128)(2,1)S(1)} %get-tuple-element.192), channel_id=1, source_target_pairs={{0,16},{8,24},{1,17},{9,25},{2,18},{10,26},{3,19},{11,27},{4,20},{... | collective-permute-start | bytes 983048 | tf_op jit(solution)/shard_map/ppermute | solution.py:687
  20.3 24.6 %conditional.4 = (bf16[64,3584]{1,0:T(8,128)(2,1)}, bf16[64,3584]{1,0:T(8,128)(2,1)}, bf16[64,3584]{1,0:T(8,128)(2,1)S(1)}, bf16[64,1792]{1,0:T(8,128)(2,1)S(1)}...) conditional(s32[]{:T(128)} %convert_element_type.102, () %tuple.55, ...), branch_computations={%region_0.1_spmd, %region_1.2_spmd} | conditional | flops 4563402752 | bytes 27799876 | solution.py:224
  25.0 5.3 %collective-permute-done.2.refs_5_ = bf16[256,640]{1,0:T(8,128)(2,1)S(1)} collective-permute-done((bf16[256,640]{1,0:T(8,128)(2,1)}, bf16[256,640]{1,0:T(8,128)(2,1)S(1)}, u32[]{:S(2)}, u32[]{:S(2)}) %collective-permute-start.2) | collective-permute-done | bytes 327712 | tf_op jit(solution)/shard_map/cond/branch_1_fun/ppermute | solution.py:201
  31.0 9.0 %attend.1.values = bf16[512,256]{1,0:T(8,128)(2,1)S(1)} custom-call(s32[11]{0:T(128)S(1)} %get-tuple-element.71.scalars.order, bf16[512,1024]{1,0:T(8,128)(2,1)S(1)} %bitcast.26, bf16[512,128]{1,0:T(8,128)(2,1)S(1)} %copy-done.14, bf16[512,640]{1,0:T(8,128)(2,1)} %get-tuple-element.74.refs_0_, bf16[512,640]{1,0:T(8,128)(2,1)S(1)} %collective-permute-done.refs_1_, ...), custom_call_target="tpu_custom_call" | custom-call | flops 3623878656 | bytes 3932160 | tf_op jit(solution)/shard_map/cond/branch_1_fun/attend/pallas_call | solution.py:459
  40.0 4.0 %project.1 = (bf16[64,3584]{1,0:T(8,128)(2,1)S(1)}, bf16[64,3584]{1,0:T(8,128)(2,1)}, bf16[64,3584]{1,0:T(8,128)(2,1)S(1)}, bf16[64,1792]{1,0:T(8,128)(2,1)S(1)}...) custom-call(s32[11]{0:T(128)S(1)} %get-tuple-element.71.scalars.orde, ...), custom_call_target="tpu_custom_call" | custom-call | flops 939524096 | bytes 5505024 | tf_op jit(solution)/shard_map/cond/branch_1_fun/project/pallas_call | solution.py:512
  47.9 44.3 %conditional.5 = ((f32[64,3584]{1,0:T(8,128)S(1)}, bf16[64,3712]{1,0:T(8,128)(2,1)S(1)})) conditional(s32[]{:T(128)} %convert_element_type.102, () %tuple.54, (bf16[64,3584]{1,0:T(8,128)(2,1)S(1)}, bf16[64,1792]{1,0:T(8,128)(2,1)S(1)}, bf16[64,3584]{1,0:T(8,128)(2,1)S(1)}, bf16[64,3584]{1,0:T(8,128)(2,1)S(1)}, bf16[64,1792]{1,0:T(8,128)(2,1)S(1)}, ...), branch_computations={%region_2.3_spmd, %region_3.4_spmd} | conditional | flops 6422528 | bytes 25719168 | solution.py:224
  51.0 5.2 %collective-permute-done.17 = bf16[64,1792]{1,0:T(8,128)(2,1)S(1)} collective-permute-done((bf16[64,1792]{1,0:T(8,128)(2,1)S(1)}, bf16[64,1792]{1,0:T(8,128)(2,1)S(1)}, u32[]{:S(2)}, u32[]{:S(2)}) %collective-permute-start.17) | collective-permute-done | bytes 229408 | tf_op jit(solution)/shard_map/cond/branch_1_fun/ppermute | solution.py:207
  61.2 8.6 %collective-permute-done.18 = bf16[64,3584]{1,0:T(8,128)(2,1)S(1)} collective-permute-done((bf16[64,3584]{1,0:T(8,128)(2,1)S(1)}, bf16[64,3584]{1,0:T(8,128)(2,1)S(1)}, u32[]{:S(2)}, u32[]{:S(2)}) %collective-permute-start.18) | collective-permute-done | bytes 458784 | tf_op jit(solution)/shard_map/cond/branch_1_fun/ppermute | solution.py:201
  72.3 7.3 %collective-permute-done.20 = bf16[64,3584]{1,0:T(8,128)(2,1)S(1)} collective-permute-done((bf16[64,3584]{1,0:T(8,128)(2,1)}, bf16[64,3584]{1,0:T(8,128)(2,1)S(1)}, u32[]{:S(2)}, u32[]{:S(2)}) %collective-permute-start.20) | collective-permute-done | bytes 458784 | tf_op jit(solution)/shard_map/cond/branch_1_fun/ppermute | solution.py:201
  82.3 5.1 %collective-permute-done.22.across = bf16[64,3584]{1,0:T(8,128)(2,1)S(1)} collective-permute-done((bf16[64,3584]{1,0:T(8,128)(2,1)}, bf16[64,3584]{1,0:T(8,128)(2,1)S(1)}, u32[]{:S(2)}, u32[]{:S(2)}) %collective-permute-start.22) | collective-permute-done | bytes 458784 | tf_op jit(solution)/shard_map/cond/branch_1_fun/ppermute | solution.py:201
  87.4 4.3 %collective-permute-done.21.moved = bf16[64,3584]{1,0:T(8,128)(2,1)S(1)} collective-permute-done((bf16[64,3584]{1,0:T(8,128)(2,1)S(1)}, bf16[64,3584]{1,0:T(8,128)(2,1)S(1)}, u32[]{:S(2)}, u32[]{:S(2)}) %collective-permute-start.21) | collective-permute-done | bytes 458784 | tf_op jit(solution)/shard_map/cond/branch_1_fun/ppermute | solution.py:207
  92.2 14.5 %conditional.6 = (bf16[64,3712]{1,0:T(8,128)(2,1)}, bf16[64,3712]{1,0:T(8,128)(2,1)}, bf16[2624,512]{1,0:T(8,128)(2,1)}, bf16[256,3584]{1,0:T(8,128)(2,1)}) conditional(s32[]{:T(128)} %convert_element_type.102, () %tuple.62, (bf16[64,3712]{1,0:T(8,128)(2,1)S(1)}, bf16[2624,512]{1,0:T(8,128)(2,1)}, bf16[256,3584]{1,0:T(8,128)(2,1)}) %tuple.91), branch_computations={%region_4.5_spmd, %region_5.6_spmd} | conditional | bytes 21889216 | solution.py:224
  93.6 12.2 %collective-permute-done.4 = bf16[64,3712]{1,0:T(8,128)(2,1)} collective-permute-done((bf16[64,3712]{1,0:T(8,128)(2,1)S(1)}, bf16[64,3712]{1,0:T(8,128)(2,1)}, u32[]{:S(2)}, u32[]{:S(2)}) %collective-permute-start.4) | collective-permute-done | bytes 475168 | tf_op jit(solution)/shard_map/cond/branch_1_fun/ppermute | solution.py:201
  111.3 44.7 %conditional.7 = (bf16[256,1024]{1,0:T(8,128)(2,1)S(1)}, bf16[256,1024]{1,0:T(8,128)(2,1)S(1)}, f32[16,128]{1,0:T(8,128)S(1)}, f32[16,128]{1,0:T(8,128)S(1)}, f3...) conditional(s32[]{:T(128)} %convert_element_type.102, () %tuple.61, (bf16[64,3712]{1,0:T(8,128)(2,1)}, ...), branch_computations={%region_6.7_spmd, %region_7.8_spmd} | conditional | flops 7516192768 | bytes 57213256 | solution.py:224
  114.6 10.3 %collective-permute-done.8.refs_3_ = bf16[64,3712]{1,0:T(8,128)(2,1)S(1)} collective-permute-done((bf16[64,3712]{1,0:T(8,128)(2,1)}, bf16[64,3712]{1,0:T(8,128)(2,1)S(1)}, u32[]{:S(2)}, u32[]{:S(2)}) %collective-permute-start.8) | collective-permute-done | bytes 475168 | tf_op jit(solution)/shard_map/cond/branch_1_fun/ppermute | solution.py:201
  128.4 11.5 %collective-permute-done.13.refs_2_ = bf16[64,3712]{1,0:T(8,128)(2,1)S(1)} collective-permute-done((bf16[64,3712]{1,0:T(8,128)(2,1)S(1)}, bf16[64,3712]{1,0:T(8,128)(2,1)S(1)}, u32[]{:S(2)}, u32[]{:S(2)}) %collective-permute-start.13) | collective-permute-done | bytes 475168 | tf_op jit(solution)/shard_map/cond/branch_1_fun/ppermute | solution.py:207
  140.4 8.5 %hidden.2 = (bf16[256,1024]{1,0:T(8,128)(2,1)S(1)}, f32[16,128]{1,0:T(8,128)S(1)}, f32[256,1]{1,0:T(8,128)S(1)}, bf16[4,3584,512]{2,1,0:T(8,128)(2,1)S(1)}) custom-call(s32[11]{0:T(128)S(1)} %get-tuple-element.108.here, bf16[64,3712]{1,0:T(8,128)(2,1)S(1)} %get-tuple-element.109.refs_0_, bf16[64,3712]{1,0:T(8,128)(2,1)} %get-tuple-element.110.refs_1_, ...), custom_call_target="tpu_custom_call" | custom-call | flops 3758096384 | bytes 16515072 | tf_op jit(solution)/shard_map/cond/branch_1_fun/hidden/pallas_call | solution.py:588
  151.0 4.9 %hidden.3 = (bf16[256,1024]{1,0:T(8,128)(2,1)S(1)}, f32[16,128]{1,0:T(8,128)S(1)}, f32[256,1]{1,0:T(8,128)S(1)}) custom-call(s32[11]{0:T(128)S(1)} %get-tuple-element.108.here, bf16[64,3712]{1,0:T(8,128)(2,1)S(1)} %collective-permute-done.11.refs_0_, bf16[64,3712]{1,0:T(8,128)(2,1)S(1)} %collective-permute-done.12.refs_1_, ...), custom_call_target="tpu_custom_call" | custom-call | flops 3758096384 | bytes 16515072 | tf_op jit(solution)/shard_map/cond/branch_1_fun/hidden/pallas_call | solution.py:588
  156.2 3.8 %collective-permute-done.28.refs_7_ = bf16[256,3584]{1,0:T(8,128)(2,1)S(1)} collective-permute-done((bf16[256,3584]{1,0:T(8,128)(2,1)S(1)}, bf16[256,3584]{1,0:T(8,128)(2,1)S(1)}, u32[]{:S(2)}, u32[]{:S(2)}) %collective-permute-start.28) | collective-permute-done | bytes 1835040 | tf_op jit(solution)/shard_map/ppermute | solution.py:211
  159.9 6.6 %down.1 = (bf16[64,3584]{1,0:T(8,128)(2,1)S(1)}, bf16[64,3584]{1,0:T(8,128)(2,1)}, bf16[64,3584]{1,0:T(8,128)(2,1)S(1)}, bf16[64,1792]{1,0:T(8,128)(2,1)S(1)}, b...) custom-call(bf16[256,1024]{1,0:T(8,128)(2,1)S(1)} %get-tuple-element, ...), custom_call_target="tpu_custom_call" | custom-call | flops 3758096384 | bytes 11010048 | tf_op jit(solution)/shard_map/down/pallas_call | solution.py:639
  169.2 6.0 %collective-permute-done.31 = bf16[64,1792]{1,0:T(8,128)(2,1)S(1)} collective-permute-done((bf16[64,1792]{1,0:T(8,128)(2,1)S(1)}, bf16[64,1792]{1,0:T(8,128)(2,1)S(1)}, u32[]{:S(2)}, u32[]{:S(2)}) %collective-permute-start.31) | collective-permute-done | bytes 229408 | tf_op jit(solution)/shard_map/ppermute | solution.py:207
  178.7 10.0 %collective-permute-done.32 = bf16[64,3584]{1,0:T(8,128)(2,1)S(1)} collective-permute-done((bf16[64,3584]{1,0:T(8,128)(2,1)S(1)}, bf16[64,3584]{1,0:T(8,128)(2,1)S(1)}, u32[]{:S(2)}, u32[]{:S(2)}) %collective-permute-start.32) | collective-permute-done | bytes 458784 | tf_op jit(solution)/shard_map/ppermute | solution.py:201
  190.7 7.8 %collective-permute-done.34 = bf16[64,3584]{1,0:T(8,128)(2,1)S(1)} collective-permute-done((bf16[64,3584]{1,0:T(8,128)(2,1)S(1)}, bf16[64,3584]{1,0:T(8,128)(2,1)S(1)}, u32[]{:S(2)}, u32[]{:S(2)}) %collective-permute-start.34) | collective-permute-done | bytes 458784 | tf_op jit(solution)/shard_map/ppermute | solution.py:201
  206.7 3.7 %collective-permute-done.35 = bf16[64,3584]{1,0:T(8,128)(2,1)S(1)} collective-permute-done((bf16[64,3584]{1,0:T(8,128)(2,1)S(1)}, bf16[64,3584]{1,0:T(8,128)(2,1)S(1)}, u32[]{:S(2)}, u32[]{:S(2)}) %collective-permute-start.35) | collective-permute-done | bytes 458784 | tf_op jit(solution)/shard_map/ppermute | solution.py:207
  (119 shorter events, 71.0 us)
Async XLA Ops:
  5.2 11.8 %collective-permute-start.23 = (bf16[256,640]{1,0:T(8,128)(2,1)S(1)}, bf16[256,640]{1,0:T(8,128)(2,1)S(1)}, u32[]{:S(2)}, u32[]{:S(2)}) collective-permute-start(bf16[256,640]{1,0:T(8,128)(2,1)S(1)} %get-tuple-element.192), channel_id=1, source_target_pairs={{0,16},{8,24},{1,17},{9,25},{2,18},{10,26},{3,19},{11,27},{4,20},{... | collective-permute-start | bytes 983048 | tf_op jit(solution)/shard_map/ppermute | solution.py:687
  17.8 27.1 %collective-permute-start.24 = (bf16[960,512]{1,0:T(8,128)(2,1)}, bf16[960,512]{1,0:T(8,128)(2,1)}, u32[]{:S(2)}, u32[]{:S(2)}) collective-permute-start(bf16[960,512]{1,0:T(8,128)(2,1)} %get-tuple-element.206), channel_id=1, source_target_pairs={{0,16},{8,24},{16,0},{24,8},{1,17},{9,25},{17,1},{25,9},{2,18},{10... | collective-permute-start | bytes 2949128 | tf_op jit(solution)/shard_map/ppermute | solution.py:211
  44.8 62.0 %collective-permute-start.25 = (bf16[2624,512]{1,0:T(8,128)(2,1)}, bf16[2624,512]{1,0:T(8,128)(2,1)}, u32[]{:S(2)}, u32[]{:S(2)}) collective-permute-start(bf16[2624,512]{1,0:T(8,128)(2,1)} %get-tuple-element.223), channel_id=1, source_target_pairs={{0,16},{8,24},{16,0},{24,8},{1,17},{9,25},{17,1},{25,9},{2,18},{10... | collective-permute-start | bytes 8060936 | tf_op jit(solution)/shard_map/ppermute | solution.py:211
  56.3 13.5 %collective-permute-start.18 = (bf16[64,3584]{1,0:T(8,128)(2,1)S(1)}, bf16[64,3584]{1,0:T(8,128)(2,1)S(1)}, u32[]{:S(2)}, u32[]{:S(2)}) collective-permute-start(bf16[64,3584]{1,0:T(8,128)(2,1)S(1)} %add_convert_fusion.2), channel_id=1, source_target_pairs={{0,1},{1,0},{2,3},{3,2},{4,5},{5,4},{6,7},{7,6},{8,9},{9,8},{10,11... | collective-permute-start | bytes 1376264 | tf_op jit(solution)/shard_map/cond/branch_1_fun/ppermute | solution.py:201
  57.9 12.1 %collective-permute-start.16 = (bf16[64,3584]{1,0:T(8,128)(2,1)S(1)}, bf16[64,3584]{1,0:T(8,128)(2,1)S(1)}, u32[]{:S(2)}, u32[]{:S(2)}) collective-permute-start(bf16[64,3584]{1,0:T(8,128)(2,1)S(1)} %add_convert_fusion.3), channel_id=1, source_target_pairs={{0,2},{1,3},{2,6},{3,7},{6,4},{7,5},{4,0},{5,1},{8,10},{9,11},{10,... | collective-permute-start | bytes 1376264 | tf_op jit(solution)/shard_map/cond/branch_1_fun/ppermute | solution.py:207
  59.7 19.9 %collective-permute-start.20 = (bf16[64,3584]{1,0:T(8,128)(2,1)}, bf16[64,3584]{1,0:T(8,128)(2,1)S(1)}, u32[]{:S(2)}, u32[]{:S(2)}) collective-permute-start(bf16[64,3584]{1,0:T(8,128)(2,1)} %get-tuple-element.98), channel_id=1, source_target_pairs={{0,1},{1,0},{2,3},{3,2},{4,5},{5,4},{6,7},{7,6},{8,9},{9,8},{10,11... | collective-permute-start | bytes 1376264 | tf_op jit(solution)/shard_map/cond/branch_1_fun/ppermute | solution.py:201
  70.2 11.2 %collective-permute-start.19 = (bf16[64,3584]{1,0:T(8,128)(2,1)S(1)}, bf16[64,3584]{1,0:T(8,128)(2,1)S(1)}, u32[]{:S(2)}, u32[]{:S(2)}) collective-permute-start(bf16[64,3584]{1,0:T(8,128)(2,1)S(1)} %add_convert_fusion.1), channel_id=1, source_target_pairs={{0,2},{1,3},{2,6},{3,7},{6,4},{7,5},{4,0},{5,1},{8,10},{9,11},{10,... | collective-permute-start | bytes 1376264 | tf_op jit(solution)/shard_map/cond/branch_1_fun/ppermute | solution.py:207
  71.0 16.4 %collective-permute-start.22 = (bf16[64,3584]{1,0:T(8,128)(2,1)}, bf16[64,3584]{1,0:T(8,128)(2,1)S(1)}, u32[]{:S(2)}, u32[]{:S(2)}) collective-permute-start(bf16[64,3584]{1,0:T(8,128)(2,1)} %get-tuple-element.101), channel_id=1, source_target_pairs={{0,1},{1,0},{2,3},{3,2},{4,5},{5,4},{6,7},{7,6},{8,9},{9,8},{10,11... | collective-permute-start | bytes 1376264 | tf_op jit(solution)/shard_map/cond/branch_1_fun/ppermute | solution.py:201
  92.3 14.4 %collective-permute-start.6 = (bf16[2624,512]{1,0:T(8,128)(2,1)}, bf16[2624,512]{1,0:T(8,128)(2,1)}, u32[]{:S(2)}, u32[]{:S(2)}) collective-permute-start(bf16[2624,512]{1,0:T(8,128)(2,1)} %get-tuple-element.106), channel_id=1, source_target_pairs={{0,8},{8,0},{16,24},{24,16},{1,9},{9,1},{17,25},{25,17},{2,10},{10... | collective-permute-start | bytes 8060936 | tf_op jit(solution)/shard_map/cond/branch_1_fun/ppermute | solution.py:211
  92.3 14.4 %collective-permute-start.7 = (bf16[256,3584]{1,0:T(8,128)(2,1)}, bf16[256,3584]{1,0:T(8,128)(2,1)}, u32[]{:S(2)}, u32[]{:S(2)}) collective-permute-start(bf16[256,3584]{1,0:T(8,128)(2,1)} %get-tuple-element.107), channel_id=1, source_target_pairs={{0,8},{8,0},{16,24},{24,16},{1,9},{9,1},{17,25},{25,17},{2,10},{10... | collective-permute-start | bytes 5505032 | tf_op jit(solution)/shard_map/cond/branch_1_fun/ppermute | solution.py:211
  92.8 13.0 %collective-permute-start.4 = (bf16[64,3712]{1,0:T(8,128)(2,1)S(1)}, bf16[64,3712]{1,0:T(8,128)(2,1)}, u32[]{:S(2)}, u32[]{:S(2)}) collective-permute-start(bf16[64,3712]{1,0:T(8,128)(2,1)S(1)} %get-tuple-element.105), channel_id=1, source_target_pairs={{0,1},{1,0},{2,3},{3,2},{4,5},{5,4},{6,7},{7,6},{8,9},{9,8},{10,11... | collective-permute-start | bytes 1425416 | tf_op jit(solution)/shard_map/cond/branch_1_fun/ppermute | solution.py:201
  92.8 13.9 %collective-permute-start.5 = (bf16[64,3712]{1,0:T(8,128)(2,1)S(1)}, bf16[64,3712]{1,0:T(8,128)(2,1)}, u32[]{:S(2)}, u32[]{:S(2)}) collective-permute-start(bf16[64,3712]{1,0:T(8,128)(2,1)S(1)} %get-tuple-element.105), channel_id=1, source_target_pairs={{0,2},{1,3},{2,6},{3,7},{6,4},{7,5},{4,0},{5,1},{8,10},{9,11},{10,... | collective-permute-start | bytes 1425416 | tf_op jit(solution)/shard_map/cond/branch_1_fun/ppermute | solution.py:207
  106.8 49.3 %collective-permute-start.27 = (bf16[256,3584]{1,0:T(8,128)(2,1)}, bf16[256,3584]{1,0:T(8,128)(2,1)S(1)}, u32[]{:S(2)}, u32[]{:S(2)}) collective-permute-start(bf16[256,3584]{1,0:T(8,128)(2,1)} %bitcast.33), channel_id=1, source_target_pairs={{0,16},{8,24},{16,0},{24,8},{1,17},{9,25},{17,1},{25,9},{2,18},{10... | collective-permute-start | bytes 5505032 | tf_op jit(solution)/shard_map/ppermute | solution.py:211
  111.3 29.1 %collective-permute-start.10 = (bf16[2624,512]{1,0:T(8,128)(2,1)}, bf16[2624,512]{1,0:T(8,128)(2,1)S(1)}, u32[]{:S(2)}, u32[]{:S(2)}) collective-permute-start(bf16[2624,512]{1,0:T(8,128)(2,1)} %get-tuple-element.117.refs_9_), channel_id=1, source_target_pairs={{0,8},{8,0},{16,24},{24,16},{1,9},{9,1},{17,25},{25,17},{2,10},{10... | collective-permute-start | bytes 8060936 | tf_op jit(solution)/shard_map/cond/branch_1_fun/ppermute | solution.py:211
  111.5 13.4 %collective-permute-start.8 = (bf16[64,3712]{1,0:T(8,128)(2,1)}, bf16[64,3712]{1,0:T(8,128)(2,1)S(1)}, u32[]{:S(2)}, u32[]{:S(2)}) collective-permute-start(bf16[64,3712]{1,0:T(8,128)(2,1)} %get-tuple-element.111.refs_2_), channel_id=1, source_target_pairs={{0,1},{1,0},{2,3},{3,2},{4,5},{5,4},{6,7},{7,6},{8,9},{9,8},{10,11... | collective-permute-start | bytes 1425416 | tf_op jit(solution)/shard_map/cond/branch_1_fun/ppermute | solution.py:201
  113.0 14.0 %collective-permute-start.11 = (bf16[64,3712]{1,0:T(8,128)(2,1)}, bf16[64,3712]{1,0:T(8,128)(2,1)S(1)}, u32[]{:S(2)}, u32[]{:S(2)}) collective-permute-start(bf16[64,3712]{1,0:T(8,128)(2,1)} %get-tuple-element.111.refs_2_), channel_id=1, source_target_pairs={{0,2},{1,3},{2,6},{3,7},{6,4},{7,5},{4,0},{5,1},{8,10},{9,11},{10,... | collective-permute-start | bytes 1425416 | tf_op jit(solution)/shard_map/cond/branch_1_fun/ppermute | solution.py:207
  114.6 25.9 %collective-permute-start.9 = (bf16[960,512]{1,0:T(8,128)(2,1)}, bf16[960,512]{1,0:T(8,128)(2,1)S(1)}, u32[]{:S(2)}, u32[]{:S(2)}) collective-permute-start(bf16[960,512]{1,0:T(8,128)(2,1)} %get-tuple-element.116.refs_8_), channel_id=1, source_target_pairs={{0,8},{8,0},{16,24},{24,16},{1,9},{9,1},{17,25},{25,17},{2,10},{10... | collective-permute-start | bytes 2949128 | tf_op jit(solution)/shard_map/cond/branch_1_fun/ppermute | solution.py:211
  127.0 12.9 %collective-permute-start.13 = (bf16[64,3712]{1,0:T(8,128)(2,1)S(1)}, bf16[64,3712]{1,0:T(8,128)(2,1)S(1)}, u32[]{:S(2)}, u32[]{:S(2)}) collective-permute-start(bf16[64,3712]{1,0:T(8,128)(2,1)S(1)} %collective-permute-done.11.refs_0_), channel_id=1, source_target_pairs={{0,2},{1,3},{2,6},{3,7},{6,4},{7,5},{4,0},{5,1},{8,10},{9,11},{10,... | collective-permute-start | bytes 1425416 | tf_op jit(solution)/shard_map/cond/branch_1_fun/ppermute | solution.py:207
  127.8 21.1 %collective-permute-start.12 = (bf16[64,3712]{1,0:T(8,128)(2,1)S(1)}, bf16[64,3712]{1,0:T(8,128)(2,1)S(1)}, u32[]{:S(2)}, u32[]{:S(2)}) collective-permute-start(bf16[64,3712]{1,0:T(8,128)(2,1)S(1)} %collective-permute-done.11.refs_0_), channel_id=1, source_target_pairs={{0,1},{1,0},{2,3},{3,2},{4,5},{5,4},{6,7},{7,6},{8,9},{9,8},{10,11... | collective-permute-start | bytes 1425416 | tf_op jit(solution)/shard_map/cond/branch_1_fun/ppermute | solution.py:201
  175.2 13.5 %collective-permute-start.32 = (bf16[64,3584]{1,0:T(8,128)(2,1)S(1)}, bf16[64,3584]{1,0:T(8,128)(2,1)S(1)}, u32[]{:S(2)}, u32[]{:S(2)}) collective-permute-start(bf16[64,3584]{1,0:T(8,128)(2,1)S(1)} %add_convert_fusion.7), channel_id=1, source_target_pairs={{0,1},{1,0},{2,3},{3,2},{4,5},{5,4},{6,7},{7,6},{8,9},{9,8},{10,11... | collective-permute-start | bytes 1376264 | tf_op jit(solution)/shard_map/ppermute | solution.py:201
  176.1 12.7 %collective-permute-start.30 = (bf16[64,3584]{1,0:T(8,128)(2,1)S(1)}, bf16[64,3584]{1,0:T(8,128)(2,1)S(1)}, u32[]{:S(2)}, u32[]{:S(2)}) collective-permute-start(bf16[64,3584]{1,0:T(8,128)(2,1)S(1)} %add_convert_fusion.8), channel_id=1, source_target_pairs={{0,2},{1,3},{2,6},{3,7},{6,4},{7,5},{4,0},{5,1},{8,10},{9,11},{10,... | collective-permute-start | bytes 1376264 | tf_op jit(solution)/shard_map/ppermute | solution.py:207
  178.2 20.4 %collective-permute-start.34 = (bf16[64,3584]{1,0:T(8,128)(2,1)S(1)}, bf16[64,3584]{1,0:T(8,128)(2,1)S(1)}, u32[]{:S(2)}, u32[]{:S(2)}) collective-permute-start(bf16[64,3584]{1,0:T(8,128)(2,1)S(1)} %get-tuple-element.247), channel_id=1, source_target_pairs={{0,1},{1,0},{2,3},{3,2},{4,5},{5,4},{6,7},{7,6},{8,9},{9,8},{10,11... | collective-permute-start | bytes 1376264 | tf_op jit(solution)/shard_map/ppermute | solution.py:201
  188.9 11.1 %collective-permute-start.33 = (bf16[64,3584]{1,0:T(8,128)(2,1)S(1)}, bf16[64,3584]{1,0:T(8,128)(2,1)S(1)}, u32[]{:S(2)}, u32[]{:S(2)}) collective-permute-start(bf16[64,3584]{1,0:T(8,128)(2,1)S(1)} %add_convert_fusion.6), channel_id=1, source_target_pairs={{0,2},{1,3},{2,6},{3,7},{6,4},{7,5},{4,0},{5,1},{8,10},{9,11},{10,... | collective-permute-start | bytes 1376264 | tf_op jit(solution)/shard_map/ppermute | solution.py:207
  190.1 16.6 %collective-permute-start.36 = (bf16[64,3584]{1,0:T(8,128)(2,1)}, bf16[64,3584]{1,0:T(8,128)(2,1)S(1)}, u32[]{:S(2)}, u32[]{:S(2)}) collective-permute-start(bf16[64,3584]{1,0:T(8,128)(2,1)} %get-tuple-element.250), channel_id=1, source_target_pairs={{0,1},{1,0},{2,3},{3,2},{4,5},{5,4},{6,7},{7,6},{8,9},{9,8},{10,11... | collective-permute-start | bytes 1376264 | tf_op jit(solution)/shard_map/ppermute | solution.py:201
  (30 other events, 228.0 us)

commit v6 on v5

--- a/solution.py
+++ b/solution.py
@@ -691,18 +691,18 @@
     far = after(far, own_both)
     both_a = swap_ctx(after(own_both[0], far), 2)
 
-    def attend_and_project(here, flat_q, q_rope, own, far, uv_weight, out_weight, expert_ids, gate_levels, bin_ids):
+    def attend_and_project(here, flat_q, q_rope, own, far, uv_weight, out_weight, expert_ids, gate_levels, bin_ids, both):
         far_across = swap_exp(far)
+        there = swap_ctx(after(both, far_across), 1)
         near = lax.ppermute(own, "ctx", [(c, c + 1) for c in range(0, ctx_devices, 2)])
         table = route_table(expert_ids, gate_levels, bin_ids, exp_devices)
         early = after(far, (flat_q, table))
         key_pieces = [own, near, *[lax.ppermute(piece, "ctx", [(3, 2)]) for piece in (early, far_across)], far, far_across]
         values = attend(here, flat_q, q_rope, key_pieces, uv_weight, rope_width)
-        return project_blocks(here, values, out_weight, exp_devices), table
-
-    there_both = [swap_ctx(piece, 1) for piece in own_both]
-    inputs = here, flat_q, q_rope, own, far, uv_weight, out_weight, expert_ids, gate_levels, bin_ids
-    partial, table = after(one_step(attend_and_project, *inputs), both_a)
+        return project_blocks(here, after(values, there), out_weight, exp_devices), table, there
+
+    inputs = here, flat_q, q_rope, own, far, uv_weight, out_weight, expert_ids, gate_levels, bin_ids, own_both[0]
+    partial, table, there_a = after(one_step(attend_and_project, *inputs), both_a)
     both_c = swap_ctx(after(own_both[1], (partial[0], both_a)), 2)
 
     def sum_and_norm(partial, *rest):
@@ -718,7 +718,7 @@
         ),
         both_c,
     )
-    there_both = [there_both[0], there_c]
+    there_both = [there_a, there_c]
     far_down = swap_ctx(after(w_down, (both_c, back)), 2)
 
     def gather_and_hide(block, across, back, here, own_both, there_both, far_both):

time: 212 us -> 210 us (level)
    ppermute x11, waiting for transfers between devices: 11.1 us -> 8.37 us  [swap_ctx(): lax.ppermute(value, 'ctx', [(c, c ^ bit) for c in range(lax.axis_size('ct...]
  transfers between devices with their start and end apart: 39 -> 39, of which waited for: 27 -> 25; matrix products, arithmetic and copies ran while one was open for 1% -> 1% of each run, Pallas kernels for 14% -> 14%
where the time goes in v6:
time: 210 us
  waiting for transfers between devices  117 us (56%)
  starting transfers between devices  43.3 us (21%)
  Pallas kernels  37.4 us (18%)
  local copies, waits for them, and re-layouts  7.85 us (4%)
  other arithmetic  2.47 us (1%)
    ppermute x13, waiting for transfers between devices, swap_exp(): lax.ppermute(value, 'exp', [(e, e ^ bit) for e in range(lax.axis_size('ex...  69.7 us
    ppermute x11, waiting for transfers between devices, ring_z(): lax.ppermute(value, 'exp', [(2 * a + x, 2 * b + x) for a, b in steps for...  37.2 us
    ppermute x11, starting transfers between devices, ring_z(): lax.ppermute(value, 'exp', [(2 * a + x, 2 * b + x) for a, b in steps for...  14.3 us
    pallas_call x2, Pallas kernels, hidden_rows(): pl.pallas_call(functools.partial(hidden_kernel, blocks=len(rows), counts=...  13.3 us
    ppermute x13, starting transfers between devices, swap_exp(): lax.ppermute(value, 'exp', [(e, e ^ bit) for e in range(lax.axis_size('ex...  12.4 us
    ppermute x11, starting transfers between devices, swap_ctx(): lax.ppermute(value, 'ctx', [(c, c ^ bit) for c in range(lax.axis_size('ct...  9 us
    pallas_call x1, Pallas kernels, attend(): pl.pallas_call(functools.partial(attend_kernel, heads=heads, rope_width=r...  8.98 us
    ppermute x11, waiting for transfers between devices, swap_ctx(): lax.ppermute(value, 'ctx', [(c, c ^ bit) for c in range(lax.axis_size('ct...  8.37 us
  transfers between devices with their start and end apart: 39, of which 25 were waited for; matrix products, arithmetic and copies ran while one was open for 1% of the time, Pallas kernels for 14%

profile of v6, /device:TPU:0, one launch (start us, length us, event | category | flops | bytes accessed | tf_op | source)
XLA Modules:
  0.0 209.6 jit_solution(12729457185233812765)
XLA Ops:
  5.2 4.9 %collective-permute-start.24 = (bf16[256,640]{1,0:T(8,128)(2,1)S(1)}, bf16[256,640]{1,0:T(8,128)(2,1)S(1)}, u32[]{:S(2)}, u32[]{:S(2)}) collective-permute-start(bf16[256,640]{1,0:T(8,128)(2,1)S(1)} %get-tuple-element.199), channel_id=1, source_target_pairs={{0,16},{8,24},{1,17},{9,25},{2,18},{10,26},{3,19},{11,27},{4,20},{... | collective-permute-start | bytes 983048 | tf_op jit(solution)/shard_map/ppermute | solution.py:687
  20.3 24.8 %conditional.4 = (bf16[64,3584]{1,0:T(8,128)(2,1)}, bf16[64,3584]{1,0:T(8,128)(2,1)}, bf16[64,3584]{1,0:T(8,128)(2,1)S(1)}, bf16[64,1792]{1,0:T(8,128)(2,1)S(1)}...) conditional(s32[]{:T(128)} %convert_element_type.102, () %tuple.57, ...), branch_computations={%region_0.1_spmd, %region_1.2_spmd} | conditional | flops 4563402752 | bytes 31732084 | solution.py:224
  23.2 5.7 %collective-permute-done.2.refs_5_ = bf16[256,640]{1,0:T(8,128)(2,1)S(1)} collective-permute-done((bf16[256,640]{1,0:T(8,128)(2,1)}, bf16[256,640]{1,0:T(8,128)(2,1)S(1)}, u32[]{:S(2)}, u32[]{:S(2)}) %collective-permute-start.2) | collective-permute-done | bytes 327712 | tf_op jit(solution)/shard_map/cond/branch_1_fun/ppermute | solution.py:201
  31.3 9.0 %attend.1.values = bf16[512,256]{1,0:T(8,128)(2,1)S(1)} custom-call(s32[11]{0:T(128)S(1)} %get-tuple-element.73.scalars.order, bf16[512,1024]{1,0:T(8,128)(2,1)S(1)} %bitcast.26, bf16[512,128]{1,0:T(8,128)(2,1)S(1)} %copy-done.14, bf16[512,640]{1,0:T(8,128)(2,1)} %get-tuple-element.76.refs_0_, bf16[512,640]{1,0:T(8,128)(2,1)S(1)} %collective-permute-done.refs_1_, ...), custom_call_target="tpu_custom_call" | custom-call | flops 3623878656 | bytes 3932160 | tf_op jit(solution)/shard_map/cond/branch_1_fun/attend/pallas_call | solution.py:459
  40.3 4.0 %project.1 = (bf16[64,3584]{1,0:T(8,128)(2,1)S(1)}, bf16[64,3584]{1,0:T(8,128)(2,1)}, bf16[64,3584]{1,0:T(8,128)(2,1)S(1)}, bf16[64,1792]{1,0:T(8,128)(2,1)S(1)}...) custom-call(s32[11]{0:T(128)S(1)} %get-tuple-element.73.scalars.orde, ...), custom_call_target="tpu_custom_call" | custom-call | flops 939524096 | bytes 5505024 | tf_op jit(solution)/shard_map/cond/branch_1_fun/project/pallas_call | solution.py:512
  45.1 3.7 %collective-permute-start.26 = (bf16[2624,512]{1,0:T(8,128)(2,1)}, bf16[2624,512]{1,0:T(8,128)(2,1)}, u32[]{:S(2)}, u32[]{:S(2)}) collective-permute-start(bf16[2624,512]{1,0:T(8,128)(2,1)} %get-tuple-element.231), channel_id=1, source_target_pairs={{0,16},{8,24},{16,0},{24,8},{1,17},{9,25},{17,1},{25,9},{2,18},{10... | collective-permute-start | bytes 8060936 | tf_op jit(solution)/shard_map/ppermute | solution.py:211
  48.8 44.3 %conditional.5 = ((f32[64,3584]{1,0:T(8,128)S(1)}, bf16[64,3712]{1,0:T(8,128)(2,1)S(1)})) conditional(s32[]{:T(128)} %convert_element_type.102, () %tuple.56, (bf16[64,3584]{1,0:T(8,128)(2,1)S(1)}, bf16[64,1792]{1,0:T(8,128)(2,1)S(1)}, bf16[64,3584]{1,0:T(8,128)(2,1)S(1)}, bf16[64,3584]{1,0:T(8,128)(2,1)S(1)}, bf16[64,1792]{1,0:T(8,128)(2,1)S(1)}, ...), branch_computations={%region_2.3_spmd, %region_3.4_spmd} | conditional | flops 6422528 | bytes 25719168 | solution.py:224
  51.9 5.2 %collective-permute-done.18 = bf16[64,1792]{1,0:T(8,128)(2,1)S(1)} collective-permute-done((bf16[64,1792]{1,0:T(8,128)(2,1)S(1)}, bf16[64,1792]{1,0:T(8,128)(2,1)S(1)}, u32[]{:S(2)}, u32[]{:S(2)}) %collective-permute-start.18) | collective-permute-done | bytes 229408 | tf_op jit(solution)/shard_map/cond/branch_1_fun/ppermute | solution.py:207
  62.1 8.6 %collective-permute-done.19 = bf16[64,3584]{1,0:T(8,128)(2,1)S(1)} collective-permute-done((bf16[64,3584]{1,0:T(8,128)(2,1)S(1)}, bf16[64,3584]{1,0:T(8,128)(2,1)S(1)}, u32[]{:S(2)}, u32[]{:S(2)}) %collective-permute-start.19) | collective-permute-done | bytes 458784 | tf_op jit(solution)/shard_map/cond/branch_1_fun/ppermute | solution.py:201
  73.2 7.3 %collective-permute-done.21 = bf16[64,3584]{1,0:T(8,128)(2,1)S(1)} collective-permute-done((bf16[64,3584]{1,0:T(8,128)(2,1)}, bf16[64,3584]{1,0:T(8,128)(2,1)S(1)}, u32[]{:S(2)}, u32[]{:S(2)}) %collective-permute-start.21) | collective-permute-done | bytes 458784 | tf_op jit(solution)/shard_map/cond/branch_1_fun/ppermute | solution.py:201
  83.2 5.1 %collective-permute-done.23.across = bf16[64,3584]{1,0:T(8,128)(2,1)S(1)} collective-permute-done((bf16[64,3584]{1,0:T(8,128)(2,1)}, bf16[64,3584]{1,0:T(8,128)(2,1)S(1)}, u32[]{:S(2)}, u32[]{:S(2)}) %collective-permute-start.23) | collective-permute-done | bytes 458784 | tf_op jit(solution)/shard_map/cond/branch_1_fun/ppermute | solution.py:201
  88.3 4.3 %collective-permute-done.22.moved = bf16[64,3584]{1,0:T(8,128)(2,1)S(1)} collective-permute-done((bf16[64,3584]{1,0:T(8,128)(2,1)S(1)}, bf16[64,3584]{1,0:T(8,128)(2,1)S(1)}, u32[]{:S(2)}, u32[]{:S(2)}) %collective-permute-start.22) | collective-permute-done | bytes 458784 | tf_op jit(solution)/shard_map/cond/branch_1_fun/ppermute | solution.py:207
  93.1 14.5 %conditional.6 = (bf16[64,3712]{1,0:T(8,128)(2,1)}, bf16[64,3712]{1,0:T(8,128)(2,1)}, bf16[2624,512]{1,0:T(8,128)(2,1)}, bf16[256,3584]{1,0:T(8,128)(2,1)}) conditional(s32[]{:T(128)} %convert_element_type.102, () %tuple.64, (bf16[64,3712]{1,0:T(8,128)(2,1)S(1)}, bf16[2624,512]{1,0:T(8,128)(2,1)}, bf16[256,3584]{1,0:T(8,128)(2,1)}) %tuple.93), branch_computations={%region_4.5_spmd, %region_5.6_spmd} | conditional | bytes 21889216 | solution.py:224
  94.5 12.2 %collective-permute-done.5 = bf16[64,3712]{1,0:T(8,128)(2,1)} collective-permute-done((bf16[64,3712]{1,0:T(8,128)(2,1)S(1)}, bf16[64,3712]{1,0:T(8,128)(2,1)}, u32[]{:S(2)}, u32[]{:S(2)}) %collective-permute-start.5) | collective-permute-done | bytes 475168 | tf_op jit(solution)/shard_map/cond/branch_1_fun/ppermute | solution.py:201
  109.5 45.1 %conditional.7 = (bf16[256,1024]{1,0:T(8,128)(2,1)S(1)}, bf16[256,1024]{1,0:T(8,128)(2,1)S(1)}, f32[16,128]{1,0:T(8,128)S(1)}, f32[16,128]{1,0:T(8,128)S(1)}, f3...) conditional(s32[]{:T(128)} %convert_element_type.102, () %tuple.63, (bf16[64,3712]{1,0:T(8,128)(2,1)}, ...), branch_computations={%region_6.7_spmd, %region_7.8_spmd} | conditional | flops 7516192768 | bytes 57213256 | solution.py:224
  112.5 10.4 %collective-permute-done.9.refs_3_ = bf16[64,3712]{1,0:T(8,128)(2,1)S(1)} collective-permute-done((bf16[64,3712]{1,0:T(8,128)(2,1)}, bf16[64,3712]{1,0:T(8,128)(2,1)S(1)}, u32[]{:S(2)}, u32[]{:S(2)}) %collective-permute-start.9) | collective-permute-done | bytes 475168 | tf_op jit(solution)/shard_map/cond/branch_1_fun/ppermute | solution.py:201
  126.5 11.7 %collective-permute-done.14.refs_2_ = bf16[64,3712]{1,0:T(8,128)(2,1)S(1)} collective-permute-done((bf16[64,3712]{1,0:T(8,128)(2,1)S(1)}, bf16[64,3712]{1,0:T(8,128)(2,1)S(1)}, u32[]{:S(2)}, u32[]{:S(2)}) %collective-permute-start.14) | collective-permute-done | bytes 475168 | tf_op jit(solution)/shard_map/cond/branch_1_fun/ppermute | solution.py:207
  138.7 8.5 %hidden.2 = (bf16[256,1024]{1,0:T(8,128)(2,1)S(1)}, f32[16,128]{1,0:T(8,128)S(1)}, f32[256,1]{1,0:T(8,128)S(1)}, bf16[4,3584,512]{2,1,0:T(8,128)(2,1)S(1)}) custom-call(s32[11]{0:T(128)S(1)} %get-tuple-element.113.here, bf16[64,3712]{1,0:T(8,128)(2,1)S(1)} %get-tuple-element.114.refs_0_, bf16[64,3712]{1,0:T(8,128)(2,1)} %get-tuple-element.115.refs_1_, ...), custom_call_target="tpu_custom_call" | custom-call | flops 3758096384 | bytes 16515072 | tf_op jit(solution)/shard_map/cond/branch_1_fun/hidden/pallas_call | solution.py:588
  149.5 4.9 %hidden.3 = (bf16[256,1024]{1,0:T(8,128)(2,1)S(1)}, f32[16,128]{1,0:T(8,128)S(1)}, f32[256,1]{1,0:T(8,128)S(1)}) custom-call(s32[11]{0:T(128)S(1)} %get-tuple-element.113.here, bf16[64,3712]{1,0:T(8,128)(2,1)S(1)} %collective-permute-done.12.refs_0_, bf16[64,3712]{1,0:T(8,128)(2,1)S(1)} %collective-permute-done.13.refs_1_, ...), custom_call_target="tpu_custom_call" | custom-call | flops 3758096384 | bytes 16515072 | tf_op jit(solution)/shard_map/cond/branch_1_fun/hidden/pallas_call | solution.py:588
  154.7 3.8 %collective-permute-done.28.refs_7_ = bf16[256,3584]{1,0:T(8,128)(2,1)S(1)} collective-permute-done((bf16[256,3584]{1,0:T(8,128)(2,1)S(1)}, bf16[256,3584]{1,0:T(8,128)(2,1)S(1)}, u32[]{:S(2)}, u32[]{:S(2)}) %collective-permute-start.28) | collective-permute-done | bytes 1835040 | tf_op jit(solution)/shard_map/ppermute | solution.py:211
  158.4 6.6 %down.1 = (bf16[64,3584]{1,0:T(8,128)(2,1)S(1)}, bf16[64,3584]{1,0:T(8,128)(2,1)}, bf16[64,3584]{1,0:T(8,128)(2,1)S(1)}, bf16[64,1792]{1,0:T(8,128)(2,1)S(1)}, b...) custom-call(bf16[256,1024]{1,0:T(8,128)(2,1)S(1)} %get-tuple-element, ...), custom_call_target="tpu_custom_call" | custom-call | flops 3758096384 | bytes 11010048 | tf_op jit(solution)/shard_map/down/pallas_call | solution.py:639
  167.5 6.2 %collective-permute-done.31 = bf16[64,1792]{1,0:T(8,128)(2,1)S(1)} collective-permute-done((bf16[64,1792]{1,0:T(8,128)(2,1)S(1)}, bf16[64,1792]{1,0:T(8,128)(2,1)S(1)}, u32[]{:S(2)}, u32[]{:S(2)}) %collective-permute-start.31) | collective-permute-done | bytes 229408 | tf_op jit(solution)/shard_map/ppermute | solution.py:207
  177.2 10.0 %collective-permute-done.32 = bf16[64,3584]{1,0:T(8,128)(2,1)S(1)} collective-permute-done((bf16[64,3584]{1,0:T(8,128)(2,1)S(1)}, bf16[64,3584]{1,0:T(8,128)(2,1)S(1)}, u32[]{:S(2)}, u32[]{:S(2)}) %collective-permute-start.32) | collective-permute-done | bytes 458784 | tf_op jit(solution)/shard_map/ppermute | solution.py:201
  189.2 7.9 %collective-permute-done.34 = bf16[64,3584]{1,0:T(8,128)(2,1)S(1)} collective-permute-done((bf16[64,3584]{1,0:T(8,128)(2,1)S(1)}, bf16[64,3584]{1,0:T(8,128)(2,1)S(1)}, u32[]{:S(2)}, u32[]{:S(2)}) %collective-permute-start.34) | collective-permute-done | bytes 458784 | tf_op jit(solution)/shard_map/ppermute | solution.py:201
  (119 shorter events, 68.4 us)
Async XLA Ops:
  5.2 11.8 %collective-permute-start.24 = (bf16[256,640]{1,0:T(8,128)(2,1)S(1)}, bf16[256,640]{1,0:T(8,128)(2,1)S(1)}, u32[]{:S(2)}, u32[]{:S(2)}) collective-permute-start(bf16[256,640]{1,0:T(8,128)(2,1)S(1)} %get-tuple-element.199), channel_id=1, source_target_pairs={{0,16},{8,24},{1,17},{9,25},{2,18},{10,26},{3,19},{11,27},{4,20},{... | collective-permute-start | bytes 983048 | tf_op jit(solution)/shard_map/ppermute | solution.py:687
  17.8 27.4 %collective-permute-start.25 = (bf16[960,512]{1,0:T(8,128)(2,1)}, bf16[960,512]{1,0:T(8,128)(2,1)}, u32[]{:S(2)}, u32[]{:S(2)}) collective-permute-start(bf16[960,512]{1,0:T(8,128)(2,1)} %get-tuple-element.214), channel_id=1, source_target_pairs={{0,16},{8,24},{16,0},{24,8},{1,17},{9,25},{17,1},{25,9},{2,18},{10... | collective-permute-start | bytes 2949128 | tf_op jit(solution)/shard_map/ppermute | solution.py:211
  28.9 11.4 %collective-permute-start.4 = (bf16[960,512]{1,0:T(8,128)(2,1)}, bf16[960,512]{1,0:T(8,128)(2,1)}, u32[]{:S(2)}, u32[]{:S(2)}) collective-permute-start(bf16[960,512]{1,0:T(8,128)(2,1)} %get-tuple-element.84), channel_id=1, source_target_pairs={{0,8},{8,0},{16,24},{24,16},{1,9},{9,1},{17,25},{25,17},{2,10},{10... | collective-permute-start | bytes 2949128 | tf_op jit(solution)/shard_map/cond/branch_1_fun/ppermute | solution.py:211
  45.1 62.6 %collective-permute-start.26 = (bf16[2624,512]{1,0:T(8,128)(2,1)}, bf16[2624,512]{1,0:T(8,128)(2,1)}, u32[]{:S(2)}, u32[]{:S(2)}) collective-permute-start(bf16[2624,512]{1,0:T(8,128)(2,1)} %get-tuple-element.231), channel_id=1, source_target_pairs={{0,16},{8,24},{16,0},{24,8},{1,17},{9,25},{17,1},{25,9},{2,18},{10... | collective-permute-start | bytes 8060936 | tf_op jit(solution)/shard_map/ppermute | solution.py:211
  57.2 13.5 %collective-permute-start.19 = (bf16[64,3584]{1,0:T(8,128)(2,1)S(1)}, bf16[64,3584]{1,0:T(8,128)(2,1)S(1)}, u32[]{:S(2)}, u32[]{:S(2)}) collective-permute-start(bf16[64,3584]{1,0:T(8,128)(2,1)S(1)} %add_convert_fusion.2), channel_id=1, source_target_pairs={{0,1},{1,0},{2,3},{3,2},{4,5},{5,4},{6,7},{7,6},{8,9},{9,8},{10,11... | collective-permute-start | bytes 1376264 | tf_op jit(solution)/shard_map/cond/branch_1_fun/ppermute | solution.py:201
  58.8 12.1 %collective-permute-start.17 = (bf16[64,3584]{1,0:T(8,128)(2,1)S(1)}, bf16[64,3584]{1,0:T(8,128)(2,1)S(1)}, u32[]{:S(2)}, u32[]{:S(2)}) collective-permute-start(bf16[64,3584]{1,0:T(8,128)(2,1)S(1)} %add_convert_fusion.3), channel_id=1, source_target_pairs={{0,2},{1,3},{2,6},{3,7},{6,4},{7,5},{4,0},{5,1},{8,10},{9,11},{10,... | collective-permute-start | bytes 1376264 | tf_op jit(solution)/shard_map/cond/branch_1_fun/ppermute | solution.py:207
  60.6 19.9 %collective-permute-start.21 = (bf16[64,3584]{1,0:T(8,128)(2,1)}, bf16[64,3584]{1,0:T(8,128)(2,1)S(1)}, u32[]{:S(2)}, u32[]{:S(2)}) collective-permute-start(bf16[64,3584]{1,0:T(8,128)(2,1)} %get-tuple-element.103), channel_id=1, source_target_pairs={{0,1},{1,0},{2,3},{3,2},{4,5},{5,4},{6,7},{7,6},{8,9},{9,8},{10,11... | collective-permute-start | bytes 1376264 | tf_op jit(solution)/shard_map/cond/branch_1_fun/ppermute | solution.py:201
  71.9 16.4 %collective-permute-start.23 = (bf16[64,3584]{1,0:T(8,128)(2,1)}, bf16[64,3584]{1,0:T(8,128)(2,1)S(1)}, u32[]{:S(2)}, u32[]{:S(2)}) collective-permute-start(bf16[64,3584]{1,0:T(8,128)(2,1)} %get-tuple-element.106), channel_id=1, source_target_pairs={{0,1},{1,0},{2,3},{3,2},{4,5},{5,4},{6,7},{7,6},{8,9},{9,8},{10,11... | collective-permute-start | bytes 1376264 | tf_op jit(solution)/shard_map/cond/branch_1_fun/ppermute | solution.py:201
  93.2 14.4 %collective-permute-start.7 = (bf16[2624,512]{1,0:T(8,128)(2,1)}, bf16[2624,512]{1,0:T(8,128)(2,1)}, u32[]{:S(2)}, u32[]{:S(2)}) collective-permute-start(bf16[2624,512]{1,0:T(8,128)(2,1)} %get-tuple-element.111), channel_id=1, source_target_pairs={{0,8},{8,0},{16,24},{24,16},{1,9},{9,1},{17,25},{25,17},{2,10},{10... | collective-permute-start | bytes 8060936 | tf_op jit(solution)/shard_map/cond/branch_1_fun/ppermute | solution.py:211
  93.2 14.4 %collective-permute-start.8 = (bf16[256,3584]{1,0:T(8,128)(2,1)}, bf16[256,3584]{1,0:T(8,128)(2,1)}, u32[]{:S(2)}, u32[]{:S(2)}) collective-permute-start(bf16[256,3584]{1,0:T(8,128)(2,1)} %get-tuple-element.112), channel_id=1, source_target_pairs={{0,8},{8,0},{16,24},{24,16},{1,9},{9,1},{17,25},{25,17},{2,10},{10... | collective-permute-start | bytes 5505032 | tf_op jit(solution)/shard_map/cond/branch_1_fun/ppermute | solution.py:211
  93.7 13.0 %collective-permute-start.5 = (bf16[64,3712]{1,0:T(8,128)(2,1)S(1)}, bf16[64,3712]{1,0:T(8,128)(2,1)}, u32[]{:S(2)}, u32[]{:S(2)}) collective-permute-start(bf16[64,3712]{1,0:T(8,128)(2,1)S(1)} %get-tuple-element.110), channel_id=1, source_target_pairs={{0,1},{1,0},{2,3},{3,2},{4,5},{5,4},{6,7},{7,6},{8,9},{9,8},{10,11... | collective-permute-start | bytes 1425416 | tf_op jit(solution)/shard_map/cond/branch_1_fun/ppermute | solution.py:201
  93.7 13.9 %collective-permute-start.6 = (bf16[64,3712]{1,0:T(8,128)(2,1)S(1)}, bf16[64,3712]{1,0:T(8,128)(2,1)}, u32[]{:S(2)}, u32[]{:S(2)}) collective-permute-start(bf16[64,3712]{1,0:T(8,128)(2,1)S(1)} %get-tuple-element.110), channel_id=1, source_target_pairs={{0,2},{1,3},{2,6},{3,7},{6,4},{7,5},{4,0},{5,1},{8,10},{9,11},{10,... | collective-permute-start | bytes 1425416 | tf_op jit(solution)/shard_map/cond/branch_1_fun/ppermute | solution.py:207
  107.7 46.9 %collective-permute-start.27 = (bf16[256,3584]{1,0:T(8,128)(2,1)}, bf16[256,3584]{1,0:T(8,128)(2,1)S(1)}, u32[]{:S(2)}, u32[]{:S(2)}) collective-permute-start(bf16[256,3584]{1,0:T(8,128)(2,1)} %bitcast.33), channel_id=1, source_target_pairs={{0,16},{8,24},{16,0},{24,8},{1,17},{9,25},{17,1},{25,9},{2,18},{10... | collective-permute-start | bytes 5505032 | tf_op jit(solution)/shard_map/ppermute | solution.py:211
  109.5 29.3 %collective-permute-start.11 = (bf16[2624,512]{1,0:T(8,128)(2,1)}, bf16[2624,512]{1,0:T(8,128)(2,1)S(1)}, u32[]{:S(2)}, u32[]{:S(2)}) collective-permute-start(bf16[2624,512]{1,0:T(8,128)(2,1)} %get-tuple-element.122.refs_9_), channel_id=1, source_target_pairs={{0,8},{8,0},{16,24},{24,16},{1,9},{9,1},{17,25},{25,17},{2,10},{10... | collective-permute-start | bytes 8060936 | tf_op jit(solution)/shard_map/cond/branch_1_fun/ppermute | solution.py:211
  109.5 13.5 %collective-permute-start.9 = (bf16[64,3712]{1,0:T(8,128)(2,1)}, bf16[64,3712]{1,0:T(8,128)(2,1)S(1)}, u32[]{:S(2)}, u32[]{:S(2)}) collective-permute-start(bf16[64,3712]{1,0:T(8,128)(2,1)} %get-tuple-element.116.refs_2_), channel_id=1, source_target_pairs={{0,1},{1,0},{2,3},{3,2},{4,5},{5,4},{6,7},{7,6},{8,9},{9,8},{10,11... | collective-permute-start | bytes 1425416 | tf_op jit(solution)/shard_map/cond/branch_1_fun/ppermute | solution.py:201
  111.0 14.1 %collective-permute-start.12 = (bf16[64,3712]{1,0:T(8,128)(2,1)}, bf16[64,3712]{1,0:T(8,128)(2,1)S(1)}, u32[]{:S(2)}, u32[]{:S(2)}) collective-permute-start(bf16[64,3712]{1,0:T(8,128)(2,1)} %get-tuple-element.116.refs_2_), channel_id=1, source_target_pairs={{0,2},{1,3},{2,6},{3,7},{6,4},{7,5},{4,0},{5,1},{8,10},{9,11},{10,... | collective-permute-start | bytes 1425416 | tf_op jit(solution)/shard_map/cond/branch_1_fun/ppermute | solution.py:207
  112.5 26.2 %collective-permute-start.10 = (bf16[960,512]{1,0:T(8,128)(2,1)}, bf16[960,512]{1,0:T(8,128)(2,1)S(1)}, u32[]{:S(2)}, u32[]{:S(2)}) collective-permute-start(bf16[960,512]{1,0:T(8,128)(2,1)} %get-tuple-element.121.refs_8_), channel_id=1, source_target_pairs={{0,8},{8,0},{16,24},{24,16},{1,9},{9,1},{17,25},{25,17},{2,10},{10... | collective-permute-start | bytes 2949128 | tf_op jit(solution)/shard_map/cond/branch_1_fun/ppermute | solution.py:211
  125.1 13.1 %collective-permute-start.14 = (bf16[64,3712]{1,0:T(8,128)(2,1)S(1)}, bf16[64,3712]{1,0:T(8,128)(2,1)S(1)}, u32[]{:S(2)}, u32[]{:S(2)}) collective-permute-start(bf16[64,3712]{1,0:T(8,128)(2,1)S(1)} %collective-permute-done.12.refs_0_), channel_id=1, source_target_pairs={{0,2},{1,3},{2,6},{3,7},{6,4},{7,5},{4,0},{5,1},{8,10},{9,11},{10,... | collective-permute-start | bytes 1425416 | tf_op jit(solution)/shard_map/cond/branch_1_fun/ppermute | solution.py:207
  126.0 21.3 %collective-permute-start.13 = (bf16[64,3712]{1,0:T(8,128)(2,1)S(1)}, bf16[64,3712]{1,0:T(8,128)(2,1)S(1)}, u32[]{:S(2)}, u32[]{:S(2)}) collective-permute-start(bf16[64,3712]{1,0:T(8,128)(2,1)S(1)} %collective-permute-done.12.refs_0_), channel_id=1, source_target_pairs={{0,1},{1,0},{2,3},{3,2},{4,5},{5,4},{6,7},{7,6},{8,9},{9,8},{10,11... | collective-permute-start | bytes 1425416 | tf_op jit(solution)/shard_map/cond/branch_1_fun/ppermute | solution.py:201
  138.2 11.3 %collective-permute-start.15 = (bf16[64,3712]{1,0:T(8,128)(2,1)S(1)}, bf16[64,3712]{1,0:T(8,128)(2,1)S(1)}, u32[]{:S(2)}, u32[]{:S(2)}) collective-permute-start(bf16[64,3712]{1,0:T(8,128)(2,1)S(1)} %collective-permute-done.14.refs_2_), channel_id=1, source_target_pairs={{0,1},{1,0},{2,3},{3,2},{4,5},{5,4},{6,7},{7,6},{8,9},{9,8},{10,11... | collective-permute-start | bytes 1425416 | tf_op jit(solution)/shard_map/cond/branch_1_fun/ppermute | solution.py:201
  173.7 13.5 %collective-permute-start.32 = (bf16[64,3584]{1,0:T(8,128)(2,1)S(1)}, bf16[64,3584]{1,0:T(8,128)(2,1)S(1)}, u32[]{:S(2)}, u32[]{:S(2)}) collective-permute-start(bf16[64,3584]{1,0:T(8,128)(2,1)S(1)} %add_convert_fusion.7), channel_id=1, source_target_pairs={{0,1},{1,0},{2,3},{3,2},{4,5},{5,4},{6,7},{7,6},{8,9},{9,8},{10,11... | collective-permute-start | bytes 1376264 | tf_op jit(solution)/shard_map/ppermute | solution.py:201
  174.4 12.9 %collective-permute-start.30 = (bf16[64,3584]{1,0:T(8,128)(2,1)S(1)}, bf16[64,3584]{1,0:T(8,128)(2,1)S(1)}, u32[]{:S(2)}, u32[]{:S(2)}) collective-permute-start(bf16[64,3584]{1,0:T(8,128)(2,1)S(1)} %add_convert_fusion.8), channel_id=1, source_target_pairs={{0,2},{1,3},{2,6},{3,7},{6,4},{7,5},{4,0},{5,1},{8,10},{9,11},{10,... | collective-permute-start | bytes 1376264 | tf_op jit(solution)/shard_map/ppermute | solution.py:207
  176.7 20.4 %collective-permute-start.34 = (bf16[64,3584]{1,0:T(8,128)(2,1)S(1)}, bf16[64,3584]{1,0:T(8,128)(2,1)S(1)}, u32[]{:S(2)}, u32[]{:S(2)}) collective-permute-start(bf16[64,3584]{1,0:T(8,128)(2,1)S(1)} %get-tuple-element.256), channel_id=1, source_target_pairs={{0,1},{1,0},{2,3},{3,2},{4,5},{5,4},{6,7},{7,6},{8,9},{9,8},{10,11... | collective-permute-start | bytes 1376264 | tf_op jit(solution)/shard_map/ppermute | solution.py:201
  188.4 16.8 %collective-permute-start.36 = (bf16[64,3584]{1,0:T(8,128)(2,1)}, bf16[64,3584]{1,0:T(8,128)(2,1)S(1)}, u32[]{:S(2)}, u32[]{:S(2)}) collective-permute-start(bf16[64,3584]{1,0:T(8,128)(2,1)} %get-tuple-element.259), channel_id=1, source_target_pairs={{0,1},{1,0},{2,3},{3,2},{4,5},{5,4},{6,7},{7,6},{8,9},{9,8},{10,11... | collective-permute-start | bytes 1376264 | tf_op jit(solution)/shard_map/ppermute | solution.py:201
  (30 other events, 230.8 us)

commit v7 on v6

--- a/solution.py
+++ b/solution.py
@@ -16,7 +16,7 @@
 norm_eps = 1e-06
 masked_score = -1e30
 LOG2_E = math.log2(math.e)
-FIRST_ROWS = 960
+FIRST_ROWS = 1024
 VMEM_BYTES = 14 * 1024 * 1024
 
 
@@ -284,9 +284,10 @@
     return found
 
 
-def pack_kernel(here, latent, k_rope, docs, own, sent):
+def pack_kernel(here, latent, k_rope, docs, own, sent, sem):
     keys, lat_width, rope_width = latent.shape[0], latent.shape[1], k_rope.shape[1]
-    own[:, :lat_width] = latent[...]
+    copy = pltpu.make_async_copy(latent, own.at[:, pl.ds(0, lat_width)], sem)
+    copy.start()
     row = lax.broadcasted_iota(jnp.int32, (128, 128), 0)
     lane = lax.broadcasted_iota(jnp.int32, (128, 128), 1)
     for at in range(keys // 128):
@@ -299,6 +300,7 @@
         own[at * 128 : (at + 1) * 128, lat_width:] = jnp.where(
             lane == rope_width, column.astype(jnp.float32), ropes
         ).astype(jnp.bfloat16)
+    copy.wait()
     half = sent.shape[0]
     sent[...] = own[pl.ds(pl.multiple_of(here[0] * half, half), half), :]
 
@@ -308,8 +310,9 @@
     whole = pl.BlockSpec(memory_space=pltpu.VMEM)
     return pl.pallas_call(
         pack_kernel,
-        in_specs=[pl.BlockSpec(memory_space=pltpu.SMEM)] + [whole] * 3,
+        in_specs=[pl.BlockSpec(memory_space=pltpu.SMEM), pl.BlockSpec(memory_space=pltpu.HBM), whole, whole],
         out_specs=[whole] * 2,
+        scratch_shapes=[pltpu.SemaphoreType.DMA],
         out_shape=[
             jax.ShapeDtypeStruct((keys, width), jnp.bfloat16),
             jax.ShapeDtypeStruct((keys // 2, width), jnp.bfloat16),
@@ -317,7 +320,7 @@
         cost_estimate=pl.CostEstimate(flops=0, bytes_accessed=6 * keys * width, transcendentals=0),
         compiler_params=pltpu.CompilerParams(vmem_limit_bytes=8 * 1024 * 1024),
         name="pack",
-    )(here, latent, k_rope, doc_ids.reshape(keys // 128, 128))
+    )(here, pltpu.with_memory_space_constraint(latent, pltpu.HBM), k_rope, doc_ids.reshape(keys // 128, 128))
 
 
 def join_kernel(left, right, *refs):

time: 210 us -> 214 us (1.019)
  waiting for transfers between devices: 117 us -> 121 us
    ppermute x13, waiting for transfers between devices: 69.7 us -> 72.3 us  [swap_exp(): lax.ppermute(value, 'exp', [(e, e ^ bit) for e in range(lax.axis_size('ex...]
    unnamed x21 -> x19, local copies, waits for them, and re-layouts: 6.44 us -> 5.37 us
  transfers between devices with their start and end apart: 39 -> 39, of which waited for: 25 -> 25; matrix products, arithmetic and copies ran while one was open for 1% -> 2% of each run, Pallas kernels for 14% -> 14%
where the time goes in v7:
time: 214 us
  waiting for transfers between devices  121 us (57%)
  starting transfers between devices  43 us (20%)
  Pallas kernels  38.2 us (18%)
  local copies, waits for them, and re-layouts  8.01 us (4%)
  other arithmetic  2.47 us (1%)
    ppermute x13, waiting for transfers between devices, swap_exp(): lax.ppermute(value, 'exp', [(e, e ^ bit) for e in range(lax.axis_size('ex...  72.3 us
    ppermute x11, waiting for transfers between devices, ring_z(): lax.ppermute(value, 'exp', [(2 * a + x, 2 * b + x) for a, b in steps for...  37.6 us
    ppermute x11, starting transfers between devices, ring_z(): lax.ppermute(value, 'exp', [(2 * a + x, 2 * b + x) for a, b in steps for...  13.6 us
    pallas_call x2, Pallas kernels, hidden_rows(): pl.pallas_call(functools.partial(hidden_kernel, blocks=len(rows), counts=...  13.4 us
    ppermute x13, starting transfers between devices, swap_exp(): lax.ppermute(value, 'exp', [(e, e ^ bit) for e in range(lax.axis_size('ex...  11.5 us
    ppermute x11, starting transfers between devices, swap_ctx(): lax.ppermute(value, 'ctx', [(c, c ^ bit) for c in range(lax.axis_size('ct...  9.29 us
    pallas_call x1, Pallas kernels, attend(): pl.pallas_call(functools.partial(attend_kernel, heads=heads, rope_width=r...  8.98 us
    ppermute x11, waiting for transfers between devices, swap_ctx(): lax.ppermute(value, 'ctx', [(c, c ^ bit) for c in range(lax.axis_size('ct...  8.5 us
  transfers between devices with their start and end apart: 39, of which 25 were waited for; matrix products, arithmetic and copies ran while one was open for 2% of the time, Pallas kernels for 14%

profile of v7, /device:TPU:0, one launch (start us, length us, event | category | flops | bytes accessed | tf_op | source)
XLA Modules:
  0.0 213.7 jit_solution(14847387833745648054)
XLA Ops:
  5.0 4.9 %collective-permute-start.24 = (bf16[256,640]{1,0:T(8,128)(2,1)S(1)}, bf16[256,640]{1,0:T(8,128)(2,1)S(1)}, u32[]{:S(2)}, u32[]{:S(2)}) collective-permute-start(bf16[256,640]{1,0:T(8,128)(2,1)S(1)} %get-tuple-element.199), channel_id=1, source_target_pairs={{0,16},{8,24},{1,17},{9,25},{2,18},{10,26},{3,19},{11,27},{4,20},{... | collective-permute-start | bytes 983048 | tf_op jit(solution)/shard_map/ppermute | solution.py:690
  20.1 28.5 %conditional.4 = (bf16[64,3584]{1,0:T(8,128)(2,1)}, bf16[64,3584]{1,0:T(8,128)(2,1)}, bf16[64,3584]{1,0:T(8,128)(2,1)S(1)}, bf16[64,1792]{1,0:T(8,128)(2,1)S(1)}...) conditional(s32[]{:T(128)} %convert_element_type.102, () %tuple.57, ...), branch_computations={%region_0.1_spmd, %region_1.2_spmd} | conditional | flops 4563402752 | bytes 31994228 | solution.py:224
  21.6 7.0 %collective-permute-done.2.refs_5_ = bf16[256,640]{1,0:T(8,128)(2,1)S(1)} collective-permute-done((bf16[256,640]{1,0:T(8,128)(2,1)}, bf16[256,640]{1,0:T(8,128)(2,1)S(1)}, u32[]{:S(2)}, u32[]{:S(2)}) %collective-permute-start.2) | collective-permute-done | bytes 327712 | tf_op jit(solution)/shard_map/cond/branch_1_fun/ppermute | solution.py:201
  34.8 9.0 %attend.1.values = bf16[512,256]{1,0:T(8,128)(2,1)S(1)} custom-call(s32[11]{0:T(128)S(1)} %get-tuple-element.73.scalars.order, bf16[512,1024]{1,0:T(8,128)(2,1)S(1)} %bitcast.26, bf16[512,128]{1,0:T(8,128)(2,1)S(1)} %copy-done.13, bf16[512,640]{1,0:T(8,128)(2,1)} %get-tuple-element.76.refs_0_, bf16[512,640]{1,0:T(8,128)(2,1)S(1)} %collective-permute-done.refs_1_, ...), custom_call_target="tpu_custom_call" | custom-call | flops 3623878656 | bytes 3932160 | tf_op jit(solution)/shard_map/cond/branch_1_fun/attend/pallas_call | solution.py:462
  43.8 4.0 %project.1 = (bf16[64,3584]{1,0:T(8,128)(2,1)S(1)}, bf16[64,3584]{1,0:T(8,128)(2,1)}, bf16[64,3584]{1,0:T(8,128)(2,1)S(1)}, bf16[64,1792]{1,0:T(8,128)(2,1)S(1)}...) custom-call(s32[11]{0:T(128)S(1)} %get-tuple-element.73.scalars.orde, ...), custom_call_target="tpu_custom_call" | custom-call | flops 939524096 | bytes 5505024 | tf_op jit(solution)/shard_map/cond/branch_1_fun/project/pallas_call | solution.py:515
  48.6 3.7 %collective-permute-start.26 = (bf16[2560,512]{1,0:T(8,128)(2,1)}, bf16[2560,512]{1,0:T(8,128)(2,1)}, u32[]{:S(2)}, u32[]{:S(2)}) collective-permute-start(bf16[2560,512]{1,0:T(8,128)(2,1)} %get-tuple-element.231), channel_id=1, source_target_pairs={{0,16},{8,24},{16,0},{24,8},{1,17},{9,25},{17,1},{25,9},{2,18},{10... | collective-permute-start | bytes 7864328 | tf_op jit(solution)/shard_map/ppermute | solution.py:211
  52.3 44.3 %conditional.5 = ((f32[64,3584]{1,0:T(8,128)S(1)}, bf16[64,3712]{1,0:T(8,128)(2,1)S(1)})) conditional(s32[]{:T(128)} %convert_element_type.102, () %tuple.56, (bf16[64,3584]{1,0:T(8,128)(2,1)S(1)}, bf16[64,1792]{1,0:T(8,128)(2,1)S(1)}, bf16[64,3584]{1,0:T(8,128)(2,1)S(1)}, bf16[64,3584]{1,0:T(8,128)(2,1)S(1)}, bf16[64,1792]{1,0:T(8,128)(2,1)S(1)}, ...), branch_computations={%region_2.3_spmd, %region_3.4_spmd} | conditional | flops 6422528 | bytes 25719168 | solution.py:224
  55.4 5.2 %collective-permute-done.18 = bf16[64,1792]{1,0:T(8,128)(2,1)S(1)} collective-permute-done((bf16[64,1792]{1,0:T(8,128)(2,1)S(1)}, bf16[64,1792]{1,0:T(8,128)(2,1)S(1)}, u32[]{:S(2)}, u32[]{:S(2)}) %collective-permute-start.18) | collective-permute-done | bytes 229408 | tf_op jit(solution)/shard_map/cond/branch_1_fun/ppermute | solution.py:207
  65.6 8.6 %collective-permute-done.19 = bf16[64,3584]{1,0:T(8,128)(2,1)S(1)} collective-permute-done((bf16[64,3584]{1,0:T(8,128)(2,1)S(1)}, bf16[64,3584]{1,0:T(8,128)(2,1)S(1)}, u32[]{:S(2)}, u32[]{:S(2)}) %collective-permute-start.19) | collective-permute-done | bytes 458784 | tf_op jit(solution)/shard_map/cond/branch_1_fun/ppermute | solution.py:201
  76.7 7.3 %collective-permute-done.21 = bf16[64,3584]{1,0:T(8,128)(2,1)S(1)} collective-permute-done((bf16[64,3584]{1,0:T(8,128)(2,1)}, bf16[64,3584]{1,0:T(8,128)(2,1)S(1)}, u32[]{:S(2)}, u32[]{:S(2)}) %collective-permute-start.21) | collective-permute-done | bytes 458784 | tf_op jit(solution)/shard_map/cond/branch_1_fun/ppermute | solution.py:201
  86.7 5.1 %collective-permute-done.23.across = bf16[64,3584]{1,0:T(8,128)(2,1)S(1)} collective-permute-done((bf16[64,3584]{1,0:T(8,128)(2,1)}, bf16[64,3584]{1,0:T(8,128)(2,1)S(1)}, u32[]{:S(2)}, u32[]{:S(2)}) %collective-permute-start.23) | collective-permute-done | bytes 458784 | tf_op jit(solution)/shard_map/cond/branch_1_fun/ppermute | solution.py:201
  91.8 4.3 %collective-permute-done.22.moved = bf16[64,3584]{1,0:T(8,128)(2,1)S(1)} collective-permute-done((bf16[64,3584]{1,0:T(8,128)(2,1)S(1)}, bf16[64,3584]{1,0:T(8,128)(2,1)S(1)}, u32[]{:S(2)}, u32[]{:S(2)}) %collective-permute-start.22) | collective-permute-done | bytes 458784 | tf_op jit(solution)/shard_map/cond/branch_1_fun/ppermute | solution.py:207
  96.6 14.5 %conditional.6 = (bf16[64,3712]{1,0:T(8,128)(2,1)}, bf16[64,3712]{1,0:T(8,128)(2,1)}, bf16[2560,512]{1,0:T(8,128)(2,1)}, bf16[256,3584]{1,0:T(8,128)(2,1)}) conditional(s32[]{:T(128)} %convert_element_type.102, () %tuple.64, (bf16[64,3712]{1,0:T(8,128)(2,1)S(1)}, bf16[2560,512]{1,0:T(8,128)(2,1)}, bf16[256,3584]{1,0:T(8,128)(2,1)}) %tuple.93), branch_computations={%region_4.5_spmd, %region_5.6_spmd} | conditional | bytes 21627072 | solution.py:224
  98.0 12.1 %collective-permute-done.5 = bf16[64,3712]{1,0:T(8,128)(2,1)} collective-permute-done((bf16[64,3712]{1,0:T(8,128)(2,1)S(1)}, bf16[64,3712]{1,0:T(8,128)(2,1)}, u32[]{:S(2)}, u32[]{:S(2)}) %collective-permute-start.5) | collective-permute-done | bytes 475168 | tf_op jit(solution)/shard_map/cond/branch_1_fun/ppermute | solution.py:201
  113.3 45.3 %conditional.7 = (bf16[256,1024]{1,0:T(8,128)(2,1)S(1)}, bf16[256,1024]{1,0:T(8,128)(2,1)S(1)}, f32[16,128]{1,0:T(8,128)S(1)}, f32[16,128]{1,0:T(8,128)S(1)}, f3...) conditional(s32[]{:T(128)} %convert_element_type.102, () %tuple.63, (bf16[64,3712]{1,0:T(8,128)(2,1)}, ...), branch_computations={%region_6.7_spmd, %region_7.8_spmd} | conditional | flops 7516192768 | bytes 57213256 | solution.py:224
  115.8 11.0 %collective-permute-done.9.refs_3_ = bf16[64,3712]{1,0:T(8,128)(2,1)S(1)} collective-permute-done((bf16[64,3712]{1,0:T(8,128)(2,1)}, bf16[64,3712]{1,0:T(8,128)(2,1)S(1)}, u32[]{:S(2)}, u32[]{:S(2)}) %collective-permute-start.9) | collective-permute-done | bytes 475168 | tf_op jit(solution)/shard_map/cond/branch_1_fun/ppermute | solution.py:201
  130.4 11.9 %collective-permute-done.14.refs_2_ = bf16[64,3712]{1,0:T(8,128)(2,1)S(1)} collective-permute-done((bf16[64,3712]{1,0:T(8,128)(2,1)S(1)}, bf16[64,3712]{1,0:T(8,128)(2,1)S(1)}, u32[]{:S(2)}, u32[]{:S(2)}) %collective-permute-start.14) | collective-permute-done | bytes 475168 | tf_op jit(solution)/shard_map/cond/branch_1_fun/ppermute | solution.py:207
  142.6 8.5 %hidden.2 = (bf16[256,1024]{1,0:T(8,128)(2,1)S(1)}, f32[16,128]{1,0:T(8,128)S(1)}, f32[256,1]{1,0:T(8,128)S(1)}, bf16[4,3584,512]{2,1,0:T(8,128)(2,1)S(1)}) custom-call(s32[11]{0:T(128)S(1)} %get-tuple-element.113.here, bf16[64,3712]{1,0:T(8,128)(2,1)S(1)} %get-tuple-element.114.refs_0_, bf16[64,3712]{1,0:T(8,128)(2,1)} %get-tuple-element.115.refs_1_, ...), custom_call_target="tpu_custom_call" | custom-call | flops 3758096384 | bytes 16515072 | tf_op jit(solution)/shard_map/cond/branch_1_fun/hidden/pallas_call | solution.py:591
  153.5 4.9 %hidden.3 = (bf16[256,1024]{1,0:T(8,128)(2,1)S(1)}, f32[16,128]{1,0:T(8,128)S(1)}, f32[256,1]{1,0:T(8,128)S(1)}) custom-call(s32[11]{0:T(128)S(1)} %get-tuple-element.113.here, bf16[64,3712]{1,0:T(8,128)(2,1)S(1)} %collective-permute-done.12.refs_0_, bf16[64,3712]{1,0:T(8,128)(2,1)S(1)} %collective-permute-done.13.refs_1_, ...), custom_call_target="tpu_custom_call" | custom-call | flops 3758096384 | bytes 16515072 | tf_op jit(solution)/shard_map/cond/branch_1_fun/hidden/pallas_call | solution.py:591
  158.7 3.8 %collective-permute-done.28.refs_7_ = bf16[256,3584]{1,0:T(8,128)(2,1)S(1)} collective-permute-done((bf16[256,3584]{1,0:T(8,128)(2,1)S(1)}, bf16[256,3584]{1,0:T(8,128)(2,1)S(1)}, u32[]{:S(2)}, u32[]{:S(2)}) %collective-permute-start.28) | collective-permute-done | bytes 1835040 | tf_op jit(solution)/shard_map/ppermute | solution.py:211
  162.5 6.6 %down.1 = (bf16[64,3584]{1,0:T(8,128)(2,1)S(1)}, bf16[64,3584]{1,0:T(8,128)(2,1)}, bf16[64,3584]{1,0:T(8,128)(2,1)S(1)}, bf16[64,1792]{1,0:T(8,128)(2,1)S(1)}, b...) custom-call(bf16[256,1024]{1,0:T(8,128)(2,1)S(1)} %get-tuple-element, ...), custom_call_target="tpu_custom_call" | custom-call | flops 3758096384 | bytes 11010048 | tf_op jit(solution)/shard_map/down/pallas_call | solution.py:642
  171.4 6.3 %collective-permute-done.31 = bf16[64,1792]{1,0:T(8,128)(2,1)S(1)} collective-permute-done((bf16[64,1792]{1,0:T(8,128)(2,1)S(1)}, bf16[64,1792]{1,0:T(8,128)(2,1)S(1)}, u32[]{:S(2)}, u32[]{:S(2)}) %collective-permute-start.31) | collective-permute-done | bytes 229408 | tf_op jit(solution)/shard_map/ppermute | solution.py:207
  181.1 10.2 %collective-permute-done.32 = bf16[64,3584]{1,0:T(8,128)(2,1)S(1)} collective-permute-done((bf16[64,3584]{1,0:T(8,128)(2,1)S(1)}, bf16[64,3584]{1,0:T(8,128)(2,1)S(1)}, u32[]{:S(2)}, u32[]{:S(2)}) %collective-permute-start.32) | collective-permute-done | bytes 458784 | tf_op jit(solution)/shard_map/ppermute | solution.py:201
  193.4 7.8 %collective-permute-done.34 = bf16[64,3584]{1,0:T(8,128)(2,1)S(1)} collective-permute-done((bf16[64,3584]{1,0:T(8,128)(2,1)S(1)}, bf16[64,3584]{1,0:T(8,128)(2,1)S(1)}, u32[]{:S(2)}, u32[]{:S(2)}) %collective-permute-start.34) | collective-permute-done | bytes 458784 | tf_op jit(solution)/shard_map/ppermute | solution.py:201
  (117 shorter events, 70.1 us)
Async XLA Ops:
  5.0 11.8 %collective-permute-start.24 = (bf16[256,640]{1,0:T(8,128)(2,1)S(1)}, bf16[256,640]{1,0:T(8,128)(2,1)S(1)}, u32[]{:S(2)}, u32[]{:S(2)}) collective-permute-start(bf16[256,640]{1,0:T(8,128)(2,1)S(1)} %get-tuple-element.199), channel_id=1, source_target_pairs={{0,16},{8,24},{1,17},{9,25},{2,18},{10,26},{3,19},{11,27},{4,20},{... | collective-permute-start | bytes 983048 | tf_op jit(solution)/shard_map/ppermute | solution.py:690
  17.6 31.0 %collective-permute-start.25 = (bf16[1024,512]{1,0:T(8,128)(2,1)}, bf16[1024,512]{1,0:T(8,128)(2,1)S(1)}, u32[]{:S(2)}, u32[]{:S(2)}) collective-permute-start(bf16[1024,512]{1,0:T(8,128)(2,1)} %get-tuple-element.214), channel_id=1, source_target_pairs={{0,16},{8,24},{16,0},{24,8},{1,17},{9,25},{17,1},{25,9},{2,18},{10... | collective-permute-start | bytes 3145736 | tf_op jit(solution)/shard_map/ppermute | solution.py:211
  28.7 15.1 %collective-permute-start.4 = (bf16[1024,512]{1,0:T(8,128)(2,1)}, bf16[1024,512]{1,0:T(8,128)(2,1)}, u32[]{:S(2)}, u32[]{:S(2)}) collective-permute-start(bf16[1024,512]{1,0:T(8,128)(2,1)} %get-tuple-element.84), channel_id=1, source_target_pairs={{0,8},{8,0},{16,24},{24,16},{1,9},{9,1},{17,25},{25,17},{2,10},{10... | collective-permute-start | bytes 3145736 | tf_op jit(solution)/shard_map/cond/branch_1_fun/ppermute | solution.py:211
  48.6 62.4 %collective-permute-start.26 = (bf16[2560,512]{1,0:T(8,128)(2,1)}, bf16[2560,512]{1,0:T(8,128)(2,1)}, u32[]{:S(2)}, u32[]{:S(2)}) collective-permute-start(bf16[2560,512]{1,0:T(8,128)(2,1)} %get-tuple-element.231), channel_id=1, source_target_pairs={{0,16},{8,24},{16,0},{24,8},{1,17},{9,25},{17,1},{25,9},{2,18},{10... | collective-permute-start | bytes 7864328 | tf_op jit(solution)/shard_map/ppermute | solution.py:211
  60.6 13.5 %collective-permute-start.19 = (bf16[64,3584]{1,0:T(8,128)(2,1)S(1)}, bf16[64,3584]{1,0:T(8,128)(2,1)S(1)}, u32[]{:S(2)}, u32[]{:S(2)}) collective-permute-start(bf16[64,3584]{1,0:T(8,128)(2,1)S(1)} %add_convert_fusion.2), channel_id=1, source_target_pairs={{0,1},{1,0},{2,3},{3,2},{4,5},{5,4},{6,7},{7,6},{8,9},{9,8},{10,11... | collective-permute-start | bytes 1376264 | tf_op jit(solution)/shard_map/cond/branch_1_fun/ppermute | solution.py:201
  62.2 12.1 %collective-permute-start.17 = (bf16[64,3584]{1,0:T(8,128)(2,1)S(1)}, bf16[64,3584]{1,0:T(8,128)(2,1)S(1)}, u32[]{:S(2)}, u32[]{:S(2)}) collective-permute-start(bf16[64,3584]{1,0:T(8,128)(2,1)S(1)} %add_convert_fusion.3), channel_id=1, source_target_pairs={{0,2},{1,3},{2,6},{3,7},{6,4},{7,5},{4,0},{5,1},{8,10},{9,11},{10,... | collective-permute-start | bytes 1376264 | tf_op jit(solution)/shard_map/cond/branch_1_fun/ppermute | solution.py:207
  64.1 19.9 %collective-permute-start.21 = (bf16[64,3584]{1,0:T(8,128)(2,1)}, bf16[64,3584]{1,0:T(8,128)(2,1)S(1)}, u32[]{:S(2)}, u32[]{:S(2)}) collective-permute-start(bf16[64,3584]{1,0:T(8,128)(2,1)} %get-tuple-element.103), channel_id=1, source_target_pairs={{0,1},{1,0},{2,3},{3,2},{4,5},{5,4},{6,7},{7,6},{8,9},{9,8},{10,11... | collective-permute-start | bytes 1376264 | tf_op jit(solution)/shard_map/cond/branch_1_fun/ppermute | solution.py:201
  75.3 16.4 %collective-permute-start.23 = (bf16[64,3584]{1,0:T(8,128)(2,1)}, bf16[64,3584]{1,0:T(8,128)(2,1)S(1)}, u32[]{:S(2)}, u32[]{:S(2)}) collective-permute-start(bf16[64,3584]{1,0:T(8,128)(2,1)} %get-tuple-element.106), channel_id=1, source_target_pairs={{0,1},{1,0},{2,3},{3,2},{4,5},{5,4},{6,7},{7,6},{8,9},{9,8},{10,11... | collective-permute-start | bytes 1376264 | tf_op jit(solution)/shard_map/cond/branch_1_fun/ppermute | solution.py:201
  96.6 14.4 %collective-permute-start.7 = (bf16[2560,512]{1,0:T(8,128)(2,1)}, bf16[2560,512]{1,0:T(8,128)(2,1)}, u32[]{:S(2)}, u32[]{:S(2)}) collective-permute-start(bf16[2560,512]{1,0:T(8,128)(2,1)} %get-tuple-element.111), channel_id=1, source_target_pairs={{0,8},{8,0},{16,24},{24,16},{1,9},{9,1},{17,25},{25,17},{2,10},{10... | collective-permute-start | bytes 7864328 | tf_op jit(solution)/shard_map/cond/branch_1_fun/ppermute | solution.py:211
  96.7 14.4 %collective-permute-start.8 = (bf16[256,3584]{1,0:T(8,128)(2,1)}, bf16[256,3584]{1,0:T(8,128)(2,1)}, u32[]{:S(2)}, u32[]{:S(2)}) collective-permute-start(bf16[256,3584]{1,0:T(8,128)(2,1)} %get-tuple-element.112), channel_id=1, source_target_pairs={{0,8},{8,0},{16,24},{24,16},{1,9},{9,1},{17,25},{25,17},{2,10},{10... | collective-permute-start | bytes 5505032 | tf_op jit(solution)/shard_map/cond/branch_1_fun/ppermute | solution.py:211
  97.2 13.0 %collective-permute-start.5 = (bf16[64,3712]{1,0:T(8,128)(2,1)S(1)}, bf16[64,3712]{1,0:T(8,128)(2,1)}, u32[]{:S(2)}, u32[]{:S(2)}) collective-permute-start(bf16[64,3712]{1,0:T(8,128)(2,1)S(1)} %get-tuple-element.110), channel_id=1, source_target_pairs={{0,1},{1,0},{2,3},{3,2},{4,5},{5,4},{6,7},{7,6},{8,9},{9,8},{10,11... | collective-permute-start | bytes 1425416 | tf_op jit(solution)/shard_map/cond/branch_1_fun/ppermute | solution.py:201
  97.2 13.9 %collective-permute-start.6 = (bf16[64,3712]{1,0:T(8,128)(2,1)S(1)}, bf16[64,3712]{1,0:T(8,128)(2,1)}, u32[]{:S(2)}, u32[]{:S(2)}) collective-permute-start(bf16[64,3712]{1,0:T(8,128)(2,1)S(1)} %get-tuple-element.110), channel_id=1, source_target_pairs={{0,2},{1,3},{2,6},{3,7},{6,4},{7,5},{4,0},{5,1},{8,10},{9,11},{10,... | collective-permute-start | bytes 1425416 | tf_op jit(solution)/shard_map/cond/branch_1_fun/ppermute | solution.py:207
  111.0 47.6 %collective-permute-start.27 = (bf16[256,3584]{1,0:T(8,128)(2,1)}, bf16[256,3584]{1,0:T(8,128)(2,1)S(1)}, u32[]{:S(2)}, u32[]{:S(2)}) collective-permute-start(bf16[256,3584]{1,0:T(8,128)(2,1)} %bitcast.33), channel_id=1, source_target_pairs={{0,16},{8,24},{16,0},{24,8},{1,17},{9,25},{17,1},{25,9},{2,18},{10... | collective-permute-start | bytes 5505032 | tf_op jit(solution)/shard_map/ppermute | solution.py:211
  113.3 29.2 %collective-permute-start.11 = (bf16[2560,512]{1,0:T(8,128)(2,1)}, bf16[2560,512]{1,0:T(8,128)(2,1)S(1)}, u32[]{:S(2)}, u32[]{:S(2)}) collective-permute-start(bf16[2560,512]{1,0:T(8,128)(2,1)} %get-tuple-element.122.refs_9_), channel_id=1, source_target_pairs={{0,8},{8,0},{16,24},{24,16},{1,9},{9,1},{17,25},{25,17},{2,10},{10... | collective-permute-start | bytes 7864328 | tf_op jit(solution)/shard_map/cond/branch_1_fun/ppermute | solution.py:211
  113.3 13.5 %collective-permute-start.9 = (bf16[64,3712]{1,0:T(8,128)(2,1)}, bf16[64,3712]{1,0:T(8,128)(2,1)S(1)}, u32[]{:S(2)}, u32[]{:S(2)}) collective-permute-start(bf16[64,3712]{1,0:T(8,128)(2,1)} %get-tuple-element.116.refs_2_), channel_id=1, source_target_pairs={{0,1},{1,0},{2,3},{3,2},{4,5},{5,4},{6,7},{7,6},{8,9},{9,8},{10,11... | collective-permute-start | bytes 1425416 | tf_op jit(solution)/shard_map/cond/branch_1_fun/ppermute | solution.py:201
  115.1 14.1 %collective-permute-start.12 = (bf16[64,3712]{1,0:T(8,128)(2,1)}, bf16[64,3712]{1,0:T(8,128)(2,1)S(1)}, u32[]{:S(2)}, u32[]{:S(2)}) collective-permute-start(bf16[64,3712]{1,0:T(8,128)(2,1)} %get-tuple-element.116.refs_2_), channel_id=1, source_target_pairs={{0,2},{1,3},{2,6},{3,7},{6,4},{7,5},{4,0},{5,1},{8,10},{9,11},{10,... | collective-permute-start | bytes 1425416 | tf_op jit(solution)/shard_map/cond/branch_1_fun/ppermute | solution.py:207
  115.8 26.8 %collective-permute-start.10 = (bf16[1024,512]{1,0:T(8,128)(2,1)}, bf16[1024,512]{1,0:T(8,128)(2,1)S(1)}, u32[]{:S(2)}, u32[]{:S(2)}) collective-permute-start(bf16[1024,512]{1,0:T(8,128)(2,1)} %get-tuple-element.121.refs_8_), channel_id=1, source_target_pairs={{0,8},{8,0},{16,24},{24,16},{1,9},{9,1},{17,25},{25,17},{2,10},{10... | collective-permute-start | bytes 3145736 | tf_op jit(solution)/shard_map/cond/branch_1_fun/ppermute | solution.py:211
  129.2 13.1 %collective-permute-start.14 = (bf16[64,3712]{1,0:T(8,128)(2,1)S(1)}, bf16[64,3712]{1,0:T(8,128)(2,1)S(1)}, u32[]{:S(2)}, u32[]{:S(2)}) collective-permute-start(bf16[64,3712]{1,0:T(8,128)(2,1)S(1)} %collective-permute-done.12.refs_0_), channel_id=1, source_target_pairs={{0,2},{1,3},{2,6},{3,7},{6,4},{7,5},{4,0},{5,1},{8,10},{9,11},{10,... | collective-permute-start | bytes 1425416 | tf_op jit(solution)/shard_map/cond/branch_1_fun/ppermute | solution.py:207
  130.1 21.0 %collective-permute-start.13 = (bf16[64,3712]{1,0:T(8,128)(2,1)S(1)}, bf16[64,3712]{1,0:T(8,128)(2,1)S(1)}, u32[]{:S(2)}, u32[]{:S(2)}) collective-permute-start(bf16[64,3712]{1,0:T(8,128)(2,1)S(1)} %collective-permute-done.12.refs_0_), channel_id=1, source_target_pairs={{0,1},{1,0},{2,3},{3,2},{4,5},{5,4},{6,7},{7,6},{8,9},{9,8},{10,11... | collective-permute-start | bytes 1425416 | tf_op jit(solution)/shard_map/cond/branch_1_fun/ppermute | solution.py:201
  142.3 11.3 %collective-permute-start.15 = (bf16[64,3712]{1,0:T(8,128)(2,1)S(1)}, bf16[64,3712]{1,0:T(8,128)(2,1)S(1)}, u32[]{:S(2)}, u32[]{:S(2)}) collective-permute-start(bf16[64,3712]{1,0:T(8,128)(2,1)S(1)} %collective-permute-done.14.refs_2_), channel_id=1, source_target_pairs={{0,1},{1,0},{2,3},{3,2},{4,5},{5,4},{6,7},{7,6},{8,9},{9,8},{10,11... | collective-permute-start | bytes 1425416 | tf_op jit(solution)/shard_map/cond/branch_1_fun/ppermute | solution.py:201
  177.8 13.5 %collective-permute-start.32 = (bf16[64,3584]{1,0:T(8,128)(2,1)S(1)}, bf16[64,3584]{1,0:T(8,128)(2,1)S(1)}, u32[]{:S(2)}, u32[]{:S(2)}) collective-permute-start(bf16[64,3584]{1,0:T(8,128)(2,1)S(1)} %add_convert_fusion.7), channel_id=1, source_target_pairs={{0,1},{1,0},{2,3},{3,2},{4,5},{5,4},{6,7},{7,6},{8,9},{9,8},{10,11... | collective-permute-start | bytes 1376264 | tf_op jit(solution)/shard_map/ppermute | solution.py:201
  178.5 12.8 %collective-permute-start.30 = (bf16[64,3584]{1,0:T(8,128)(2,1)S(1)}, bf16[64,3584]{1,0:T(8,128)(2,1)S(1)}, u32[]{:S(2)}, u32[]{:S(2)}) collective-permute-start(bf16[64,3584]{1,0:T(8,128)(2,1)S(1)} %add_convert_fusion.8), channel_id=1, source_target_pairs={{0,2},{1,3},{2,6},{3,7},{6,4},{7,5},{4,0},{5,1},{8,10},{9,11},{10,... | collective-permute-start | bytes 1376264 | tf_op jit(solution)/shard_map/ppermute | solution.py:207
  180.8 20.3 %collective-permute-start.34 = (bf16[64,3584]{1,0:T(8,128)(2,1)S(1)}, bf16[64,3584]{1,0:T(8,128)(2,1)S(1)}, u32[]{:S(2)}, u32[]{:S(2)}) collective-permute-start(bf16[64,3584]{1,0:T(8,128)(2,1)S(1)} %get-tuple-element.256), channel_id=1, source_target_pairs={{0,1},{1,0},{2,3},{3,2},{4,5},{5,4},{6,7},{7,6},{8,9},{9,8},{10,11... | collective-permute-start | bytes 1376264 | tf_op jit(solution)/shard_map/ppermute | solution.py:201
  192.5 16.7 %collective-permute-start.36 = (bf16[64,3584]{1,0:T(8,128)(2,1)}, bf16[64,3584]{1,0:T(8,128)(2,1)S(1)}, u32[]{:S(2)}, u32[]{:S(2)}) collective-permute-start(bf16[64,3584]{1,0:T(8,128)(2,1)} %get-tuple-element.259), channel_id=1, source_target_pairs={{0,1},{1,0},{2,3},{3,2},{4,5},{5,4},{6,7},{7,6},{8,9},{9,8},{10,11... | collective-permute-start | bytes 1376264 | tf_op jit(solution)/shard_map/ppermute | solution.py:201
  (29 other events, 230.2 us)
